TPU v7x, 32 devices: a whole 2x2x4 slice. The times are simulated.
32 devices in a mesh: section: 2 (over x), seq: 4 (over z), fsdp: 4 (over y, core).
Axes of the slice: x: 2, y: 2, z: 4, core: 2. Of those that a mesh axis runs over, the one named last changes fastest.
Arguments:
- ends: bfloat16 [2, 2, 4, 1024, 1536], P('section', None, 'fsdp', 'seq'), may hold values from -6 to 6
- segment_ids: int32 [2, 4, 1024], P(None, 'fsdp'), may hold values from 0 to 3, as said below
- norm_one: bfloat16 [2, 1536], P('section', ('seq', 'fsdp')), may hold values from 0.099609375 to 1.8984375
- w_branch: bfloat16 [2, 1536, 2048], P('section', ('seq', 'fsdp')), may hold values from -0.15625 to 0.15625
- w_input: bfloat16 [2, 1536, 2048], P('section', ('seq', 'fsdp')), may hold values from -0.15625 to 0.15625
- conv_weight: bfloat16 [2, 4, 2048], P('section', None, ('seq', 'fsdp')), may hold values from -3 to 3
- conv_bias: bfloat16 [2, 2048], P('section', ('seq', 'fsdp')), may hold values from -3 to 3
- gate_a: bfloat16 [2, 16, 128, 128], P('section', None, ('seq', 'fsdp')), may hold values from -0.5 to 0.5
- gate_i: bfloat16 [2, 16, 128, 128], P('section', None, ('seq', 'fsdp')), may hold values from -0.5 to 0.5
- bias_a: bfloat16 [2, 2048], P('section', ('seq', 'fsdp')), may hold values from -4 to 4
- bias_i: bfloat16 [2, 2048], P('section', ('seq', 'fsdp')), may hold values from -4 to 4
- decay: bfloat16 [2, 2048], P('section', ('seq', 'fsdp')), may hold values from -12 to -4
- w_out: bfloat16 [2, 2048, 1536], P('section', ('seq', 'fsdp')), may hold values from -0.375 to 0.375
- norm_two: bfloat16 [2, 1536], P('section', ('seq', 'fsdp')), may hold values from 0.099609375 to 1.8984375
- w_gate: bfloat16 [2, 1536, 4608], P('section', ('seq', 'fsdp')), may hold values from -0.15625 to 0.15625
- w_up: bfloat16 [2, 1536, 4608], P('section', ('seq', 'fsdp')), may hold values from -0.15625 to 0.15625
- w_down: bfloat16 [2, 4608, 1536], P('section', ('seq', 'fsdp')), may hold values from -0.15625 to 0.15625
Outputs:
- section_outputs: bfloat16 [2, 2, 4, 1024, 1536], P('section', None, 'fsdp', 'seq')
- input_grads: bfloat16 [2, 2, 4, 1024, 1536], P('section', None, 'fsdp', 'seq')
- grad_norm_one: float32 [2, 1536], P('section', ('seq', 'fsdp'))
- grad_w_branch: float32 [2, 1536, 2048], P('section', ('seq', 'fsdp'))
- grad_w_input: float32 [2, 1536, 2048], P('section', ('seq', 'fsdp'))
- grad_conv_weight: float32 [2, 4, 2048], P('section', None, ('seq', 'fsdp'))
- grad_conv_bias: float32 [2, 2048], P('section', ('seq', 'fsdp'))
- grad_gate_a: float32 [2, 16, 128, 128], P('section', None, ('seq', 'fsdp'))
- grad_gate_i: float32 [2, 16, 128, 128], P('section', None, ('seq', 'fsdp'))
- grad_bias_a: float32 [2, 2048], P('section', ('seq', 'fsdp'))
- grad_bias_i: float32 [2, 2048], P('section', ('seq', 'fsdp'))
- grad_decay: float32 [2, 2048], P('section', ('seq', 'fsdp'))
- grad_w_out: float32 [2, 2048, 1536], P('section', ('seq', 'fsdp'))
- grad_norm_two: float32 [2, 1536], P('section', ('seq', 'fsdp'))
- grad_w_gate: float32 [2, 1536, 4608], P('section', ('seq', 'fsdp'))
- grad_w_up: float32 [2, 1536, 4608], P('section', ('seq', 'fsdp'))
- grad_w_down: float32 [2, 4608, 1536], P('section', ('seq', 'fsdp'))
Inputs may be any that keep to these rules, and one draw needn't show every extreme that they name: `segment_ids`: within each sequence the ids start at 0, never fall, and rise where a document begins; for each index of the second dimension one micro-batch's sequence is a single document.
All inputs are finite; a program needn't handle non-finite values.
Results may differ from a plain program's by a relative error of at most 0.017.
Values may be sent and summed in bfloat16 or wider, within the bound.
No kernel may reach another device: no remote copies, remote signals or barrier semaphores. Data moves between devices by JAX's collectives and lax.ppermute only.
A program may use at most 448 MiB of HBM per device.

v0:
```python
import functools

import jax
import jax.numpy as jnp
from jax import lax
from jax.experimental import pallas as pl
from jax.experimental.pallas import tpu as pltpu
from jax.sharding import PartitionSpec as P

CONV = 4
EPS = 1e-06
F32 = jnp.float32
BF16 = jnp.bfloat16
VMEM_BYTES = 56 << 20
LANES = 128
SUB = 8


def nn_dot(a, b):
    return lax.dot_general(a, b, (((1,), (0,)), ((), ())), preferred_element_type=F32)


def nt_dot(a, b):
    return lax.dot_general(a, b, (((1,), (1,)), ((), ())), preferred_element_type=F32)


def tn_dot(a, b):
    return lax.dot_general(a, b, (((0,), (0,)), ((), ())), preferred_element_type=F32)


def sigmoid(v):
    return 0.5 * jnp.tanh(0.5 * v) + 0.5


K0 = 0.7978845608028654
K1 = 0.044715


def gelu(v):
    return 0.5 * v * (1.0 + jnp.tanh(K0 * (v + K1 * v * v * v)))


def gelu_both(v):
    square = v * v
    t = jnp.tanh(K0 * v * (1.0 + K1 * square))
    half = 0.5 * (1.0 + t)
    slope = half + (0.5 * K0) * v * (1.0 - t * t) * (1.0 + (3.0 * K1) * square)
    return v * half, slope


def lanes(mask, width):
    return jnp.concatenate([mask] * (width // LANES), axis=1) if width > LANES else mask


def call(kernel, grid, in_specs, out_specs, out_shape, scratch, flops, bytes_accessed, args):
    return pl.pallas_call(
        kernel,
        grid=grid,
        in_specs=in_specs,
        out_specs=out_specs,
        out_shape=out_shape,
        scratch_shapes=scratch,
        compiler_params=pltpu.CompilerParams(
            dimension_semantics=("arbitrary",) * len(grid), vmem_limit_bytes=VMEM_BYTES
        ),
        cost_estimate=pl.CostEstimate(
            flops=int(flops), bytes_accessed=int(bytes_accessed), transcendentals=0
        ),
    )(*args)


def whole(shape):
    return pl.BlockSpec(shape, lambda c: (0,) * len(shape))


def columns(rows, width, offset=0):
    return pl.BlockSpec((rows, width), lambda c: (0, c + offset))


def struct(shape, dtype):
    return jax.ShapeDtypeStruct(shape, dtype)


def recur_in_kernel(
    groups, length,
    x_ref, halo_ref, gain_ref, wb_ref, wi_ref, ga_ref, gi_ref, vec_ref, mask_ref,
    normed_ref, branch_ref, ext_ref, rate_ref, igate_ref, keep_ref, local_ref, segp_ref, agg_ref,
    xn, conv, pre_a, pre_i,
):
    rows = groups * length
    steps = length // SUB
    width = wb_ref.shape[1]

    @pl.when(pl.program_id(0) == 0)
    def _():
        gain = gain_ref[...]
        for at, ref in ((0, x_ref), (rows, halo_ref)):
            v = ref[...].astype(F32)
            r = lax.rsqrt(jnp.mean(v * v, axis=-1, keepdims=True) + EPS)
            xn[at : at + ref.shape[0], :] = (v * r * gain).astype(BF16)
        normed_ref[...] = xn[0:rows, :]

    branch_ref[...] = nn_dot(xn[0:rows, :], wb_ref[...])
    conv_in = nn_dot(xn[...], wi_ref[...]).astype(BF16).astype(F32)
    sub = lax.broadcasted_iota(jnp.int32, (SUB, width), 0)
    for g in range(groups):
        base = conv_in[g * length : (g + 1) * length]
        halo = conv_in[rows + g * SUB : rows + (g + 1) * SUB]
        for k in (3, 2, 1):
            block = pltpu.roll(base[(steps - k) * SUB : (steps - k + 1) * SUB], 1, 0)
            ext_ref[g, (3 - k) * SUB : (4 - k) * SUB, :] = jnp.where(sub == 0, halo[3 - k : 4 - k], block)
        ext_ref[g, 3 * SUB : 3 * SUB + length, :] = base
    taps = [vec_ref[k : k + 1, :] for k in range(CONV)]
    for g in range(groups):
        part = slice(g * length, (g + 1) * length)
        out = vec_ref[4:5, :] + taps[0] * ext_ref[g, 3 * SUB : 3 * SUB + length, :]
        for k in range(1, CONV):
            link = lanes(mask_ref[k, part, :], width)
            out = out + taps[k] * (link * ext_ref[g, (3 - k) * SUB : (3 - k) * SUB + length, :])
        conv[part, :] = out
    rounded = conv[...].astype(BF16)
    for h in range(width // LANES):
        col = slice(h * LANES, (h + 1) * LANES)
        pre_a[:, col] = nn_dot(rounded[:, col], ga_ref[h])
        pre_i[:, col] = nn_dot(rounded[:, col], gi_ref[h])
    bias_a, bias_i, scale = vec_ref[5:6, :], vec_ref[6:7, :], vec_ref[7:8, :]
    chunk = 4

    def step(i, carry):
        out = []
        for g in range(groups):
            h, p = carry[g]
            at = pl.multiple_of(g * length + i * (chunk * SUB), chunk * SUB)
            here = pl.ds(at, chunk * SUB)
            rate = sigmoid(pre_a[here, :] + bias_a)
            igate = sigmoid(pre_i[here, :] + bias_i)
            keep = jnp.exp(scale * rate) * lanes(mask_ref[0, here, :], width)
            driven = igate * conv[here, :] * jnp.sqrt(1.0 + 0.0001 - keep * keep)
            rate_ref[here, :] = rate
            igate_ref[here, :] = igate
            keep_ref[here, :] = keep
            states = []
            for q in range(chunk):
                kq = keep[q * SUB : (q + 1) * SUB]
                h = kq * h + driven[q * SUB : (q + 1) * SUB]
                p = kq * p
                states.append(h)
            local_ref[here, :] = jnp.concatenate(states, axis=0)
            out.append((h, p))
        return tuple(out)

    start = tuple((jnp.zeros((SUB, width), F32), jnp.ones((SUB, width), F32)) for _ in range(groups))
    done = lax.fori_loop(0, steps // chunk, step, start)
    for g in range(groups):
        h, p = done[g]
        segp_ref[g * SUB : (g + 1) * SUB, :] = p
        a, b = jnp.ones((1, width), F32), jnp.zeros((1, width), F32)
        for s in range(SUB):
            b = p[s : s + 1] * b + h[s : s + 1]
            a = p[s : s + 1] * a
        agg_ref[2 * g : 2 * g + 1, :] = a
        agg_ref[2 * g + 1 : 2 * g + 2, :] = b


def recur_in(x, halo, gain, w_in, gate_a, gate_i, vec, masks, groups, length):
    rows, dim = x.shape
    recur = w_in.shape[1] // 2
    width = 256
    blocks = recur // width
    block_f32 = columns(rows, width)
    heads = width // LANES
    ext_len = length + 3 * SUB
    return call(
        functools.partial(recur_in_kernel, groups, length),
        (blocks,),
        [
            whole(x.shape), whole(halo.shape), whole(gain.shape),
            columns(dim, width), columns(dim, width, blocks),
            pl.BlockSpec((heads, LANES, LANES), lambda c: (c, 0, 0)),
            pl.BlockSpec((heads, LANES, LANES), lambda c: (c, 0, 0)),
            columns(8, width), whole(masks.shape),
        ],
        [
            whole((rows, dim)), block_f32,
            pl.BlockSpec((groups, ext_len, width), lambda c: (0, 0, c)),
            block_f32, block_f32, block_f32, block_f32,
            columns(SUB * groups, width), columns(2 * groups, width),
        ],
        [
            struct((rows, dim), BF16), struct((rows, recur), F32), struct((groups, ext_len, recur), F32),
            struct((rows, recur), F32), struct((rows, recur), F32), struct((rows, recur), F32),
            struct((rows, recur), F32), struct((SUB * groups, recur), F32), struct((2 * groups, recur), F32),
        ],
        [
            pltpu.VMEM((rows + SUB * groups, dim), BF16), pltpu.VMEM((rows, width), F32),
            pltpu.VMEM((rows, width), F32), pltpu.VMEM((rows, width), F32),
        ],
        4 * rows * dim * recur * 1.5,
        dim * recur * 4 + rows * recur * 4 * 6,
        (x, halo, gain, w_in, w_in, gate_a, gate_i, vec, masks),
    )


def recur_out_kernel(
    groups, length,
    x_ref, keep_ref, local_ref, branch_ref, segp_ref, hin_ref, wo_ref, gain_ref,
    hidden_ref, mixed_ref, middle_ref, normed_ref,
    acc,
):
    steps = length // SUB
    width = keep_ref.shape[1]
    chunk = 4
    c = pl.program_id(0)
    start = []
    for g in range(groups):
        ends = local_ref[(g + 1) * length - SUB : (g + 1) * length, :]
        prods = segp_ref[g * SUB : (g + 1) * SUB, :]
        state = hin_ref[g : g + 1, :]
        entering = []
        for s in range(SUB):
            entering.append(state)
            state = prods[s : s + 1] * state + ends[s : s + 1]
        start.append(jnp.concatenate(entering, axis=0))

    def step(i, carry):
        out = []
        for g in range(groups):
            q = carry[g]
            at = pl.multiple_of(g * length + i * (chunk * SUB), chunk * SUB)
            here = pl.ds(at, chunk * SUB)
            keep = keep_ref[here, :]
            moved = []
            for r in range(chunk):
                q = keep[r * SUB : (r + 1) * SUB] * q
                moved.append(q)
            hidden = local_ref[here, :] + jnp.concatenate(moved, axis=0)
            hidden_ref[here, :] = hidden
            mixed_ref[here, :] = (hidden * gelu(branch_ref[here, :])).astype(BF16)
            out.append(q)
        return tuple(out)

    lax.fori_loop(0, steps // chunk, step, tuple(start))
    part = nn_dot(mixed_ref[...], wo_ref[...])

    @pl.when(c == 0)
    def _():
        acc[...] = x_ref[...].astype(F32) + part

    @pl.when(c > 0)
    def _():
        acc[...] += part

    @pl.when(c == pl.num_programs(0) - 1)
    def _():
        m = acc[...]
        middle_ref[...] = m
        r = lax.rsqrt(jnp.mean(m * m, axis=-1, keepdims=True) + EPS)
        normed_ref[...] = (m * r * gain_ref[...]).astype(BF16)


def recur_out(x, keep, local, branch, segp, hin, w_out, gain, groups, length):
    rows, dim = x.shape
    recur = keep.shape[1]
    width = 256
    block = columns(rows, width)
    return call(
        functools.partial(recur_out_kernel, groups, length),
        (recur // width,),
        [
            whole(x.shape), block, block, block, columns(SUB * groups, width), columns(groups, width),
            pl.BlockSpec((width, dim), lambda c: (c, 0)), whole(gain.shape),
        ],
        [block, block, whole((rows, dim)), whole((rows, dim))],
        [
            struct((rows, recur), F32), struct((rows, recur), BF16),
            struct((rows, dim), F32), struct((rows, dim), BF16),
        ],
        [pltpu.VMEM((rows, dim), F32)],
        2 * rows * dim * recur * 1.5,
        dim * recur * 2 + rows * recur * 18,
        (x, keep, local, branch, segp, hin, w_out, gain),
    )


def ff_kernel(x_ref, mid_ref, wg_ref, wu_ref, wd_ref, gate_ref, up_ref, product_ref, out_ref, acc):
    c = pl.program_id(0)
    x = x_ref[...]
    gate = nn_dot(x, wg_ref[...])
    up = nn_dot(x, wu_ref[...])
    gate_ref[...] = gate.astype(BF16)
    up_ref[...] = up.astype(BF16)
    product = (gelu(gate) * up).astype(BF16)
    product_ref[...] = product
    part = nn_dot(product, wd_ref[...])

    @pl.when(c == 0)
    def _():
        acc[...] = mid_ref[...] + part

    @pl.when(c > 0)
    def _():
        acc[...] += part

    @pl.when(c == pl.num_programs(0) - 1)
    def _():
        out_ref[...] = acc[...].astype(BF16)


def feed_forward(x, middle, w_gu, w_down):
    rows, dim = x.shape
    hidden = w_down.shape[0]
    width = 512
    blocks = hidden // width
    block = columns(rows, width)
    return call(
        ff_kernel,
        (blocks,),
        [
            whole(x.shape), whole(middle.shape), columns(dim, width), columns(dim, width, blocks),
            pl.BlockSpec((width, dim), lambda c: (c, 0)),
        ],
        [block, block, block, whole((rows, dim))],
        [struct((rows, hidden), BF16)] * 3 + [struct((rows, dim), BF16)],
        [pltpu.VMEM((rows, dim), F32)],
        6 * rows * dim * hidden,
        6 * dim * hidden,
        (x, middle, w_gu, w_gu, w_down),
    )


def norm_back(values, gain, grad):
    q = lax.rsqrt(jnp.mean(values * values, axis=-1, keepdims=True) + EPS)
    t = gain * grad
    back = q * t - values * (q * q * q * jnp.mean(values * t, axis=-1, keepdims=True))
    return back, jnp.sum(values * q * grad, axis=0, keepdims=True)


def ff_back_kernel(
    dout_ref, mid_ref, gain_ref, gate_ref, up_ref, wg_ref, wu_ref, wd_ref,
    dgate_ref, dup_ref, dmid_ref, low_ref, dgain_ref,
    acc,
):
    c = pl.program_id(0)
    dproduct = nt_dot(dout_ref[...], wd_ref[...])
    act, slope = gelu_both(gate_ref[...].astype(F32))
    dgate = (dproduct * up_ref[...].astype(F32) * slope).astype(BF16)
    dup = (dproduct * act).astype(BF16)
    dgate_ref[...] = dgate
    dup_ref[...] = dup
    part = nt_dot(dgate, wg_ref[...]) + nt_dot(dup, wu_ref[...])

    @pl.when(c == 0)
    def _():
        acc[...] = part

    @pl.when(c > 0)
    def _():
        acc[...] += part

    @pl.when(c == pl.num_programs(0) - 1)
    def _():
        back, dgain = norm_back(mid_ref[...], gain_ref[...], acc[...])
        dmid = dout_ref[...].astype(F32) + back
        dmid_ref[...] = dmid
        low_ref[...] = dmid.astype(BF16)
        dgain_ref[...] = dgain


def feed_forward_back(dout, middle, gain, gate, up, w_gu, w_down):
    rows, dim = dout.shape
    hidden = w_down.shape[0]
    width = 512
    blocks = hidden // width
    block = columns(rows, width)
    full = whole((rows, dim))
    return call(
        ff_back_kernel,
        (blocks,),
        [
            full, full, whole(gain.shape), block, block, columns(dim, width), columns(dim, width, blocks),
            pl.BlockSpec((width, dim), lambda c: (c, 0)),
        ],
        [block, block, full, full, whole((1, dim))],
        [
            struct((rows, hidden), BF16), struct((rows, hidden), BF16), struct((rows, dim), F32),
            struct((rows, dim), BF16), struct((1, dim), F32),
        ],
        [pltpu.VMEM((rows, dim), F32)],
        6 * rows * dim * hidden * 1.2,
        6 * dim * hidden,
        (dout, middle, gain, gate, up, w_gu, w_gu, w_down),
    )


def mix_back_kernel(
    groups, length,
    low_ref, wo_ref, branch_ref, hidden_ref, keep_ref,
    dbranch_ref, local_ref, sege_ref, segf_ref, agg_ref,
    dmixed,
):
    steps = length // SUB
    width = keep_ref.shape[1]
    chunk = 4
    dmixed[...] = nt_dot(low_ref[...], wo_ref[...])

    def step(i, carry):
        out = []
        for g in range(groups):
            s, p, after = carry[g]
            at = pl.multiple_of(g * length + (steps // chunk - 1 - i) * (chunk * SUB), chunk * SUB)
            here = pl.ds(at, chunk * SUB)
            act, slope = gelu_both(branch_ref[here, :])
            d = dmixed[here, :]
            dbranch_ref[here, :] = (d * hidden_ref[here, :] * slope).astype(BF16)
            dhidden = d * act
            keep = keep_ref[here, :]
            states = [None] * chunk
            for r in reversed(range(chunk)):
                s = dhidden[r * SUB : (r + 1) * SUB] + after * s
                p = after * p
                after = keep[r * SUB : (r + 1) * SUB]
                states[r] = s
            local_ref[here, :] = jnp.concatenate(states, axis=0)
            out.append((s, p, after))
        return tuple(out)

    one = jnp.ones((SUB, width), F32)
    start = tuple((jnp.zeros((SUB, width), F32), one, one) for _ in range(groups))
    done = lax.fori_loop(0, steps // chunk, step, start)
    for g in range(groups):
        s, p, after = done[g]
        e, f = after * s, after * p
        sege_ref[g * SUB : (g + 1) * SUB, :] = e
        segf_ref[g * SUB : (g + 1) * SUB, :] = f
        a, b = jnp.ones((1, width), F32), jnp.zeros((1, width), F32)
        for r in reversed(range(SUB)):
            b = e[r : r + 1] + f[r : r + 1] * b
            a = f[r : r + 1] * a
        agg_ref[2 * g : 2 * g + 1, :] = a
        agg_ref[2 * g + 1 : 2 * g + 2, :] = b


def mix_back(low, w_out, branch, hidden, keep, groups, length):
    rows, dim = low.shape
    recur = keep.shape[1]
    width = 256
    block = columns(rows, width)
    return call(
        functools.partial(mix_back_kernel, groups, length),
        (recur // width,),
        [whole(low.shape), pl.BlockSpec((width, dim), lambda c: (c, 0)), block, block, block],
        [block, block, columns(SUB * groups, width), columns(SUB * groups, width), columns(2 * groups, width)],
        [
            struct((rows, recur), BF16), struct((rows, recur), F32), struct((SUB * groups, recur), F32),
            struct((SUB * groups, recur), F32), struct((2 * groups, recur), F32),
        ],
        [pltpu.VMEM((rows, width), F32)],
        2 * rows * dim * recur * 2,
        dim * recur * 2 + rows * recur * 18,
        (low, w_out, branch, hidden, keep),
    )


def gates_back_kernel(
    groups, length,
    local_ref, keep_ref, hidden_ref, ext_ref, rate_ref, igate_ref, sege_ref, segf_ref, gin_ref, hin_ref,
    ga_ref, gi_ref, vec_ref, mask_ref,
    din_ref, head_ref, dga_ref, dgi_ref, dvec_ref,
    dconv, low_a, low_i, rounded,
):
    steps = length // SUB
    width = keep_ref.shape[1]
    chunk = 4
    sub = lax.broadcasted_iota(jnp.int32, (SUB, width), 0)
    taps = [vec_ref[k : k + 1, :] for k in range(CONV)]
    conv_bias, scale = vec_ref[4:5, :], vec_ref[7:8, :]
    start = []
    for g in range(groups):
        e = sege_ref[g * SUB : (g + 1) * SUB, :]
        f = segf_ref[g * SUB : (g + 1) * SUB, :]
        y = gin_ref[g : g + 1, :]
        entering = [None] * SUB
        for s in reversed(range(SUB)):
            entering[s] = y
            y = e[s : s + 1] + f[s : s + 1] * y
        start.append((jnp.concatenate(entering, axis=0), jnp.ones((SUB, width), F32)))
    zero = jnp.zeros((SUB, width), F32)

    def fold(v):
        return functools.reduce(jnp.add, [v[q * SUB : (q + 1) * SUB] for q in range(v.shape[0] // SUB)])

    def step(i, carry):
        chains, sum_a, sum_i, sum_d = carry
        out = []
        j = steps // chunk - 1 - i
        for g in range(groups):
            r, after = chains[g]
            at = pl.multiple_of(g * length + j * (chunk * SUB), chunk * SUB)
            here = pl.ds(at, chunk * SUB)
            keep = keep_ref[here, :]
            parts = [None] * chunk
            for q in reversed(range(chunk)):
                r = after * r
                after = keep[q * SUB : (q + 1) * SUB]
                parts[q] = r
            state = local_ref[here, :] + jnp.concatenate(parts, axis=0)
            last = hidden_ref[(g + 1) * length - SUB : (g + 1) * length, :]
            wrapped = jnp.where(sub == 0, hin_ref[g : g + 1, :], pltpu.roll(last, 1, 0))
            before = pl.multiple_of(jnp.maximum(at - SUB, g * length), SUB)
            first = jnp.where(j == 0, wrapped, hidden_ref[pl.ds(before, SUB), :])
            rest = hidden_ref[pl.ds(at, (chunk - 1) * SUB), :]
            previous = jnp.concatenate([first, rest], axis=0)
            inner = pl.multiple_of(j * (chunk * SUB), chunk * SUB)
            conv = conv_bias + taps[0] * ext_ref[g, pl.ds(inner + 3 * SUB, chunk * SUB), :]
            for k in range(1, CONV):
                link = lanes(mask_ref[k, here, :], width)
                conv = conv + taps[k] * (link * ext_ref[g, pl.ds(inner + (3 - k) * SUB, chunk * SUB), :])
            rate, igate = rate_ref[here, :], igate_ref[here, :]
            space = 1.0 + 0.0001 - keep * keep
            inverse = lax.rsqrt(space)
            scaling = space * inverse
            both = state * igate
            dconv[here, :] = both * scaling
            with_conv = both * conv
            dlog = (state * previous - with_conv * (keep * inverse)) * keep
            dpre_a = (dlog * scale) * (rate * (1.0 - rate))
            dpre_i = (with_conv * scaling) * (1.0 - igate)
            low_a[here, :] = dpre_a.astype(BF16)
            low_i[here, :] = dpre_i.astype(BF16)
            rounded[here, :] = conv.astype(BF16)
            sum_a = sum_a + fold(dpre_a)
            sum_i = sum_i + fold(dpre_i)
            sum_d = sum_d + fold(dlog * rate)
            out.append((r, after))
        return tuple(out), sum_a, sum_i, sum_d

    _, sum_a, sum_i, sum_d = lax.fori_loop(0, steps // chunk, step, (tuple(start), zero, zero, zero))
    dvec_ref[5:6, :] = jnp.sum(sum_a, axis=0, keepdims=True)
    dvec_ref[6:7, :] = jnp.sum(sum_i, axis=0, keepdims=True)
    dvec_ref[7:8, :] = jnp.sum(sum_d, axis=0, keepdims=True)
    for h in range(width // LANES):
        col = slice(h * LANES, (h + 1) * LANES)
        dga_ref[h] = tn_dot(rounded[:, col], low_a[:, col])
        dgi_ref[h] = tn_dot(rounded[:, col], low_i[:, col])
        dconv[:, col] += nt_dot(low_a[:, col], ga_ref[h]) + nt_dot(low_i[:, col], gi_ref[h])

    sums = [zero] * (CONV + 1)
    for g in range(groups):

        def conv_step(i, carry, g=g):
            carry = list(carry)
            inner = pl.multiple_of(i * (chunk * SUB), chunk * SUB)
            here = pl.ds(pl.multiple_of(g * length + inner, chunk * SUB), chunk * SUB)
            d = dconv[here, :]
            carry[4] = carry[4] + fold(d)
            for k in range(CONV):
                masked = d if k == 0 else d * lanes(mask_ref[k, here, :], width)
                carry[k] = carry[k] + fold(masked * ext_ref[g, pl.ds(inner + (3 - k) * SUB, chunk * SUB), :])
            return tuple(carry)

        sums = list(lax.fori_loop(0, steps // chunk, conv_step, tuple(sums)))
        base = g * length
        tail = length - 3 * SUB
        total = taps[0] * dconv[base : base + tail, :]
        for k in range(1, CONV):
            there = slice(base + k * SUB, base + k * SUB + tail)
            total = total + taps[k] * (dconv[there, :] * lanes(mask_ref[k, there, :], width))
        din_ref[base : base + tail, :] = total

        def term(k, block):
            there = slice(base + block * SUB, base + (block + 1) * SUB)
            v = taps[k] * dconv[there, :]
            return v if k == 0 else v * lanes(mask_ref[k, there, :], width)

        heads = []
        for i in (3, 2, 1):
            j = steps - i
            value = term(0, j)
            head = None
            for k in range(1, CONV):
                if j + k < steps:
                    value = value + term(k, j + k)
                else:
                    t = term(k, j + k - steps)
                    value = value + jnp.where(sub == SUB - 1, 0.0, pltpu.roll(t, SUB - 1, 0))
                    head = t if head is None else head + t
            din_ref[base + j * SUB : base + (j + 1) * SUB, :] = value
            heads.append(head[0:1])
        head_ref[g * SUB : (g + 1) * SUB, :] = jnp.concatenate(heads + [jnp.zeros((SUB - 3, width), F32)], axis=0)
    for k in range(CONV + 1):
        dvec_ref[k : k + 1, :] = jnp.sum(sums[k], axis=0, keepdims=True)


def gates_back(local, keep, hidden, ext, rate, igate, sege, segf, gin, hin, gate_a, gate_i, vec, masks, groups, length):
    rows, recur = local.shape
    width = 256
    heads = width // LANES
    block = columns(rows, width)
    seg = columns(SUB * groups, width)
    gate = pl.BlockSpec((heads, LANES, LANES), lambda c: (c, 0, 0))
    return call(
        functools.partial(gates_back_kernel, groups, length),
        (recur // width,),
        [
            block, block, block, pl.BlockSpec((groups, length + 3 * SUB, width), lambda c: (0, 0, c)),
            block, block, seg, seg, columns(groups, width), columns(groups, width),
            gate, gate, columns(8, width), whole(masks.shape),
        ],
        [block, seg, gate, gate, columns(8, width)],
        [
            struct((rows, recur), F32), struct((SUB * groups, recur), F32), struct(gate_a.shape, F32),
            struct(gate_a.shape, F32), struct((8, recur), F32),
        ],
        [
            pltpu.VMEM((rows, width), F32), pltpu.VMEM((rows, width), BF16),
            pltpu.VMEM((rows, width), BF16), pltpu.VMEM((rows, width), BF16),
        ],
        rows * recur * 128 * 8 * 4,
        rows * recur * 28,
        (local, keep, hidden, ext, rate, igate, sege, segf, gin, hin, gate_a, gate_i, vec, masks),
    )


def recur_in_back_kernel(
    groups, length,
    dbranch_ref, din_ref, back_ref, wb_ref, wi_ref, x_ref, gain_ref, dmid_ref,
    low_ref, dx_ref, dgain_ref,
    acc,
):
    c = pl.program_id(0)
    width = din_ref.shape[1]
    rim = 4 * SUB
    sub = lax.broadcasted_iota(jnp.int32, (SUB, width), 0)
    for g in range(groups):
        base = g * length
        if length > rim:
            low_ref[base : base + length - rim, :] = din_ref[base : base + length - rim, :].astype(BF16)
        extra = [jnp.zeros((SUB, width), F32)]
        for i in range(3):
            extra.append(jnp.where(sub == SUB - 1, back_ref[g * SUB + i : g * SUB + i + 1, :], 0.0))
        tail = slice(base + length - rim, base + length)
        low_ref[tail, :] = (din_ref[tail, :] + jnp.concatenate(extra, axis=0)).astype(BF16)
    part = nt_dot(dbranch_ref[...], wb_ref[...]) + nt_dot(low_ref[...], wi_ref[...])

    @pl.when(c == 0)
    def _():
        acc[...] = part

    @pl.when(c > 0)
    def _():
        acc[...] += part

    @pl.when(c == pl.num_programs(0) - 1)
    def _():
        back, dgain = norm_back(x_ref[...].astype(F32), gain_ref[...], acc[...])
        dx_ref[...] = (dmid_ref[...] + back).astype(BF16)
        dgain_ref[...] = dgain


def recur_in_back(dbranch, din, back, w_in, x, gain, dmid, groups, length):
    rows, dim = x.shape
    recur = din.shape[1]
    width = 256
    blocks = recur // width
    block = columns(rows, width)
    full = whole((rows, dim))
    return call(
        functools.partial(recur_in_back_kernel, groups, length),
        (blocks,),
        [
            block, block, columns(SUB * groups, width), columns(dim, width), columns(dim, width, blocks),
            full, whole(gain.shape), full,
        ],
        [block, full, whole((1, dim))],
        [struct((rows, recur), BF16), struct((rows, dim), BF16), struct((1, dim), F32)],
        [pltpu.VMEM((rows, dim), F32)],
        4 * rows * dim * recur,
        4 * dim * recur + rows * recur * 8,
        (dbranch, din, back, w_in, w_in, x, gain, dmid),
    )


def outer_kernel(keep_a, keep_b, send_a, send_b, right_a, right_b, keep_ref, send_ref):
    a, b = right_a[...], right_b[...]
    send_ref[...] = (nn_dot(send_a[...], a) + nn_dot(send_b[...], b)).astype(BF16)
    keep_ref[...] = (nn_dot(keep_a[...], a) + nn_dot(keep_b[...], b)).astype(BF16)


def outer_block(total):
    for width in (768, 512, 384, 256, 128):
        if total % width == 0:
            return width
    return total


def outer(left, right, first, total):
    k, rows = left[0].shape
    width = outer_block(total)
    offset = first // width
    out = columns(k, width)
    return call(
        outer_kernel,
        (total // width,),
        [whole((k, rows))] * 4 + [columns(rows, width, offset)] * 2,
        [out, out],
        [struct((k, total), BF16)] * 2,
        [],
        8 * k * rows * total,
        4 * k * total + 4 * rows * total,
        (*left, *right),
    )


def shifted(value, axis, by):
    length = lax.axis_size(axis)
    pairs = [(i, i + by) for i in range(length) if 0 <= i + by < length]
    return lax.ppermute(value, axis, pairs)


def entering(agg, groups, reverse):
    n = lax.axis_size("seq")
    sign = -1 if reverse else 1
    got = {k: shifted(agg, "seq", sign * k) for k in range(1, n)}
    state = jnp.zeros((groups, agg.shape[1]), F32)
    for k in range(n - 1, 0, -1):
        part = got[k].reshape(groups, 2, -1)
        state = part[:, 0] * state + part[:, 1]
    return state


def add(*parts):
    return functools.reduce(jnp.add, [p.astype(F32) for p in parts])


def line_sum(slots, mine, n, send):
    def at(offset):
        return slots((mine + offset) % n)

    up, down = at(n - 1), at(1)
    for s in range(1, n):
        got_up = send(up, [(i, i + 1) for i in range(s)])
        got_down = send(down, [(i, i - 1) for i in range(n - s, n)])
        if s < n - 1:
            up = add(at(n - 1 - s), got_up).astype(BF16)
            down = add(at(s + 1), got_down).astype(BF16)
    return add(at(0), got_up, got_down)


class Scatter:
    def __init__(self):
        self.n, self.fs = lax.axis_size("seq"), lax.axis_size("fsdp")
        self.ny = self.fs // 2
        self.z, f = lax.axis_index("seq"), lax.axis_index("fsdp")
        self.y, self.core = f // 2, f % 2
        self.swaps = []

    def core_swap(self, value):
        return lax.ppermute(value, "fsdp", [(i, i ^ 1) for i in range(self.fs)])

    def y_send(self, value, pairs):
        return lax.ppermute(value, "fsdp", [(2 * a + c, 2 * b + c) for a, b in pairs for c in range(2)])

    def over_y(self, keep, send):
        if len(self.swaps) >= 2:
            send, _ = lax.optimization_barrier((send, self.swaps[-2]))
        got = self.y_send(send, [(0, 1), (1, 0)])
        self.swaps.append(got)
        return add(keep, got).astype(BF16)

    def over_z(self, shares):
        def slots(d):
            return lax.dynamic_index_in_dim(shares, d, 0, keepdims=False)

        if self.n == 1:
            return shares[0].astype(F32)
        return line_sum(slots, self.z, self.n, lambda v, pairs: lax.ppermute(v, "seq", pairs))

    def finish(self, keep, send):
        return self.over_z(self.over_y(keep, send))


def pick(value, index, axis):
    return lax.dynamic_index_in_dim(value, index, axis, keepdims=False)


def reorder(v):
    length, d = v.shape[-2:]
    return jnp.swapaxes(v.reshape(-1, SUB, length // SUB, d), 1, 2).reshape(-1, d)


def restore(v, shape):
    length, d = shape[-2:]
    return jnp.swapaxes(v.reshape(-1, length // SUB, SUB, d), 1, 2).reshape(shape)


def tail_rows(v, groups, length):
    d = v.shape[1]
    last = v.reshape(groups, length // SUB, SUB, d)[:, length // SUB - 3 :, SUB - 1]
    return jnp.pad(last, ((0, 0), (0, SUB - 3), (0, 0))).reshape(groups * SUB, d)


def gather(shard):
    return lax.all_gather(shard, ("seq", "fsdp"), axis=0, tiled=True)


def body(
    ends, segment_ids, norm_one, w_branch, w_input, conv_weight, conv_bias, gate_a, gate_i, bias_a, bias_i,
    decay, w_out, norm_two, w_gate, w_up, w_down,
):
    is_first = lax.axis_index("section") == 0
    z = lax.axis_index("seq")
    n, fs = lax.axis_size("seq"), lax.axis_size("fsdp")
    places = n * fs
    micro, seqs, length, dim = ends.shape[1:]
    groups = micro * seqs
    rows = groups * length
    recur = w_branch.shape[2]
    heads, part, block = gate_a.shape[1:]
    hidden_dim = w_gate.shape[2]

    small = jnp.concatenate(
        [norm_one[0].reshape(-1), norm_two[0].reshape(-1), conv_weight[0].reshape(-1), conv_bias[0], bias_a[0],
         bias_i[0], decay[0], gate_a[0].reshape(-1), gate_i[0].reshape(-1)]
    )
    count = small.shape[0]
    padded = -(-count // 2048) * 2048
    small = gather(jnp.pad(small, (0, padded - count)).reshape(1, -1, LANES)).reshape(places, padded)
    w_in = gather(jnp.concatenate([w_branch[0], w_input[0]], axis=1))
    w_out_all = gather(w_out[0])
    w_gu = gather(jnp.concatenate([w_gate[0], w_up[0]], axis=1))
    w_down_all = gather(w_down[0])

    dshare, rshare = dim // places, recur // places
    cuts = [dshare, dshare, CONV * rshare, rshare, rshare, rshare, rshare, heads * part * block, heads * part * block]
    pieces, at = [], 0
    for size in cuts:
        pieces.append(small[:, at : at + size])
        at += size
    gain_one = pieces[0].reshape(1, dim).astype(F32)
    gain_two = pieces[1].reshape(1, dim).astype(F32)
    taps = jnp.swapaxes(pieces[2].reshape(places, CONV, rshare), 0, 1).reshape(CONV, recur).astype(F32)
    decays = pieces[6].reshape(1, recur).astype(F32)
    vec = jnp.concatenate(
        [taps] + [p.reshape(1, recur).astype(F32) for p in pieces[3:6]] + [-8.0 * jax.nn.softplus(decays)], axis=0
    )
    gates_a, gates_i = [
        jnp.swapaxes(p.reshape(places, heads, part, block), 0, 1).reshape(heads, block, block) for p in pieces[7:9]
    ]

    padded_ids = jnp.pad(segment_ids, ((0, 0), (0, 0), (CONV - 1, 0)), constant_values=-1)
    window = lax.dynamic_slice_in_dim(padded_ids, z * length, length + CONV - 1, axis=2)
    current = window[:, :, CONV - 1 :]
    masks = jnp.stack(
        [window[:, :, CONV - 1 - k : CONV - 1 - k + length] == current for k in (1, 1, 2, 3)]
    ).astype(F32)
    masks = jnp.swapaxes(masks.reshape(4, groups, SUB, length // SUB), 2, 3).reshape(4, rows, 1)
    masks = jnp.broadcast_to(masks, (4, rows, LANES))

    def forward(x, halo):
        normed, branch, ext, rate, igate, keep, local, segp, agg = recur_in(
            x, halo, gain_one, w_in, gates_a, gates_i, vec, masks, groups, length
        )
        hin = entering(agg, groups, False)
        hidden, mixed, middle, normed_two = recur_out(
            x, keep, local, branch, segp, hin, w_out_all, gain_two, groups, length
        )
        gate, up, product, out = feed_forward(normed_two, middle, w_gu, w_down_all)
        saved = (normed, branch, ext, rate, igate, keep, hin, hidden, mixed, middle, normed_two, gate, up, product)
        return out, saved

    def backward(dout, x, saved):
        normed, branch, ext, rate, igate, keep, hin, hidden, mixed, middle, normed_two, gate, up, product = saved
        dgate, dup, dmid, out_low, dgain_two = feed_forward_back(
            dout, middle, gain_two, gate, up, w_gu, w_down_all
        )
        dbranch, local, sege, segf, agg = mix_back(out_low, w_out_all, branch, hidden, keep, groups, length)
        gin = entering(agg, groups, True)
        din, head, dga, dgi, dvec = gates_back(
            local, keep, hidden, ext, rate, igate, sege, segf, gin, hin, gates_a, gates_i, vec, masks, groups, length
        )
        back = shifted(head, "seq", -1)
        input_low, dx, dgain_one = recur_in_back(dbranch, din, back, w_in, x, gain_one, dmid, groups, length)
        return dx, dgate, dup, out_low, dbranch, input_low, dgain_one, dgain_two, dga, dgi, dvec

    own = reorder(ends[0])
    tails = tail_rows(own, groups, length)
    out, _ = forward(own, shifted(tails, "seq", 1))
    received = shifted(out, "section", 1)
    received_halo = lax.ppermute(
        tail_rows(out, groups, length), ("section", "seq"), [(i, n + i + 1) for i in range(n - 1)]
    )
    x = jnp.where(is_first, own, received)
    halo = jnp.where(is_first, shifted(tails, "seq", 1), received_halo)
    out, saved = forward(x, halo)
    dx = backward(own, x, saved)[0]
    dout = jnp.where(is_first, shifted(dx, "section", -1), own)
    dx, dgate, dup, out_low, dbranch, input_low, dgain_one, dgain_two, dga, dgi, dvec = backward(dout, x, saved)

    outputs = restore(out, ends.shape)
    grads = restore(dx, ends.shape)

    normed, mixed, normed_two, product = saved[0], saved[8], saved[10], saved[13]
    scatter = Scatter()

    def left(v):
        k = v.shape[1]
        t = v.T.reshape(n, scatter.ny, 2, k // places, rows)
        mine, other = pick(t, scatter.core, 2), scatter.core_swap(pick(t, 1 - scatter.core, 2))
        if scatter.ny == 2:
            keep = [pick(w, scatter.y, 1).reshape(-1, rows) for w in (mine, other)]
            send = [pick(w, 1 - scatter.y, 1).reshape(-1, rows) for w in (mine, other)]
            return tuple(keep + send)
        return mine, other

    def right(v):
        return v, scatter.core_swap(v)

    def sum_of(lefts, rights, chunks):
        total = rights[0].shape[1]
        if scatter.ny == 2:
            step = total // chunks
            parts = []
            for i in range(chunks):
                keep, send = outer(lefts, rights, i * step, step)
                parts.append(scatter.finish(keep.reshape(n, -1, step), send.reshape(n, -1, step)))
            return parts[0] if chunks == 1 else jnp.concatenate(parts, axis=1)
        mine, other = lefts
        grad = nn_dot(mine.reshape(-1, rows), rights[0]) + nn_dot(other.reshape(-1, rows), rights[1])
        grad = grad.astype(BF16).reshape(n, scatter.ny, -1, total)
        return sum_rest(grad)

    def sum_rest(grad):
        over_y = line_sum(lambda d: pick(grad, d, 1), scatter.y, scatter.ny, scatter.y_send).astype(BF16)
        return scatter.over_z(over_y)

    normed_t, mixed_t, normed_two_t, product_t = left(normed), left(mixed), left(normed_two), left(product)
    sum_down = sum_of(product_t, right(dout), 2)
    sum_gate = sum_of(normed_two_t, right(dgate), 2)
    sum_up = sum_of(normed_two_t, right(dup), 2)
    sum_out = sum_of(mixed_t, right(out_low), 1)
    sum_branch = sum_of(normed_t, right(dbranch), 1)
    sum_input = sum_of(normed_t, right(input_low), 1)

    ddecay = -8.0 * jax.nn.sigmoid(decays) * dvec[7:8]
    by_place = [
        dgain_one.reshape(places, -1), dgain_two.reshape(places, -1),
        jnp.swapaxes(dvec[:CONV].reshape(CONV, places, rshare), 0, 1).reshape(places, -1),
        dvec[4].reshape(places, -1), dvec[5].reshape(places, -1), dvec[6].reshape(places, -1),
        ddecay.reshape(places, -1),
        jnp.swapaxes(dga.reshape(heads, places, part, block), 0, 1).reshape(places, -1),
        jnp.swapaxes(dgi.reshape(heads, places, part, block), 0, 1).reshape(places, -1),
    ]
    packed = jnp.pad(jnp.concatenate(by_place, axis=1), ((0, 0), (0, padded - count)))
    packed = packed.reshape(n, scatter.ny, 2, -1, LANES)
    theirs = scatter.core_swap(pick(packed, 1 - scatter.core, 2).astype(BF16))
    packed = add(pick(packed, scatter.core, 2), theirs).astype(BF16)
    if scatter.ny == 2:
        small_sum = scatter.finish(pick(packed, scatter.y, 1), pick(packed, 1 - scatter.y, 1))
    else:
        small_sum = sum_rest(packed)
    small_sum = small_sum.reshape(-1)
    sums, at = [], 0
    for size in cuts:
        sums.append(small_sum[at : at + size])
        at += size

    return (
        outputs,
        grads,
        sums[0][None],
        sum_branch[None],
        sum_input[None],
        sums[2].reshape(1, CONV, rshare),
        sums[3][None],
        sums[7].reshape(gate_a.shape),
        sums[8].reshape(gate_a.shape),
        sums[4][None],
        sums[5][None],
        sums[6][None],
        sum_out[None],
        sums[1][None],
        sum_gate[None],
        sum_up[None],
        sum_down[None],
    )


def solution(mesh):
    tokens = P("section", None, "fsdp", "seq", None)
    vector = P("section", ("seq", "fsdp"))
    matrix = P("section", ("seq", "fsdp"), None)
    taps = P("section", None, ("seq", "fsdp"))
    gates = P("section", None, ("seq", "fsdp"), None)
    weights = (
        vector, matrix, matrix, taps, vector, gates, gates, vector, vector, vector, matrix, vector, matrix, matrix, matrix,
    )
    return jax.shard_map(
        body,
        mesh=mesh,
        in_specs=(tokens, P(None, "fsdp", None)) + weights,
        out_specs=(tokens, tokens) + weights,
        check_vma=False,
    )
```

profile of v0, /device:TPU:0, one launch (start us, length us, event | category | flops | bytes accessed | tf_op | source)
XLA Modules:
  0.0 1439.8 jit_solution(17334095285142532930)
XLA Ops:
  30.0 25.3 %all-gather.8.cloned.1.call-done = bf16[16,272,128]{2,1,0:T(8,128)(2,1)} async-done(((bf16[1,272,128]{2,1,0:T(8,128)(2,1)}), bf16[16,272,128]{2,1,0:T(8,128)(2,1)}) %all-gather.8.cloned.1.call-update) | async-done | bytes 1114128 | tf_op jit(solution)/shard_map/all_gather | solution.py:803
  60.4 97.5 %all-gather.10.cloned.1.call-done.wb_ref.wi_ref = bf16[1536,4096]{1,0:T(8,128)(2,1)} async-done(((bf16[96,4096]{1,0:T(8,128)(2,1)}), bf16[1536,4096]{1,0:T(8,128)(2,1)}) %all-gather.10.cloned.1.call-update) | async-done | bytes 12582928 | tf_op jit(solution)/shard_map/all_gather | solution.py:803
  159.2 23.2 %shard_map.296 = (bf16[512,1536]{1,0:T(8,128)(2,1)}, f32[512,2048]{1,0:T(8,128)}, f32[2,280,2048]{2,1,0:T(8,128)}, f32[512,2048]{1,0:T(8,128)}, f32[512,2048]{1,...) custom-call(bf16[512,1536]{1,0:T(8,128)(2,1)} %bitcast.360, ...), custom_call_target="tpu_custom_call" | custom-call | flops 9663676416 | bytes 37748736 | tf_op jit(solution)/shard_map/pallas_call | solution.py:56
  192.8 27.4 %all-gather.14.cloned.1.call-done = bf16[1,2048,1536]{2,1,0:T(8,128)(2,1)} async-done(((bf16[1,128,1536]{2,1,0:T(8,128)(2,1)}), bf16[1,2048,1536]{2,1,0:T(8,128)(2,1)}) %all-gather.14.cloned.1.call-update) | async-done | bytes 6291472 | tf_op jit(solution)/shard_map/all_gather | solution.py:803
  220.2 18.0 %shard_map.297 = (f32[512,2048]{1,0:T(8,128)}, bf16[512,2048]{1,0:T(8,128)(2,1)}, f32[512,1536]{1,0:T(8,128)}, bf16[512,1536]{1,0:T(8,128)(2,1)}) custom-call(bf16[512,1536]{1,0:T(8,128)(2,1)} %bitcast.361, f32[512,2048]{1,0:T(8,128)} %get-tuple-element.96.keep_ref, f32[512,2048]{1,0:T(8,128)} %get-tuple-element.97.local_ref, ...), custom_call_target="tpu_custom_call" | custom-call | flops 4831838208 | bytes 25165824 | tf_op jit(solution)/shard_map/pallas_call | solution.py:56
  238.2 93.4 %all-gather.16.cloned.1.call-done = bf16[1,4608,1536]{2,1,0:T(8,128)(2,1)} async-done(((bf16[1,288,1536]{2,1,0:T(8,128)(2,1)}), bf16[1,4608,1536]{2,1,0:T(8,128)(2,1)}) %all-gather.16.cloned.1.call-update) | async-done | bytes 14155792 | tf_op jit(solution)/shard_map/all_gather | solution.py:803
  331.6 143.6 %all-gather.12.cloned.1.call-done.wg_ref.wu_ref = bf16[1536,9216]{1,0:T(8,128)(2,1)} async-done(((bf16[96,9216]{1,0:T(8,128)(2,1)}), bf16[1536,9216]{1,0:T(8,128)(2,1)}) %all-gather.12.cloned.1.call-update) | async-done | bytes 28311568 | tf_op jit(solution)/shard_map/all_gather | solution.py:803
  475.3 32.9 %shard_map.298 = (bf16[512,4608]{1,0:T(8,128)(2,1)}, bf16[512,4608]{1,0:T(8,128)(2,1)}, bf16[512,4608]{1,0:T(8,128)(2,1)}, bf16[512,1536]{1,0:T(8,128)(2,1)}) custom-call(bf16[512,1536]{1,0:T(8,128)(2,1)} %get-tuple-element.101.x_ref, f32[512,1536]{1,0:T(8,128)} %get-tuple-element.102.mid_ref, ...), custom_call_target="tpu_custom_call" | custom-call | flops 21743271936 | bytes 42467328 | tf_op jit(solution)/shard_map/pallas_call | solution.py:56
  517.2 28.8 %collective-permute-done.4 = bf16[512,1536]{1,0:T(8,128)(2,1)S(1)} collective-permute-done((bf16[512,1536]{1,0:T(8,128)(2,1)}, bf16[512,1536]{1,0:T(8,128)(2,1)S(1)}, u32[]{:S(2)}, u32[]{:S(2)}) %collective-permute-start.4) | collective-permute-done | bytes 1572896 | tf_op jit(solution)/shard_map/ppermute | solution.py:717
  547.4 23.1 %shard_map.299 = (bf16[512,1536]{1,0:T(8,128)(2,1)}, f32[512,2048]{1,0:T(8,128)}, f32[2,280,2048]{2,1,0:T(8,128)}, f32[512,2048]{1,0:T(8,128)}, f32[512,2048]{1,...) custom-call(bf16[512,1536]{1,0:T(8,128)(2,1)} %broadcast_select_fusion.1.x_ref, ...), custom_call_target="tpu_custom_call" | custom-call | flops 9663676416 | bytes 37748736 | tf_op jit(solution)/shard_map/pallas_call | solution.py:56
  583.2 17.7 %shard_map.300 = (f32[512,2048]{1,0:T(8,128)}, bf16[512,2048]{1,0:T(8,128)(2,1)}, f32[512,1536]{1,0:T(8,128)}, bf16[512,1536]{1,0:T(8,128)(2,1)}) custom-call(bf16[512,1536]{1,0:T(8,128)(2,1)} %broadcast_select_fusion.1.x_ref, f32[512,2048]{1,0:T(8,128)} %get-tuple-element.104.keep_ref, f32[512,2048]{1,0:T(8,128)} %get-tuple-element.105.local_ref, ...), custom_call_target="tpu_custom_call" | custom-call | flops 4831838208 | bytes 25165824 | tf_op jit(solution)/shard_map/pallas_call | solution.py:56
  600.9 32.9 %shard_map.301 = (bf16[512,4608]{1,0:T(8,128)(2,1)}, bf16[512,4608]{1,0:T(8,128)(2,1)}, bf16[512,4608]{1,0:T(8,128)(2,1)}, bf16[512,1536]{1,0:T(8,128)(2,1)}) custom-call(bf16[512,1536]{1,0:T(8,128)(2,1)} %get-tuple-element.109.x_ref, f32[512,1536]{1,0:T(8,128)} %get-tuple-element.110.mid_ref, ...), custom_call_target="tpu_custom_call" | custom-call | flops 21743271936 | bytes 42467328 | tf_op jit(solution)/shard_map/pallas_call | solution.py:56
  633.8 41.3 %shard_map.302 = (bf16[512,4608]{1,0:T(8,128)(2,1)}, bf16[512,4608]{1,0:T(8,128)(2,1)}, f32[512,1536]{1,0:T(8,128)}, bf16[512,1536]{1,0:T(8,128)(2,1)}, f32[1,1536]{1,0:T(1,128)}) custom-call(bf16[512,1536]{1,0:T(8,128)(2,1)} %bitcast.362, f32[512,1536]{1,0:T(8,128)} %get-tuple-element.110.mid_ref, f32[1,1536]{1,0:T(1,128)} %reshape.624.gain_ref, ...), custom_call_target="tpu_custom_call" | custom-call | flops 26091925504 | bytes 42467328 | tf_op jit(solution)/shard_map/pallas_call | solution.py:56
  675.1 14.9 %shard_map.303 = (bf16[512,2048]{1,0:T(8,128)(2,1)}, f32[512,2048]{1,0:T(8,128)}, f32[16,2048]{1,0:T(8,128)}, f32[16,2048]{1,0:T(8,128)}, f32[4,2048]{1,0:T(4,128)}) custom-call(bf16[512,1536]{1,0:T(8,128)(2,1)} %get-tuple-element.114.low_ref, bf16[2048,1536]{1,0:T(8,128)(2,1)} %bitcast.365, f32[512,2048]{1,0:T(8,128)} %get-tuple-element.106.branch_ref, ...), custom_call_target="tpu_custom_call" | custom-call | flops 6442450944 | bytes 25165824 | tf_op jit(solution)/shard_map/pallas_call | solution.py:56
  702.2 18.9 %shard_map.304 = (f32[512,2048]{1,0:T(8,128)}, f32[16,2048]{1,0:T(8,128)}, f32[16,128,128]{2,1,0:T(8,128)}, f32[16,128,128]{2,1,0:T(8,128)}, f32[8,2048]{1,0:T(8,128)}) custom-call(f32[512,2048]{1,0:T(8,128)} %get-tuple-element.117.local_ref, f32[512,2048]{1,0:T(8,128)} %get-tuple-element.104.keep_ref, f32[512,2048]{1,0:T(8,128)} %get-tuple-element.115.hidden_ref, ...), custom_call_target="tpu_custom_call" | custom-call | flops 4294967296 | bytes 29360128 | tf_op jit(solution)/shard_map/pallas_call | solution.py:56
  728.9 18.4 %shard_map.305 = (bf16[512,2048]{1,0:T(8,128)(2,1)}, bf16[512,1536]{1,0:T(8,128)(2,1)}, f32[1,1536]{1,0:T(1,128)}) custom-call(bf16[512,2048]{1,0:T(8,128)(2,1)} %get-tuple-element.116.dbranch_ref, f32[512,2048]{1,0:T(8,128)} %get-tuple-element.124.din_ref, f32[16,2048]{1,0:T(8,128)} %copy-done.27, ...), custom_call_target="tpu_custom_call" | custom-call | flops 6442450944 | bytes 20971520 | tf_op jit(solution)/shard_map/pallas_call | solution.py:56
  784.4 41.4 %shard_map.306 = (bf16[512,4608]{1,0:T(8,128)(2,1)}, bf16[512,4608]{1,0:T(8,128)(2,1)}, f32[512,1536]{1,0:T(8,128)}, bf16[512,1536]{1,0:T(8,128)(2,1)}, f32[1,1536]{1,0:T(1,128)}) custom-call(bf16[512,1536]{1,0:T(8,128)(2,1)} %broadcast_select_fusion.dout_ref.right_a, f32[512,1536]{1,0:T(8,128)} %get-tuple-element.110.mid_ref, f32[1,1536]{1,0:T(1,128)} %reshape.624.gain_ref, ...), custom_call_target="tpu_custom_call" | custom-call | flops 26091925504 | bytes 42467328 | tf_op jit(solution)/shard_map/pallas_call | solution.py:56
  825.8 14.9 %shard_map.307 = (bf16[512,2048]{1,0:T(8,128)(2,1)}, f32[512,2048]{1,0:T(8,128)}, f32[16,2048]{1,0:T(8,128)}, f32[16,2048]{1,0:T(8,128)}, f32[4,2048]{1,0:T(4,128)}) custom-call(bf16[512,1536]{1,0:T(8,128)(2,1)} %get-tuple-element.128.low_ref.right_a, bf16[2048,1536]{1,0:T(8,128)(2,1)} %bitcast.366, f32[512,2048]{1,0:T(8,128)} %get-tuple-element.106.branch_ref, ...), custom_call_target="tpu_custom_call" | custom-call | flops 6442450944 | bytes 25165824 | tf_op jit(solution)/shard_map/pallas_call | solution.py:56
  860.3 18.9 %shard_map.308 = (f32[512,2048]{1,0:T(8,128)}, f32[16,2048]{1,0:T(8,128)}, f32[16,128,128]{2,1,0:T(8,128)}, f32[16,128,128]{2,1,0:T(8,128)}, f32[8,2048]{1,0:T(8,128)}) custom-call(f32[512,2048]{1,0:T(8,128)} %get-tuple-element.130.local_ref, f32[512,2048]{1,0:T(8,128)} %get-tuple-element.104.keep_ref, f32[512,2048]{1,0:T(8,128)} %get-tuple-element.115.hidden_ref, ...), custom_call_target="tpu_custom_call" | custom-call | flops 4294967296 | bytes 29360128 | tf_op jit(solution)/shard_map/pallas_call | solution.py:56
  897.7 18.5 %shard_map.309 = (bf16[512,2048]{1,0:T(8,128)(2,1)}, bf16[512,1536]{1,0:T(8,128)(2,1)}, f32[1,1536]{1,0:T(1,128)}) custom-call(bf16[512,2048]{1,0:T(8,128)(2,1)} %get-tuple-element.129.dbranch_ref.right_a, f32[512,2048]{1,0:T(8,128)} %get-tuple-element.134.din_ref, f32[16,2048]{1,0:T(8,128)} %copy-done.26, ...), custom_call_target="tpu_custom_call" | custom-call | flops 6442450944 | bytes 20971520 | tf_op jit(solution)/shard_map/pallas_call | solution.py:56
  978.3 12.3 collective-permute-done.46
  1110.7 32.1 %collective-permute-done.47 = bf16[4,96,2304]{2,1,0:T(8,128)(2,1)S(1)} collective-permute-done((bf16[4,96,2304]{2,1,0:T(8,128)(2,1)}, bf16[4,96,2304]{2,1,0:T(8,128)(2,1)S(1)}, u32[]{:S(2)}, u32[]{:S(2)}) %collective-permute-start.47) | collective-permute-done | bytes 1769504 | tf_op jit(solution)/shard_map/ppermute | solution.py:761
  1194.0 21.9 %collective-permute-done.48 = bf16[4,96,2304]{2,1,0:T(8,128)(2,1)S(1)} collective-permute-done((bf16[4,96,2304]{2,1,0:T(8,128)(2,1)S(1)}, bf16[4,96,2304]{2,1,0:T(8,128)(2,1)S(1)}, u32[]{:S(2)}, u32[]{:S(2)}) %collective-permute-start.48) | collective-permute-done | bytes 1769504 | tf_op jit(solution)/shard_map/ppermute | solution.py:761
  1417.8 14.2 collective-permute-done.56
  (489 shorter events, 592.2 us)
Async XLA Ops:
  14.3 143.6 %all-gather.10.cloned.1.call-start = ((), (), s32[]{:S(2)}) async-start(), calls=%async_computation.1 | async-start | bytes 13369344 | tf_op jit(solution)/shard_map/all_gather | solution.py:803
  16.5 203.7 %all-gather.14.cloned.1.call-start = ((), (), s32[]{:S(2)}) async-start(), calls=%async_computation.3 | async-start | bytes 6684672 | tf_op jit(solution)/shard_map/all_gather | solution.py:803
  17.3 314.4 %all-gather.16.cloned.1.call-start = ((), (), s32[]{:S(2)}) async-start(), calls=%async_computation.4 | async-start | bytes 15040512 | tf_op jit(solution)/shard_map/all_gather | solution.py:803
  17.9 457.4 %all-gather.12.cloned.1.call-start = ((), (), s32[]{:S(2)}) async-start(), calls=%async_computation.2 | async-start | bytes 30081024 | tf_op jit(solution)/shard_map/all_gather | solution.py:803
  750.4 191.0 %collective-permute-start.19 = (bf16[4,2,96,512]{3,2,1,0:T(8,128)(2,1)}, bf16[4,2,96,512]{3,2,1,0:T(8,128)(2,1)}, u32[]{:S(2)}, u32[]{:S(2)}) collective-permute-start(bf16[4,2,96,512]{3,2,1,0:T(8,128)(2,1)} %dynamic-slice_bitcast_fusion.2), channel_id=1, source_target_pairs={{0,1},{1,0},{2,3},{3,2},{4,5},{5,4},{6,7},{7,6},{8,9},{9,8},{10,11... | collective-permute-start | bytes 2359304 | tf_op jit(solution)/shard_map/ppermute | solution.py:758
  753.5 195.8 %collective-permute-start.21 = (bf16[4,2,96,512]{3,2,1,0:T(8,128)(2,1)}, bf16[4,2,96,512]{3,2,1,0:T(8,128)(2,1)}, u32[]{:S(2)}, u32[]{:S(2)}) collective-permute-start(bf16[4,2,96,512]{3,2,1,0:T(8,128)(2,1)} %dynamic-slice_bitcast_fusion.1), channel_id=1, source_target_pairs={{0,1},{1,0},{2,3},{3,2},{4,5},{5,4},{6,7},{7,6},{8,9},{9,8},{10,11... | collective-permute-start | bytes 2359304 | tf_op jit(solution)/shard_map/ppermute | solution.py:758
  763.3 120.7 %collective-permute-start.24 = (bf16[4,2,288,512]{3,2,1,0:T(8,128)(2,1)}, bf16[4,2,288,512]{3,2,1,0:T(8,128)(2,1)}, u32[]{:S(2)}, u32[]{:S(2)}) collective-permute-start(bf16[4,2,288,512]{3,2,1,0:T(8,128)(2,1)} %dynamic-slice_bitcast_fusion), channel_id=1, source_target_pairs={{0,1},{1,0},{2,3},{3,2},{4,5},{5,4},{6,7},{7,6},{8,9},{9,8},{10,11... | collective-permute-start | bytes 7077896 | tf_op jit(solution)/shard_map/ppermute | solution.py:758
  856.1 94.6 %collective-permute-start.44 = (bf16[4,2,128,512]{3,2,0,1:T(8,128)(2,1)}, bf16[4,2,128,512]{3,2,0,1:T(8,128)(2,1)}, u32[]{:S(2)}, u32[]{:S(2)}) collective-permute-start(bf16[4,2,128,512]{3,2,0,1:T(8,128)(2,1)} %bitcast.103), channel_id=1, source_target_pairs={{0,1},{1,0},{2,3},{3,2},{4,5},{5,4},{6,7},{7,6},{8,9},{9,8},{10,11... | collective-permute-start | bytes 3145736 | tf_op jit(solution)/shard_map/ppermute | solution.py:758
  884.0 172.0 %collective-permute-start.23 = (bf16[512,4608]{1,0:T(8,128)(2,1)}, bf16[512,4608]{1,0:T(8,128)(2,1)}, u32[]{:S(2)}, u32[]{:S(2)}) collective-permute-start(bf16[512,4608]{1,0:T(8,128)(2,1)} %get-tuple-element.147.right_a), channel_id=1, source_target_pairs={{0,1},{1,0},{2,3},{3,2},{4,5},{5,4},{6,7},{7,6},{8,9},{9,8},{10,11... | collective-permute-start | bytes 14155784 | tf_op jit(solution)/shard_map/ppermute | solution.py:758
  897.0 76.5 %collective-permute-start.26 = (bf16[4,288,768]{2,1,0:T(8,128)(2,1)}, bf16[4,288,768]{2,1,0:T(8,128)(2,1)}, u32[]{:S(2)}, u32[]{:S(2)}) collective-permute-start(bf16[4,288,768]{2,1,0:T(8,128)(2,1)} %bitcast.477), channel_id=1, source_target_pairs={{0,2},{1,3},{2,0},{3,1},{4,6},{5,7},{6,4},{7,5},{8,10},{9,11},{10,... | collective-permute-start | bytes 5308424 | tf_op jit(solution)/shard_map/ppermute | solution.py:761
  965.0 106.7 %collective-permute-start.22 = (bf16[512,4608]{1,0:T(8,128)(2,1)}, bf16[512,4608]{1,0:T(8,128)(2,1)}, u32[]{:S(2)}, u32[]{:S(2)}) collective-permute-start(bf16[512,4608]{1,0:T(8,128)(2,1)} %get-tuple-element.145.right_a), channel_id=1, source_target_pairs={{0,1},{1,0},{2,3},{3,2},{4,5},{5,4},{6,7},{7,6},{8,9},{9,8},{10,11... | collective-permute-start | bytes 14155784 | tf_op jit(solution)/shard_map/ppermute | solution.py:758
  973.5 48.2 %collective-permute-start.20 = (bf16[512,2048]{1,0:T(8,128)(2,1)S(1)}, bf16[512,2048]{1,0:T(8,128)(2,1)}, u32[]{:S(2)}, u32[]{:S(2)}) collective-permute-start(bf16[512,2048]{1,0:T(8,128)(2,1)S(1)} %copy-done.7), channel_id=1, source_target_pairs={{0,1},{1,0},{2,3},{3,2},{4,5},{5,4},{6,7},{7,6},{8,9},{9,8},{10,11... | collective-permute-start | bytes 6291464 | tf_op jit(solution)/shard_map/ppermute | solution.py:758
  978.0 62.1 %collective-permute-start.43 = (bf16[512,2048]{1,0:T(8,128)(2,1)}, bf16[512,2048]{1,0:T(8,128)(2,1)}, u32[]{:S(2)}, u32[]{:S(2)}) collective-permute-start(bf16[512,2048]{1,0:T(8,128)(2,1)} %get-tuple-element.156.right_a), channel_id=1, source_target_pairs={{0,1},{1,0},{2,3},{3,2},{4,5},{5,4},{6,7},{7,6},{8,9},{9,8},{10,11... | collective-permute-start | bytes 6291464 | tf_op jit(solution)/shard_map/ppermute | solution.py:758
  1071.7 71.1 %collective-permute-start.47 = (bf16[4,96,2304]{2,1,0:T(8,128)(2,1)}, bf16[4,96,2304]{2,1,0:T(8,128)(2,1)S(1)}, u32[]{:S(2)}, u32[]{:S(2)}) collective-permute-start(bf16[4,96,2304]{2,1,0:T(8,128)(2,1)} %bitcast.481), channel_id=1, source_target_pairs={{0,2},{1,3},{2,0},{3,1},{4,6},{5,7},{6,4},{7,5},{8,10},{9,11},{10,... | collective-permute-start | bytes 5308424 | tf_op jit(solution)/shard_map/ppermute | solution.py:761
  1109.3 83.5 %collective-permute-start.28 = (bf16[4,96,2304]{2,1,0:T(8,128)(2,1)S(1)}, bf16[4,96,2304]{2,1,0:T(8,128)(2,1)S(1)}, u32[]{:S(2)}, u32[]{:S(2)}) collective-permute-start(bf16[4,96,2304]{2,1,0:T(8,128)(2,1)S(1)} %bitcast.479), channel_id=1, source_target_pairs={{0,2},{1,3},{2,0},{3,1},{4,6},{5,7},{6,4},{7,5},{8,10},{9,11},{10,... | collective-permute-start | bytes 5308424 | tf_op jit(solution)/shard_map/ppermute | solution.py:761
  1142.8 73.1 %collective-permute-start.48 = (bf16[4,96,2304]{2,1,0:T(8,128)(2,1)S(1)}, bf16[4,96,2304]{2,1,0:T(8,128)(2,1)S(1)}, u32[]{:S(2)}, u32[]{:S(2)}) collective-permute-start(bf16[4,96,2304]{2,1,0:T(8,128)(2,1)S(1)} %bitcast.480), channel_id=1, source_target_pairs={{0,2},{1,3},{2,0},{3,1},{4,6},{5,7},{6,4},{7,5},{8,10},{9,11},{10,... | collective-permute-start | bytes 5308424 | tf_op jit(solution)/shard_map/ppermute | solution.py:761
  1177.8 64.0 %collective-permute-start.71 = (bf16[96,2304]{1,0:T(8,128)(2,1)S(1)}, bf16[96,2304]{1,0:T(8,128)(2,1)S(1)}, u32[]{:S(2)}, u32[]{:S(2)}) collective-permute-start(bf16[96,2304]{1,0:T(8,128)(2,1)S(1)} %get-tuple-element.188), channel_id=1, source_target_pairs={{0,4},{4,8},{8,12},{1,5},{5,9},{9,13},{2,6},{6,10},{10,14},{3,7},{... | collective-permute-start | bytes 1327112 | tf_op jit(solution)/shard_map/ppermute | solution.py:776
  1187.4 68.9 %collective-permute-start.65 = (bf16[96,2304]{1,0:T(8,128)(2,1)S(1)}, bf16[96,2304]{1,0:T(8,128)(2,1)S(1)}, u32[]{:S(2)}, u32[]{:S(2)}) collective-permute-start(bf16[96,2304]{1,0:T(8,128)(2,1)S(1)} %get-tuple-element.186), channel_id=1, source_target_pairs={{0,4},{4,8},{8,12},{1,5},{5,9},{9,13},{2,6},{6,10},{10,14},{3,7},{... | collective-permute-start | bytes 1327112 | tf_op jit(solution)/shard_map/ppermute | solution.py:776
  1215.9 66.4 %collective-permute-start.29 = (bf16[4,96,2048]{2,1,0:T(8,128)(2,1)S(1)}, bf16[4,96,2048]{2,1,0:T(8,128)(2,1)S(1)}, u32[]{:S(2)}, u32[]{:S(2)}) collective-permute-start(bf16[4,96,2048]{2,1,0:T(8,128)(2,1)S(1)} %bitcast.485), channel_id=1, source_target_pairs={{0,2},{1,3},{2,0},{3,1},{4,6},{5,7},{6,4},{7,5},{8,10},{9,11},{10,... | collective-permute-start | bytes 4718600 | tf_op jit(solution)/shard_map/ppermute | solution.py:761
  1219.2 64.9 %collective-permute-start.49 = (bf16[4,128,1536]{2,1,0:T(8,128)(2,1)S(1)}, bf16[4,128,1536]{2,1,0:T(8,128)(2,1)S(1)}, u32[]{:S(2)}, u32[]{:S(2)}) collective-permute-start(bf16[4,128,1536]{2,1,0:T(8,128)(2,1)S(1)} %bitcast.484), channel_id=1, source_target_pairs={{0,2},{1,3},{2,0},{3,1},{4,6},{5,7},{6,4},{7,5},{8,10},{9,11},{10,... | collective-permute-start | bytes 4718600 | tf_op jit(solution)/shard_map/ppermute | solution.py:761
  1267.5 76.1 %collective-permute-start.83 = (bf16[96,2304]{1,0:T(8,128)(2,1)S(1)}, bf16[96,2304]{1,0:T(8,128)(2,1)S(1)}, u32[]{:S(2)}, u32[]{:S(2)}) collective-permute-start(bf16[96,2304]{1,0:T(8,128)(2,1)S(1)} %get-tuple-element.184), channel_id=1, source_target_pairs={{0,4},{4,8},{8,12},{1,5},{5,9},{9,13},{2,6},{6,10},{10,14},{3,7},{... | collective-permute-start | bytes 1327112 | tf_op jit(solution)/shard_map/ppermute | solution.py:776
  1276.9 74.3 %collective-permute-start.77 = (bf16[96,2304]{1,0:T(8,128)(2,1)S(1)}, bf16[96,2304]{1,0:T(8,128)(2,1)S(1)}, u32[]{:S(2)}, u32[]{:S(2)}) collective-permute-start(bf16[96,2304]{1,0:T(8,128)(2,1)S(1)} %get-tuple-element.182), channel_id=1, source_target_pairs={{0,4},{4,8},{8,12},{1,5},{5,9},{9,13},{2,6},{6,10},{10,14},{3,7},{... | collective-permute-start | bytes 1327112 | tf_op jit(solution)/shard_map/ppermute | solution.py:776
  1316.9 53.2 %collective-permute-start.50 = (bf16[4,96,2048]{2,1,0:T(8,128)(2,1)S(1)}, bf16[4,96,2048]{2,1,0:T(8,128)(2,1)S(1)}, u32[]{:S(2)}, u32[]{:S(2)}) collective-permute-start(bf16[4,96,2048]{2,1,0:T(8,128)(2,1)S(1)} %bitcast.483), channel_id=1, source_target_pairs={{0,2},{1,3},{2,0},{3,1},{4,6},{5,7},{6,4},{7,5},{8,10},{9,11},{10,... | collective-permute-start | bytes 4718600 | tf_op jit(solution)/shard_map/ppermute | solution.py:761
  1357.7 56.2 %collective-permute-start.39 = (bf16[96,2048]{1,0:T(8,128)(2,1)S(1)}, bf16[96,2048]{1,0:T(8,128)(2,1)S(1)}, u32[]{:S(2)}, u32[]{:S(2)}) collective-permute-start(bf16[96,2048]{1,0:T(8,128)(2,1)S(1)} %get-tuple-element.194), channel_id=1, source_target_pairs={{0,4},{4,8},{8,12},{1,5},{5,9},{9,13},{2,6},{6,10},{10,14},{3,7},{... | collective-permute-start | bytes 1179656 | tf_op jit(solution)/shard_map/ppermute | solution.py:776
  (124 other events, 1953.4 us)
Sparse Core Ops, SparseCore 0:
  14.4 40.8 all-gather.7
  58.2 99.6 all-gather.9
  160.2 60.0 all-gather.13
  222.4 109.2 all-gather.15
  333.7 141.5 all-gather.11
where the time goes:
time: 1450 us; the launch traced here: 1440 us
  waiting for transfers between devices  658 us (45%)
  Pallas kernels  400 us (28%)
  starting transfers between devices  212 us (15%)
  local copies, waits for them, and re-layouts  112 us (8%)
  other arithmetic  41.8 us (3%)
  between operations  16 us (1%)
    pallas_call x23, Pallas kernels, call(): pl.pallas_call(kernel, grid=grid, in_specs=in_specs, out_specs=out_specs,...  400 us
    all_gather x5, waiting for transfers between devices, gather(): return lax.all_gather(shard, ('seq', 'fsdp'), axis=0, tiled=True)  387 us
    ppermute x60, starting transfers between devices, over_z(): lax.ppermute(v, 'seq', pairs)  157 us
    ppermute x60, waiting for transfers between devices, over_z(): lax.ppermute(v, 'seq', pairs)  135 us
    ppermute x10, waiting for transfers between devices, y_send(): lax.ppermute(value, 'fsdp', [(2 * a + c, 2 * b + c) for a, b in pairs for...  70.4 us
    ppermute x17, waiting for transfers between devices, shifted(): return lax.ppermute(value, axis, pairs)  62.7 us
    ppermute x17, starting transfers between devices, shifted(): return lax.ppermute(value, axis, pairs)  38.5 us
    unnamed x110, local copies, waits for them, and re-layouts  36.1 us
  transfers between devices with their start and end apart: 104, of which 51 were waited for; matrix products, arithmetic and copies ran while one was open for 9% of the time, Pallas kernels for 14%

commit v1 on v0

--- a/solution.py
+++ b/solution.py
@@ -14,6 +14,7 @@
 VMEM_BYTES = 56 << 20
 LANES = 128
 SUB = 8
+COST = 4
 
 
 def nn_dot(a, b):
@@ -64,7 +65,7 @@
             dimension_semantics=("arbitrary",) * len(grid), vmem_limit_bytes=VMEM_BYTES
         ),
         cost_estimate=pl.CostEstimate(
-            flops=int(flops), bytes_accessed=int(bytes_accessed), transcendentals=0
+            flops=int(flops) // COST, bytes_accessed=int(bytes_accessed) // COST, transcendentals=0
         ),
     )(*args)
 
@@ -83,13 +84,13 @@
 
 def recur_in_kernel(
     groups, length,
-    x_ref, halo_ref, gain_ref, wb_ref, wi_ref, ga_ref, gi_ref, vec_ref, mask_ref,
-    normed_ref, branch_ref, ext_ref, rate_ref, igate_ref, keep_ref, local_ref, segp_ref, agg_ref,
+    x_ref, halo_ref, gain_ref, wi_ref, ga_ref, gi_ref, vec_ref, mask_ref,
+    normed_ref, ext_ref, rate_ref, igate_ref, keep_ref, local_ref, segp_ref, agg_ref,
     xn, conv, pre_a, pre_i,
 ):
     rows = groups * length
     steps = length // SUB
-    width = wb_ref.shape[1]
+    width = wi_ref.shape[1]
 
     @pl.when(pl.program_id(0) == 0)
     def _():
@@ -100,7 +101,6 @@
             xn[at : at + ref.shape[0], :] = (v * r * gain).astype(BF16)
         normed_ref[...] = xn[0:rows, :]
 
-    branch_ref[...] = nn_dot(xn[0:rows, :], wb_ref[...])
     conv_in = nn_dot(xn[...], wi_ref[...]).astype(BF16).astype(F32)
     sub = lax.broadcasted_iota(jnp.int32, (SUB, width), 0)
     for g in range(groups):
@@ -162,9 +162,9 @@
         agg_ref[2 * g + 1 : 2 * g + 2, :] = b
 
 
-def recur_in(x, halo, gain, w_in, gate_a, gate_i, vec, masks, groups, length):
+def recur_in(x, halo, gain, w_in, first, gate_a, gate_i, vec, masks, groups, length):
     rows, dim = x.shape
-    recur = w_in.shape[1] // 2
+    recur = vec.shape[1]
     width = 256
     blocks = recur // width
     block_f32 = columns(rows, width)
@@ -175,35 +175,58 @@
         (blocks,),
         [
             whole(x.shape), whole(halo.shape), whole(gain.shape),
-            columns(dim, width), columns(dim, width, blocks),
+            columns(dim, width, (first + recur) // width),
             pl.BlockSpec((heads, LANES, LANES), lambda c: (c, 0, 0)),
             pl.BlockSpec((heads, LANES, LANES), lambda c: (c, 0, 0)),
             columns(8, width), whole(masks.shape),
         ],
         [
-            whole((rows, dim)), block_f32,
+            whole((rows, dim)),
             pl.BlockSpec((groups, ext_len, width), lambda c: (0, 0, c)),
             block_f32, block_f32, block_f32, block_f32,
             columns(SUB * groups, width), columns(2 * groups, width),
         ],
         [
-            struct((rows, dim), BF16), struct((rows, recur), F32), struct((groups, ext_len, recur), F32),
+            struct((rows, dim), BF16), struct((groups, ext_len, recur), F32),
             struct((rows, recur), F32), struct((rows, recur), F32), struct((rows, recur), F32),
             struct((rows, recur), F32), struct((SUB * groups, recur), F32), struct((2 * groups, recur), F32),
         ],
         [
-            pltpu.VMEM((rows + SUB * groups, dim), BF16), pltpu.VMEM((rows, width), F32),
+            pltpu.VMEM((rows + halo.shape[0], dim), BF16), pltpu.VMEM((rows, width), F32),
             pltpu.VMEM((rows, width), F32), pltpu.VMEM((rows, width), F32),
         ],
-        4 * rows * dim * recur * 1.5,
-        dim * recur * 4 + rows * recur * 4 * 6,
-        (x, halo, gain, w_in, w_in, gate_a, gate_i, vec, masks),
+        2 * rows * dim * recur * 2.5,
+        dim * recur * 2 + rows * recur * 4 * 5,
+        (x, halo, gain, w_in, gate_a, gate_i, vec, masks),
+    )
+
+
+def branch_kernel(x_ref, w_ref, act_ref, slope_ref):
+    act, slope = gelu_both(nn_dot(x_ref[...], w_ref[...]))
+    act_ref[...] = act
+    slope_ref[...] = slope
+
+
+def branch_in(x, w_in, first, recur):
+    rows, dim = x.shape
+    width = 256
+    block = columns(rows, width)
+    return call(
+        branch_kernel,
+        (recur // width,),
+        [whole(x.shape), columns(dim, width, first // width)],
+        [block, block],
+        [struct((rows, recur), F32)] * 2,
+        [],
+        2 * rows * dim * recur * 1.5,
+        dim * recur * 2 + rows * recur * 8,
+        (x, w_in),
     )
 
 
 def recur_out_kernel(
     groups, length,
-    x_ref, keep_ref, local_ref, branch_ref, segp_ref, hin_ref, wo_ref, gain_ref,
+    x_ref, keep_ref, local_ref, act_ref, segp_ref, hin_ref, wo_ref, gain_ref,
     hidden_ref, mixed_ref, middle_ref, normed_ref,
     acc,
 ):
@@ -235,7 +258,7 @@
                 moved.append(q)
             hidden = local_ref[here, :] + jnp.concatenate(moved, axis=0)
             hidden_ref[here, :] = hidden
-            mixed_ref[here, :] = (hidden * gelu(branch_ref[here, :])).astype(BF16)
+            mixed_ref[here, :] = (hidden * act_ref[here, :]).astype(BF16)
             out.append(q)
         return tuple(out)
 
@@ -258,7 +281,7 @@
         normed_ref[...] = (m * r * gain_ref[...]).astype(BF16)
 
 
-def recur_out(x, keep, local, branch, segp, hin, w_out, gain, groups, length):
+def recur_out(x, keep, local, act, segp, hin, w_out, gain, groups, length):
     rows, dim = x.shape
     recur = keep.shape[1]
     width = 256
@@ -278,19 +301,25 @@
         [pltpu.VMEM((rows, dim), F32)],
         2 * rows * dim * recur * 1.5,
         dim * recur * 2 + rows * recur * 18,
-        (x, keep, local, branch, segp, hin, w_out, gain),
-    )
-
-
-def ff_kernel(x_ref, mid_ref, wg_ref, wu_ref, wd_ref, gate_ref, up_ref, product_ref, out_ref, acc):
+        (x, keep, local, act, segp, hin, w_out, gain),
+    )
+
+
+def ff_kernel(save, x_ref, mid_ref, wg_ref, wu_ref, wd_ref, *refs):
     c = pl.program_id(0)
+    out_ref, acc = refs[-2:]
     x = x_ref[...]
     gate = nn_dot(x, wg_ref[...])
     up = nn_dot(x, wu_ref[...])
-    gate_ref[...] = gate.astype(BF16)
-    up_ref[...] = up.astype(BF16)
-    product = (gelu(gate) * up).astype(BF16)
-    product_ref[...] = product
+    if save:
+        act_ref, slope_ref, product_ref = refs[:3]
+        act, slope = gelu_both(gate)
+        act_ref[...] = act.astype(BF16)
+        slope_ref[...] = (up * slope).astype(BF16)
+        product = (act * up).astype(BF16)
+        product_ref[...] = product
+    else:
+        product = (gelu(gate) * up).astype(BF16)
     part = nn_dot(product, wd_ref[...])
 
     @pl.when(c == 0)
@@ -306,23 +335,24 @@
         out_ref[...] = acc[...].astype(BF16)
 
 
-def feed_forward(x, middle, w_gu, w_down):
+def feed_forward(x, middle, w_gu, w_down, save):
     rows, dim = x.shape
     hidden = w_down.shape[0]
     width = 512
     blocks = hidden // width
     block = columns(rows, width)
+    kept = 3 if save else 0
     return call(
-        ff_kernel,
+        functools.partial(ff_kernel, save),
         (blocks,),
         [
             whole(x.shape), whole(middle.shape), columns(dim, width), columns(dim, width, blocks),
             pl.BlockSpec((width, dim), lambda c: (c, 0)),
         ],
-        [block, block, block, whole((rows, dim))],
-        [struct((rows, hidden), BF16)] * 3 + [struct((rows, dim), BF16)],
+        [block] * kept + [whole((rows, dim))],
+        [struct((rows, hidden), BF16)] * kept + [struct((rows, dim), BF16)],
         [pltpu.VMEM((rows, dim), F32)],
-        6 * rows * dim * hidden,
+        6 * rows * dim * hidden * 1.5,
         6 * dim * hidden,
         (x, middle, w_gu, w_gu, w_down),
     )
@@ -336,17 +366,16 @@
 
 
 def ff_back_kernel(
-    dout_ref, mid_ref, gain_ref, gate_ref, up_ref, wg_ref, wu_ref, wd_ref,
-    dgate_ref, dup_ref, dmid_ref, low_ref, dgain_ref,
+    dout_ref, mid_ref, gain_ref, act_ref, slope_ref, wg_ref, wu_ref, wd_ref,
+    dgu_ref, dmid_ref, low_ref, dgain_ref,
     acc,
 ):
     c = pl.program_id(0)
     dproduct = nt_dot(dout_ref[...], wd_ref[...])
-    act, slope = gelu_both(gate_ref[...].astype(F32))
-    dgate = (dproduct * up_ref[...].astype(F32) * slope).astype(BF16)
-    dup = (dproduct * act).astype(BF16)
-    dgate_ref[...] = dgate
-    dup_ref[...] = dup
+    dgate = (dproduct * slope_ref[...].astype(F32)).astype(BF16)
+    dup = (dproduct * act_ref[...].astype(F32)).astype(BF16)
+    dgu_ref[0] = dgate
+    dgu_ref[1] = dup
     part = nt_dot(dgate, wg_ref[...]) + nt_dot(dup, wu_ref[...])
 
     @pl.when(c == 0)
@@ -366,7 +395,7 @@
         dgain_ref[...] = dgain
 
 
-def feed_forward_back(dout, middle, gain, gate, up, w_gu, w_down):
+def feed_forward_back(dout, middle, gain, act, slope, w_gu, w_down):
     rows, dim = dout.shape
     hidden = w_down.shape[0]
     width = 512
@@ -380,21 +409,21 @@
             full, full, whole(gain.shape), block, block, columns(dim, width), columns(dim, width, blocks),
             pl.BlockSpec((width, dim), lambda c: (c, 0)),
         ],
-        [block, block, full, full, whole((1, dim))],
-        [
-            struct((rows, hidden), BF16), struct((rows, hidden), BF16), struct((rows, dim), F32),
+        [pl.BlockSpec((2, rows, width), lambda c: (0, 0, c)), full, full, whole((1, dim))],
+        [
+            struct((2, rows, hidden), BF16), struct((rows, dim), F32),
             struct((rows, dim), BF16), struct((1, dim), F32),
         ],
         [pltpu.VMEM((rows, dim), F32)],
         6 * rows * dim * hidden * 1.2,
         6 * dim * hidden,
-        (dout, middle, gain, gate, up, w_gu, w_gu, w_down),
+        (dout, middle, gain, act, slope, w_gu, w_gu, w_down),
     )
 
 
 def mix_back_kernel(
     groups, length,
-    low_ref, wo_ref, branch_ref, hidden_ref, keep_ref,
+    low_ref, wo_ref, act_ref, slope_ref, hidden_ref, keep_ref,
     dbranch_ref, local_ref, sege_ref, segf_ref, agg_ref,
     dmixed,
 ):
@@ -409,10 +438,9 @@
             s, p, after = carry[g]
             at = pl.multiple_of(g * length + (steps // chunk - 1 - i) * (chunk * SUB), chunk * SUB)
             here = pl.ds(at, chunk * SUB)
-            act, slope = gelu_both(branch_ref[here, :])
             d = dmixed[here, :]
-            dbranch_ref[here, :] = (d * hidden_ref[here, :] * slope).astype(BF16)
-            dhidden = d * act
+            dbranch_ref[here, :] = (d * hidden_ref[here, :] * slope_ref[here, :]).astype(BF16)
+            dhidden = d * act_ref[here, :]
             keep = keep_ref[here, :]
             states = [None] * chunk
             for r in reversed(range(chunk)):
@@ -440,7 +468,7 @@
         agg_ref[2 * g + 1 : 2 * g + 2, :] = b
 
 
-def mix_back(low, w_out, branch, hidden, keep, groups, length):
+def mix_back(low, w_out, act, slope, hidden, keep, groups, length):
     rows, dim = low.shape
     recur = keep.shape[1]
     width = 256
@@ -448,7 +476,7 @@
     return call(
         functools.partial(mix_back_kernel, groups, length),
         (recur // width,),
-        [whole(low.shape), pl.BlockSpec((width, dim), lambda c: (c, 0)), block, block, block],
+        [whole(low.shape), pl.BlockSpec((width, dim), lambda c: (c, 0)), block, block, block, block],
         [block, block, columns(SUB * groups, width), columns(SUB * groups, width), columns(2 * groups, width)],
         [
             struct((rows, recur), BF16), struct((rows, recur), F32), struct((SUB * groups, recur), F32),
@@ -457,7 +485,7 @@
         [pltpu.VMEM((rows, width), F32)],
         2 * rows * dim * recur * 2,
         dim * recur * 2 + rows * recur * 18,
-        (low, w_out, branch, hidden, keep),
+        (low, w_out, act, slope, hidden, keep),
     )
 
 
@@ -621,9 +649,37 @@
     )
 
 
+def branch_back_kernel(dbranch_ref, w_ref, out_ref):
+    part = nt_dot(dbranch_ref[...], w_ref[...])
+
+    @pl.when(pl.program_id(0) == 0)
+    def _():
+        out_ref[...] = part
+
+    @pl.when(pl.program_id(0) > 0)
+    def _():
+        out_ref[...] += part
+
+
+def branch_back(dbranch, w_in, first, dim):
+    rows, recur = dbranch.shape
+    width = 512
+    return call(
+        branch_back_kernel,
+        (recur // width,),
+        [columns(rows, width), columns(dim, width, first // width)],
+        whole((rows, dim)),
+        struct((rows, dim), F32),
+        [],
+        2 * rows * dim * recur,
+        dim * recur * 2,
+        (dbranch, w_in),
+    )
+
+
 def recur_in_back_kernel(
     groups, length,
-    dbranch_ref, din_ref, back_ref, wb_ref, wi_ref, x_ref, gain_ref, dmid_ref,
+    part_ref, din_ref, back_ref, wi_ref, x_ref, gain_ref, dmid_ref,
     low_ref, dx_ref, dgain_ref,
     acc,
 ):
@@ -640,11 +696,11 @@
             extra.append(jnp.where(sub == SUB - 1, back_ref[g * SUB + i : g * SUB + i + 1, :], 0.0))
         tail = slice(base + length - rim, base + length)
         low_ref[tail, :] = (din_ref[tail, :] + jnp.concatenate(extra, axis=0)).astype(BF16)
-    part = nt_dot(dbranch_ref[...], wb_ref[...]) + nt_dot(low_ref[...], wi_ref[...])
+    part = nt_dot(low_ref[...], wi_ref[...])
 
     @pl.when(c == 0)
     def _():
-        acc[...] = part
+        acc[...] = part_ref[...] + part
 
     @pl.when(c > 0)
     def _():
@@ -657,57 +713,105 @@
         dgain_ref[...] = dgain
 
 
-def recur_in_back(dbranch, din, back, w_in, x, gain, dmid, groups, length):
+def recur_in_back(part, din, back, w_in, first, x, gain, dmid, groups, length):
     rows, dim = x.shape
     recur = din.shape[1]
-    width = 256
-    blocks = recur // width
+    width = 512
     block = columns(rows, width)
     full = whole((rows, dim))
     return call(
         functools.partial(recur_in_back_kernel, groups, length),
-        (blocks,),
-        [
-            block, block, columns(SUB * groups, width), columns(dim, width), columns(dim, width, blocks),
+        (recur // width,),
+        [
+            full, block, columns(SUB * groups, width), columns(dim, width, (first + recur) // width),
             full, whole(gain.shape), full,
         ],
         [block, full, whole((1, dim))],
         [struct((rows, recur), BF16), struct((rows, dim), BF16), struct((1, dim), F32)],
         [pltpu.VMEM((rows, dim), F32)],
-        4 * rows * dim * recur,
-        4 * dim * recur + rows * recur * 8,
-        (dbranch, din, back, w_in, w_in, x, gain, dmid),
-    )
-
-
-def outer_kernel(keep_a, keep_b, send_a, send_b, right_a, right_b, keep_ref, send_ref):
-    a, b = right_a[...], right_b[...]
-    send_ref[...] = (nn_dot(send_a[...], a) + nn_dot(send_b[...], b)).astype(BF16)
-    keep_ref[...] = (nn_dot(keep_a[...], a) + nn_dot(keep_b[...], b)).astype(BF16)
-
-
-def outer_block(total):
-    for width in (768, 512, 384, 256, 128):
-        if total % width == 0:
-            return width
-    return total
-
-
-def outer(left, right, first, total):
-    k, rows = left[0].shape
-    width = outer_block(total)
-    offset = first // width
-    out = columns(k, width)
+        2 * rows * dim * recur * 1.5,
+        2 * dim * recur + rows * recur * 8,
+        (part, din, back, w_in, x, gain, dmid),
+    )
+
+
+def outer_kernel(places, pieces, place_ref, left_a, left_b, right_a, right_b, *refs):
+    outs, (keep, send) = refs[:-2], refs[-2:]
+    n, fs, share = places
+    rows = left_a.shape[1]
+    c = pl.program_id(0)
+    per = pl.num_programs(0) // pieces
+
+    @pl.when(c == 0)
+    def _():
+        core, y = place_ref[0], place_ref[1]
+        for at in range(n):
+            there = slice(at * share, (at + 1) * share)
+            for scratch, side in ((keep, y), (send, 1 - y)):
+                first = pl.multiple_of((at * fs + 2 * side + core) * share, share)
+                scratch[there, 0:rows] = left_a[pl.ds(first, share), :]
+                scratch[there, rows : 2 * rows] = left_b[pl.ds(first, share), :]
+
+    right = jnp.concatenate([right_a[0], right_b[0]], axis=0)
+    to_keep = nn_dot(keep[...], right).astype(BF16)
+    to_send = nn_dot(send[...], right).astype(BF16)
+    for p in range(pieces):
+
+        @pl.when(c // per == p)
+        def _(p=p):
+            outs[2 * p][...] = to_keep
+            outs[2 * p + 1][...] = to_send
+
+
+def outer(lefts, at, k, rights, pieces, chosen, place, n, fs):
+    rows = lefts[0].shape[1]
+    count, _, total = rights[0].shape
+    share = k // (n * fs)
+    piece = count * total // pieces
+    width = next(w for w in (768, 512, 384, 256, 128, piece) if piece % w == 0)
+    across, per = total // width, piece // width
+    skipped, pieces = chosen[0] * per, chosen[1]
+
+    def out_block(p):
+        return pl.BlockSpec((n * share, width), lambda c, place: (0, jnp.clip(c - p * per, 0, per - 1)))
+
+    left = pl.BlockSpec((k, rows), lambda c, place: (at // k, 0))
+    right = pl.BlockSpec((1, rows, width), lambda c, place: ((c + skipped) // across, 0, (c + skipped) % across))
+    outs = pl.pallas_call(
+        functools.partial(outer_kernel, (n, fs, share), pieces),
+        grid_spec=pltpu.PrefetchScalarGridSpec(
+            num_scalar_prefetch=1,
+            grid=(pieces * per,),
+            in_specs=[left, left, right, right],
+            out_specs=[out_block(p) for p in range(pieces) for _ in range(2)],
+            scratch_shapes=[pltpu.VMEM((n * share, 2 * rows), BF16)] * 2,
+        ),
+        out_shape=[struct((n * share, piece), BF16)] * (2 * pieces),
+        compiler_params=pltpu.CompilerParams(dimension_semantics=("arbitrary",), vmem_limit_bytes=VMEM_BYTES),
+        cost_estimate=pl.CostEstimate(
+            flops=8 * n * share * rows * pieces * piece // COST, bytes_accessed=1, transcendentals=0
+        ),
+    )(place, *lefts, *rights)
+    return [(outs[2 * p], outs[2 * p + 1]) for p in range(pieces)]
+
+
+def unfold_kernel(folded_ref, out_ref):
+    height, width = folded_ref.shape[0], out_ref.shape[1]
+    for q in range(out_ref.shape[0] // height):
+        out_ref[q * height : (q + 1) * height, :] = folded_ref[:, q * width : (q + 1) * width]
+
+
+def unfold_first(packed, places, height, rows, width):
     return call(
-        outer_kernel,
-        (total // width,),
-        [whole((k, rows))] * 4 + [columns(rows, width, offset)] * 2,
-        [out, out],
-        [struct((k, total), BF16)] * 2,
+        unfold_kernel,
+        (places,),
+        [pl.BlockSpec((height, rows // height * width), lambda c: (c, 0))],
+        pl.BlockSpec((rows, width), lambda c: (c, 0)),
+        struct((places * rows, width), packed.dtype),
         [],
-        8 * k * rows * total,
-        4 * k * total + 4 * rows * total,
-        (*left, *right),
+        0,
+        places * rows * width * 4,
+        (packed,),
     )
 
 
@@ -752,7 +856,7 @@
         self.ny = self.fs // 2
         self.z, f = lax.axis_index("seq"), lax.axis_index("fsdp")
         self.y, self.core = f // 2, f % 2
-        self.swaps = []
+        self.got = None
 
     def core_swap(self, value):
         return lax.ppermute(value, "fsdp", [(i, i ^ 1) for i in range(self.fs)])
@@ -760,23 +864,14 @@
     def y_send(self, value, pairs):
         return lax.ppermute(value, "fsdp", [(2 * a + c, 2 * b + c) for a, b in pairs for c in range(2)])
 
-    def over_y(self, keep, send):
-        if len(self.swaps) >= 2:
-            send, _ = lax.optimization_barrier((send, self.swaps[-2]))
-        got = self.y_send(send, [(0, 1), (1, 0)])
-        self.swaps.append(got)
-        return add(keep, got).astype(BF16)
+    def over_y(self, keep, send, beside=()):
+        if self.got is not None:
+            send = after(send, self.got)
+        self.got = self.y_send(send, [(0, 1), (1, 0)])
+        return add(after(keep, beside), self.got).astype(BF16)
 
     def over_z(self, shares):
-        def slots(d):
-            return lax.dynamic_index_in_dim(shares, d, 0, keepdims=False)
-
-        if self.n == 1:
-            return shares[0].astype(F32)
-        return line_sum(slots, self.z, self.n, lambda v, pairs: lax.ppermute(v, "seq", pairs))
-
-    def finish(self, keep, send):
-        return self.over_z(self.over_y(keep, send))
+        return lax.psum_scatter(shares, "seq", scatter_dimension=0, tiled=True)[0].astype(F32)
 
 
 def pick(value, index, axis):
@@ -796,7 +891,31 @@
 def tail_rows(v, groups, length):
     d = v.shape[1]
     last = v.reshape(groups, length // SUB, SUB, d)[:, length // SUB - 3 :, SUB - 1]
-    return jnp.pad(last, ((0, 0), (0, SUB - 3), (0, 0))).reshape(groups * SUB, d)
+    last = jnp.pad(last, ((0, 0), (0, SUB - 3), (0, 0))).reshape(groups * SUB, d)
+    return jnp.pad(last, ((0, -groups * SUB % 16), (0, 0)))
+
+
+def fold_rows(v, height):
+    count = -(-v.shape[0] // height)
+    v = jnp.pad(v, ((0, count * height - v.shape[0]), (0, 0)))
+    return jnp.concatenate([v[i * height : (i + 1) * height] for i in range(count)], axis=1)
+
+
+def fold_places(v, height):
+    places, rows, width = v.shape
+    count = -(-rows // height)
+    v = jnp.pad(v, ((0, 0), (0, count * height - rows), (0, 0))).reshape(places, count, height, width)
+    return jnp.swapaxes(v, 1, 2).reshape(places, height, count * width)
+
+
+def unfold_rows(v, rows, width):
+    places, height, total = v.shape
+    v = jnp.swapaxes(v.reshape(places, height, total // width, width), 1, 2)
+    return v.reshape(places, -1, width)[:, :rows]
+
+
+def after(value, *others):
+    return lax.optimization_barrier((value, others))[0]
 
 
 def gather(shard):
@@ -812,39 +931,44 @@
     n, fs = lax.axis_size("seq"), lax.axis_size("fsdp")
     places = n * fs
     micro, seqs, length, dim = ends.shape[1:]
-    groups = micro * seqs
+    parts_of = 1
+    groups = micro * seqs // parts_of
     rows = groups * length
     recur = w_branch.shape[2]
     heads, part, block = gate_a.shape[1:]
     hidden_dim = w_gate.shape[2]
 
-    small = jnp.concatenate(
-        [norm_one[0].reshape(-1), norm_two[0].reshape(-1), conv_weight[0].reshape(-1), conv_bias[0], bias_a[0],
-         bias_i[0], decay[0], gate_a[0].reshape(-1), gate_i[0].reshape(-1)]
-    )
-    count = small.shape[0]
-    padded = -(-count // 2048) * 2048
-    small = gather(jnp.pad(small, (0, padded - count)).reshape(1, -1, LANES)).reshape(places, padded)
-    w_in = gather(jnp.concatenate([w_branch[0], w_input[0]], axis=1))
-    w_out_all = gather(w_out[0])
-    w_gu = gather(jnp.concatenate([w_gate[0], w_up[0]], axis=1))
-    w_down_all = gather(w_down[0])
-
     dshare, rshare = dim // places, recur // places
-    cuts = [dshare, dshare, CONV * rshare, rshare, rshare, rshare, rshare, heads * part * block, heads * part * block]
-    pieces, at = [], 0
-    for size in cuts:
-        pieces.append(small[:, at : at + size])
-        at += size
-    gain_one = pieces[0].reshape(1, dim).astype(F32)
-    gain_two = pieces[1].reshape(1, dim).astype(F32)
-    taps = jnp.swapaxes(pieces[2].reshape(places, CONV, rshare), 0, 1).reshape(CONV, recur).astype(F32)
-    decays = pieces[6].reshape(1, recur).astype(F32)
-    vec = jnp.concatenate(
-        [taps] + [p.reshape(1, recur).astype(F32) for p in pieces[3:6]] + [-8.0 * jax.nn.softplus(decays)], axis=0
-    )
+    vectors = [norm_one, norm_two] + [conv_weight[:, k] for k in range(CONV)] + [conv_bias, bias_a, bias_i, decay]
+    vectors = jnp.concatenate([jnp.pad(v, ((0, 0), (0, LANES - v.shape[1]))) for v in vectors], axis=0)
+    vectors = jnp.pad(vectors, ((0, 2 * SUB - vectors.shape[0]), (0, 0)))
+    small = jnp.concatenate([vectors, gate_a.reshape(-1, block), gate_i.reshape(-1, block)], axis=0)
+    small_rows = small.shape[0]
+    small = fold_rows(small, dshare)
+    first = hidden_dim
+    w_in = gather(
+        jnp.concatenate(
+            [fold_rows(w_down[0], dshare), w_branch[0], w_input[0], w_out[0].reshape(dshare, recur), small], axis=1
+        )
+    )
+    w_gu = gather(jnp.concatenate([after(w_gate[0], small), w_up[0]], axis=1))
+    w_out_all = w_in[:, first + 2 * recur : first + 3 * recur].reshape(recur, dim)
+    small = unfold_rows(w_in[:, first + 3 * recur :].reshape(places, dshare, -1), small_rows, LANES)
+    hshare = hidden_dim // places
+    if dshare % 16 == 0:
+        w_down_all = unfold_first(w_in, places, dshare, hshare, dim)
+    else:
+        w_down_all = unfold_rows(w_in[:, :first].reshape(places, dshare, -1), hshare, dim).reshape(hidden_dim, dim)
+
+    def vector(row, share):
+        return small[:, row, :share].reshape(1, places * share).astype(F32)
+
+    gain_one, gain_two = vector(0, dshare), vector(1, dshare)
+    decays = vector(9, rshare)
+    vec = jnp.concatenate([vector(r, rshare) for r in range(2, 9)] + [-8.0 * jax.nn.softplus(decays)], axis=0)
     gates_a, gates_i = [
-        jnp.swapaxes(p.reshape(places, heads, part, block), 0, 1).reshape(heads, block, block) for p in pieces[7:9]
+        jnp.swapaxes(small[:, r : r + heads * part].reshape(places, heads, part, block), 0, 1).reshape(heads, block, block)
+        for r in (2 * SUB, 2 * SUB + heads * part)
     ]
 
     padded_ids = jnp.pad(segment_ids, ((0, 0), (0, 0), (CONV - 1, 0)), constant_values=-1)
@@ -853,132 +977,191 @@
     masks = jnp.stack(
         [window[:, :, CONV - 1 - k : CONV - 1 - k + length] == current for k in (1, 1, 2, 3)]
     ).astype(F32)
-    masks = jnp.swapaxes(masks.reshape(4, groups, SUB, length // SUB), 2, 3).reshape(4, rows, 1)
-    masks = jnp.broadcast_to(masks, (4, rows, LANES))
-
-    def forward(x, halo):
-        normed, branch, ext, rate, igate, keep, local, segp, agg = recur_in(
-            x, halo, gain_one, w_in, gates_a, gates_i, vec, masks, groups, length
+    masks = jnp.swapaxes(masks.reshape(4, parts_of, groups, SUB, length // SUB), 3, 4).reshape(4, parts_of, rows, 1)
+    masks = jnp.broadcast_to(masks, (4, parts_of, rows, LANES))
+    masks = [masks[:, m] for m in range(parts_of)]
+    micros = range(parts_of)
+
+    def forward(xs, halos, save):
+        got = []
+        for m in micros:
+            got.append(recur_in(xs[m], halos[m], gain_one, w_in, first, gates_a, gates_i, vec, masks[m], groups, length))
+        hin = entering(jnp.concatenate([g[7] for g in got], axis=0), parts_of * groups, False)
+        acts = [branch_in(after(g[0], got[-1][7]), w_in, first, recur) for g in got]
+        outs, saved = [], []
+        for m in micros:
+            normed, ext, rate, igate, keep, local, segp, _ = got[m]
+            act, slope = acts[m]
+            mine = hin[m * groups : (m + 1) * groups]
+            if m:
+                keep = after(keep, outs[-1])
+            hidden, mixed, middle, normed_two = recur_out(
+                xs[m], keep, local, act, segp, mine, w_out_all, gain_two, groups, length
+            )
+            results = feed_forward(normed_two, middle, w_gu, w_down_all, save)
+            outs.append(results[-1])
+            saved.append(
+                (normed, ext, rate, igate, keep, mine, hidden, mixed, middle, normed_two, act, slope) + tuple(results[:-1])
+            )
+        return outs, saved
+
+    def back_ff(m, dout, saved):
+        return feed_forward_back(dout, saved[m][8], gain_two, saved[m][12], saved[m][13], w_gu, w_down_all)
+
+    def back_mix(m, low, saved):
+        return mix_back(low, w_out_all, saved[m][10], saved[m][11], saved[m][6], saved[m][4], groups, length)
+
+    def back_gates(m, mixed_back, gin, saved):
+        normed, ext, rate, igate, keep, hin, hidden = saved[m][:7]
+        _, local, sege, segf, _ = mixed_back
+        din, head, dga, dgi, dvec = gates_back(
+            local, keep, hidden, ext, rate, igate, sege, segf, gin[m * groups : (m + 1) * groups], hin,
+            gates_a, gates_i, vec, masks[m], groups, length,
         )
-        hin = entering(agg, groups, False)
-        hidden, mixed, middle, normed_two = recur_out(
-            x, keep, local, branch, segp, hin, w_out_all, gain_two, groups, length
+        return din, shifted(head, "seq", -1), dga, dgi, dvec
+
+    def back_in(m, part, gates, dmid, xs):
+        return recur_in_back(part, gates[0], gates[1], w_in, first, xs[m], gain_one, dmid, groups, length)
+
+    own = [reorder(v) for v in ends[0].reshape((parts_of, -1) + ends.shape[3:])]
+    tails = [shifted(tail_rows(v, groups, length), "seq", 1) for v in own]
+    outs, _ = forward(own, tails, False)
+    xs, halos = [], []
+    for m in micros:
+        received = shifted(outs[m], "section", 1)
+        received_halo = lax.ppermute(
+            tail_rows(outs[m], groups, length), ("section", "seq"), [(i, n + i + 1) for i in range(n - 1)]
         )
-        gate, up, product, out = feed_forward(normed_two, middle, w_gu, w_down_all)
-        saved = (normed, branch, ext, rate, igate, keep, hin, hidden, mixed, middle, normed_two, gate, up, product)
-        return out, saved
-
-    def backward(dout, x, saved):
-        normed, branch, ext, rate, igate, keep, hin, hidden, mixed, middle, normed_two, gate, up, product = saved
-        dgate, dup, dmid, out_low, dgain_two = feed_forward_back(
-            dout, middle, gain_two, gate, up, w_gu, w_down_all
-        )
-        dbranch, local, sege, segf, agg = mix_back(out_low, w_out_all, branch, hidden, keep, groups, length)
-        gin = entering(agg, groups, True)
-        din, head, dga, dgi, dvec = gates_back(
-            local, keep, hidden, ext, rate, igate, sege, segf, gin, hin, gates_a, gates_i, vec, masks, groups, length
-        )
-        back = shifted(head, "seq", -1)
-        input_low, dx, dgain_one = recur_in_back(dbranch, din, back, w_in, x, gain_one, dmid, groups, length)
-        return dx, dgate, dup, out_low, dbranch, input_low, dgain_one, dgain_two, dga, dgi, dvec
-
-    own = reorder(ends[0])
-    tails = tail_rows(own, groups, length)
-    out, _ = forward(own, shifted(tails, "seq", 1))
-    received = shifted(out, "section", 1)
-    received_halo = lax.ppermute(
-        tail_rows(out, groups, length), ("section", "seq"), [(i, n + i + 1) for i in range(n - 1)]
-    )
-    x = jnp.where(is_first, own, received)
-    halo = jnp.where(is_first, shifted(tails, "seq", 1), received_halo)
-    out, saved = forward(x, halo)
-    dx = backward(own, x, saved)[0]
-    dout = jnp.where(is_first, shifted(dx, "section", -1), own)
-    dx, dgate, dup, out_low, dbranch, input_low, dgain_one, dgain_two, dga, dgi, dvec = backward(dout, x, saved)
-
-    outputs = restore(out, ends.shape)
-    grads = restore(dx, ends.shape)
-
-    normed, mixed, normed_two, product = saved[0], saved[8], saved[10], saved[13]
+        xs.append(jnp.where(is_first, own[m], received))
+        halos.append(jnp.where(is_first, tails[m], received_halo))
+    outs, saved = forward(xs, halos, True)
+
+    ff = [back_ff(m, own[m], saved) for m in micros]
+    mix = [back_mix(m, ff[m][2], saved) for m in micros]
+    gin = entering(jnp.concatenate([v[4] for v in mix], axis=0), parts_of * groups, True)
+    parts = [branch_back(after(v[0], mix[-1][4]), w_in, first, dim) for v in mix]
+    gates = [back_gates(m, mix[m], gin, saved) for m in micros]
+    sent = []
+    for m in micros:
+        dx = back_in(m, after(parts[m], gates[-1][0], *sent[-1:]), gates[m], ff[m][1], xs)[1]
+        sent.append(dx)
+
     scatter = Scatter()
-
-    def left(v):
-        k = v.shape[1]
-        t = v.T.reshape(n, scatter.ny, 2, k // places, rows)
-        mine, other = pick(t, scatter.core, 2), scatter.core_swap(pick(t, 1 - scatter.core, 2))
+    swap = scatter.core_swap
+    place = jnp.stack([scatter.core, scatter.y]).astype(jnp.int32)
+    dx = sent[-1]
+    kinds = {"product": 14, "two": 9, "one": 0, "mixed": 7}
+    starts_at, stacked, total_rows = {}, [], 0
+    for name, index in kinds.items():
+        v = after(saved[0][index], dx)
+        gap = -total_rows % v.shape[1]
+        if gap:
+            stacked.append(jnp.zeros((rows, gap), BF16))
+        starts_at[name] = (total_rows + gap, v.shape[1])
+        total_rows += gap + v.shape[1]
+        stacked.append(v)
+    lefts = jnp.concatenate([v.T for v in stacked], axis=0)
+    lefts = (lefts, swap(lefts))
+    dout = jnp.where(is_first, after(shifted(dx, "section", -1), lefts[0]), own[0])
+    dout, lefts = lax.optimization_barrier((dout, lefts))
+
+    def pair(value):
+        value = value if value.ndim == 3 else value[None]
+        return value, swap(value)
+
+    def products(name, rights, pieces=1, chosen=None):
+        at, k = starts_at[name]
+        chosen = chosen or (0, pieces)
         if scatter.ny == 2:
-            keep = [pick(w, scatter.y, 1).reshape(-1, rows) for w in (mine, other)]
-            send = [pick(w, 1 - scatter.y, 1).reshape(-1, rows) for w in (mine, other)]
-            return tuple(keep + send)
-        return mine, other
-
-    def right(v):
-        return v, scatter.core_swap(v)
-
-    def sum_of(lefts, rights, chunks):
-        total = rights[0].shape[1]
+            return outer(lefts, at, k, rights, pieces, chosen, place, n, fs)
+        left = jnp.concatenate([v[at : at + k] for v in lefts], axis=1)
+        right = jnp.concatenate([jnp.concatenate(list(v), axis=1) for v in rights], axis=0)
+        grad = nn_dot(left, right).astype(BF16)
+        grad = pick(grad.reshape(n, scatter.ny, 2, -1, grad.shape[1]), scatter.core, 2)
+        return [(p,) for p in jnp.split(grad, pieces, axis=3)[chosen[0] : sum(chosen)]]
+
+    def over_y(grads, *beside):
         if scatter.ny == 2:
-            step = total // chunks
-            parts = []
-            for i in range(chunks):
-                keep, send = outer(lefts, rights, i * step, step)
-                parts.append(scatter.finish(keep.reshape(n, -1, step), send.reshape(n, -1, step)))
-            return parts[0] if chunks == 1 else jnp.concatenate(parts, axis=1)
-        mine, other = lefts
-        grad = nn_dot(mine.reshape(-1, rows), rights[0]) + nn_dot(other.reshape(-1, rows), rights[1])
-        grad = grad.astype(BF16).reshape(n, scatter.ny, -1, total)
-        return sum_rest(grad)
-
-    def sum_rest(grad):
-        over_y = line_sum(lambda d: pick(grad, d, 1), scatter.y, scatter.ny, scatter.y_send).astype(BF16)
-        return scatter.over_z(over_y)
-
-    normed_t, mixed_t, normed_two_t, product_t = left(normed), left(mixed), left(normed_two), left(product)
-    sum_down = sum_of(product_t, right(dout), 2)
-    sum_gate = sum_of(normed_two_t, right(dgate), 2)
-    sum_up = sum_of(normed_two_t, right(dup), 2)
-    sum_out = sum_of(mixed_t, right(out_low), 1)
-    sum_branch = sum_of(normed_t, right(dbranch), 1)
-    sum_input = sum_of(normed_t, right(input_low), 1)
-
+            return scatter.over_y(*[g.reshape(n, -1, g.shape[1]) for g in grads], beside)
+        (grad,) = grads
+        return line_sum(lambda d: pick(grad, d, 1), scatter.y, scatter.ny, scatter.y_send).astype(BF16)
+
+    down = products("product", pair(dout), 2)
+    dgu, dmid, out_low, dgain_two = back_ff(0, after(dout, down), saved)
+    down_sums = [over_y(down[0], out_low)]
+    dgu, out_low = after((dgu, out_low), down_sums[0])
+    gu_pair = pair(dgu)
+    mix = back_mix(0, out_low, saved)
+    down_sums.append(over_y(down[1], mix[0]))
+    first_gate = products("two", after(gu_pair, down_sums[1]), 4, (0, 1))
+    gin = entering(after(mix[4], first_gate), groups, True)
+    gate_up = first_gate + products("two", after(gu_pair, first_gate), 4, (1, 3))
+    gate_up_sums = [over_y(gate_up[0], gate_up[1], gin)]
+    gates = back_gates(0, after(mix, gate_up_sums[0]), gin, saved)
+    gate_up_sums.append(over_y(gate_up[1], gates[0]))
+    out_low, dbranch, gates = after((out_low, mix[0], gates), gate_up_sums[1])
+    out_pair, branch_pair = pair(out_low), pair(dbranch)
+    base = branch_back(dbranch, w_in, first, dim)
+    results = back_in(0, base, gates, dmid, xs)
+    gate_up_sums.append(over_y(gate_up[2], results[1], out_pair[1], branch_pair[1]))
+    input_pair = pair(after(results[0], gate_up_sums[2]))
+    out = products("mixed", after(out_pair, gate_up_sums[2]))
+    branch = products("one", after(branch_pair, out))
+    gate_up_sums.append(over_y(gate_up[3], branch))
+    into = products("one", after(input_pair, gate_up_sums[3]))
+    out_sum = over_y(out[0], into)
+    branch_sum = over_y(branch[0])
+
+    outputs = restore(outs[0], ends.shape)
+    input_grads = restore(results[1], ends.shape)
+    dgain_one = results[2]
+    dga, dgi, dvec = gates[2:5]
     ddecay = -8.0 * jax.nn.sigmoid(decays) * dvec[7:8]
-    by_place = [
-        dgain_one.reshape(places, -1), dgain_two.reshape(places, -1),
-        jnp.swapaxes(dvec[:CONV].reshape(CONV, places, rshare), 0, 1).reshape(places, -1),
-        dvec[4].reshape(places, -1), dvec[5].reshape(places, -1), dvec[6].reshape(places, -1),
-        ddecay.reshape(places, -1),
-        jnp.swapaxes(dga.reshape(heads, places, part, block), 0, 1).reshape(places, -1),
-        jnp.swapaxes(dgi.reshape(heads, places, part, block), 0, 1).reshape(places, -1),
+    shares = [dgain_one, dgain_two] + [dvec[k : k + 1] for k in range(7)] + [ddecay]
+    shares = [v.reshape(places, 1, -1) for v in shares]
+    shares = [jnp.pad(v, ((0, 0), (0, 0), (0, LANES - v.shape[2]))) for v in shares]
+    shares = jnp.pad(jnp.concatenate(shares, axis=1), ((0, 0), (0, 2 * SUB - len(shares)), (0, 0)))
+    packed = jnp.concatenate(
+        [shares]
+        + [jnp.swapaxes(v.reshape(heads, places, part, block), 0, 1).reshape(places, -1, block) for v in (dga, dgi)],
+        axis=1,
+    )
+    extra = fold_places(packed, dshare).reshape(n, scatter.ny, 2, dshare, -1)
+    theirs = swap(pick(extra, 1 - scatter.core, 2).astype(BF16))
+    extra = add(pick(extra, scatter.core, 2), theirs).astype(BF16)
+    if scatter.ny == 2:
+        sides = (pick(extra, scatter.y, 1), pick(extra, 1 - scatter.y, 1))
+        into = [
+            jnp.concatenate([g.reshape(n, dshare, -1), v], axis=2).reshape(n * dshare, -1) for g, v in zip(into[0], sides)
+        ]
+    else:
+        into = (jnp.concatenate([into[0][0], extra], axis=3),)
+    input_sum = over_y(into)
+
+    sum_down = jnp.concatenate([scatter.over_z(v) for v in down_sums], axis=1)
+    sum_gate, sum_up = [
+        jnp.concatenate([scatter.over_z(v) for v in gate_up_sums[i : i + 2]], axis=1) for i in (0, 2)
     ]
-    packed = jnp.pad(jnp.concatenate(by_place, axis=1), ((0, 0), (0, padded - count)))
-    packed = packed.reshape(n, scatter.ny, 2, -1, LANES)
-    theirs = scatter.core_swap(pick(packed, 1 - scatter.core, 2).astype(BF16))
-    packed = add(pick(packed, scatter.core, 2), theirs).astype(BF16)
-    if scatter.ny == 2:
-        small_sum = scatter.finish(pick(packed, scatter.y, 1), pick(packed, 1 - scatter.y, 1))
-    else:
-        small_sum = sum_rest(packed)
-    small_sum = small_sum.reshape(-1)
-    sums, at = [], 0
-    for size in cuts:
-        sums.append(small_sum[at : at + size])
-        at += size
+    sum_out, sum_branch, sum_input = [scatter.over_z(v) for v in (out_sum, branch_sum, input_sum)]
+    sum_input, sums = sum_input[:, :recur], sum_input[:, recur:]
+    sums = unfold_rows(sums[None], small_rows, LANES)[0]
+    gate_sums = [sums[r : r + heads * part].reshape(gate_a.shape) for r in (2 * SUB, 2 * SUB + heads * part)]
 
     return (
         outputs,
-        grads,
-        sums[0][None],
+        input_grads,
+        sums[0:1, :dshare],
         sum_branch[None],
         sum_input[None],
-        sums[2].reshape(1, CONV, rshare),
-        sums[3][None],
-        sums[7].reshape(gate_a.shape),
-        sums[8].reshape(gate_a.shape),
-        sums[4][None],
-        sums[5][None],
-        sums[6][None],
+        sums[2 : 2 + CONV, :rshare][None],
+        sums[6:7, :rshare],
+        gate_sums[0],
+        gate_sums[1],
+        sums[7:8, :rshare],
+        sums[8:9, :rshare],
+        sums[9:10, :rshare],
         sum_out[None],
-        sums[1][None],
+        sums[1:2, :dshare],
         sum_gate[None],
         sum_up[None],
         sum_down[None],

time: 1450 us -> 1160 us (0.80)
  waiting for transfers between devices: 658 us -> 500 us
  starting transfers between devices: 212 us -> 61.1 us
  Pallas kernels: 400 us -> 435 us
  local copies, waits for them, and re-layouts: 112 us -> 90.9 us
    all_gather x5 -> x2, waiting for transfers between devices: 387 us -> 207 us  [gather(): return lax.all_gather(shard, ('seq', 'fsdp'), axis=0, tiled=True)]
    ppermute x61 -> x1, starting transfers between devices: 159 us -> 2.97 us  [body(): lax.ppermute(tail_rows(outs[m], groups, length), ('section', 'seq'), [(i,...]
    ppermute x61 -> x1, waiting for transfers between devices: 137 us -> 1.73 us  [body(): lax.ppermute(tail_rows(outs[m], groups, length), ('section', 'seq'), [(i,...]
    ppermute x10 -> x9, waiting for transfers between devices: 70.4 us -> 181 us  [y_send(): lax.ppermute(value, 'fsdp', [(2 * a + c, 2 * b + c) for a, b in pairs for...]
    pallas_call x0 -> x6, Pallas kernels: none -> 72 us  [outer(): pl.pallas_call(functools.partial(outer_kernel, (n, fs, share), pieces), g...]
    pallas_call x23 -> x19, Pallas kernels: 400 us -> 363 us  [call(): pl.pallas_call(kernel, grid=grid, in_specs=in_specs, out_specs=out_specs,...]
    dynamic_slice x10 -> x0, local copies, waits for them, and re-layouts: 27 us -> none  [pick(): return lax.dynamic_index_in_dim(value, index, axis, keepdims=False)]
    reduce_scatter x0 -> x9, waiting for transfers between devices: none -> 24.4 us  [over_z(): lax.psum_scatter(shares, 'seq', scatter_dimension=0, tiled=True)[0]]
  transfers between devices with their start and end apart: 104 -> 45, of which waited for: 51 -> 22; matrix products, arithmetic and copies ran while one was open for 9% -> 7% of each run, Pallas kernels for 14% -> 20%
where the time goes in v1:
time: 1160 us; the launch traced here: 1150 us
  waiting for transfers between devices  500 us (43%)
  Pallas kernels  435 us (38%)
  local copies, waits for them, and re-layouts  90.9 us (8%)
  starting transfers between devices  61.1 us (5%)
  other arithmetic  43 us (4%)
  between operations  15.6 us (1%)
    pallas_call x19, Pallas kernels, call(): pl.pallas_call(kernel, grid=grid, in_specs=in_specs, out_specs=out_specs,...  363 us
    all_gather x2, waiting for transfers between devices, gather(): return lax.all_gather(shard, ('seq', 'fsdp'), axis=0, tiled=True)  207 us
    ppermute x9, waiting for transfers between devices, y_send(): lax.ppermute(value, 'fsdp', [(2 * a + c, 2 * b + c) for a, b in pairs for...  181 us
    ppermute x17, waiting for transfers between devices, shifted(): return lax.ppermute(value, axis, pairs)  78.7 us
    pallas_call x6, Pallas kernels, outer(): pl.pallas_call(functools.partial(outer_kernel, (n, fs, share), pieces), g...  72 us
    ppermute x17, starting transfers between devices, shifted(): return lax.ppermute(value, axis, pairs)  40.8 us
    reduce_scatter x9, waiting for transfers between devices, over_z(): lax.psum_scatter(shares, 'seq', scatter_dimension=0, tiled=True)[0]  24.4 us
  transfers between devices with their start and end apart: 45, of which 22 were waited for; matrix products, arithmetic and copies ran while one was open for 7% of the time, Pallas kernels for 20%

profile of v1, /device:TPU:0, one launch (start us, length us, event | category | flops | bytes accessed | tf_op | source)
XLA Modules:
  0.0 1145.6 jit_solution(847569998633714559)
XLA Ops:
  26.6 161.9 %all-gather.3.cloned.1.call-done.wi_ref.w_ref.folded_ref = bf16[1536,11136]{1,0:T(8,128)(2,1)} async-done(((bf16[96,11136]{1,0:T(8,128)(2,1)}), bf16[1536,11136]{1,0:T(8,128)(2,1)}) %all-gather.3.cloned.1.call-update) | async-done | bytes 34209808 | tf_op jit(solution)/shard_map/all_gather | solution.py:922
  197.3 20.3 %shard_map.296 = (bf16[512,1536]{1,0:T(8,128)(2,1)}, f32[2,280,2048]{2,1,0:T(8,128)}, f32[512,2048]{1,0:T(8,128)}, f32[512,2048]{1,0:T(8,128)}, f32[512,2048]{1,...) custom-call(bf16[512,1536]{1,0:T(8,128)(2,1)} %bitcast.257, bf16[16,1536]{1,0:T(8,128)(2,1)} %copy-done.30, ...), custom_call_target="tpu_custom_call" | custom-call | flops 2013265920 | bytes 6815744 | tf_op jit(solution)/shard_map/pallas_call | solution.py:57
  256.5 16.0 %shard_map.299.wd_ref = bf16[4608,1536]{1,0:T(8,128)(2,1)} custom-call(bf16[1536,11136]{1,0:T(8,128)(2,1)} %all-gather.3.cloned.1.call-done.wi_ref.w_ref.folded_ref), custom_call_target="tpu_custom_call" | custom-call | bytes 7077888 | tf_op jit(solution)/shard_map/pallas_call | solution.py:57
  273.4 17.2 %shard_map.298 = (f32[512,2048]{1,0:T(8,128)}, bf16[512,2048]{1,0:T(8,128)(2,1)}, f32[512,1536]{1,0:T(8,128)}, bf16[512,1536]{1,0:T(8,128)(2,1)}) custom-call(bf16[512,1536]{1,0:T(8,128)(2,1)} %bitcast.258, f32[512,2048]{1,0:T(8,128)} %get-tuple-element.140.keep_ref, f32[512,2048]{1,0:T(8,128)} %get-tuple-element.141.local_ref, ...), custom_call_target="tpu_custom_call" | custom-call | flops 1207959552 | bytes 6291456 | tf_op jit(solution)/shard_map/pallas_call | solution.py:57
  290.6 44.6 %all-gather.5.cloned.1.call-done.wg_ref.wu_ref = bf16[1536,9216]{1,0:T(8,128)(2,1)} async-done(((bf16[96,9216]{1,0:T(8,128)(2,1)}), bf16[1536,9216]{1,0:T(8,128)(2,1)}) %all-gather.5.cloned.1.call-update) | async-done | bytes 28311568 | tf_op jit(solution)/shard_map/all_gather | solution.py:922
  335.1 32.2 %shard_map.300 = bf16[512,1536]{1,0:T(8,128)(2,1)} custom-call(bf16[512,1536]{1,0:T(8,128)(2,1)} %get-tuple-element.147.x_ref, f32[512,1536]{1,0:T(8,128)} %get-tuple-element.148.mid_ref, bf16[1536,9216]{1,0:T(8,128)(2,1)} %all-gather.5.cloned.1.call-done.wg_ref.wu_ref, bf16[1536,9216]{1,0:T(8,128)(2,1)} %all-gather.5.cloned.1.call-done.wg_ref.wu_ref, ...), custom_call_target="tpu_custom_call" | custom-call | flops 8153726976 | bytes 10616832 | tf_op jit(solution)/shard_map/pallas_call | solution.py:57
  377.1 27.9 %collective-permute-done.4 = bf16[512,1536]{1,0:T(8,128)(2,1)S(1)} collective-permute-done((bf16[512,1536]{1,0:T(8,128)(2,1)}, bf16[512,1536]{1,0:T(8,128)(2,1)S(1)}, u32[]{:S(2)}, u32[]{:S(2)}) %collective-permute-start.4) | collective-permute-done | bytes 1572896 | tf_op jit(solution)/shard_map/ppermute | solution.py:821
  406.5 19.3 %shard_map.301 = (bf16[512,1536]{1,0:T(8,128)(2,1)}, f32[2,280,2048]{2,1,0:T(8,128)}, f32[512,2048]{1,0:T(8,128)}, f32[512,2048]{1,0:T(8,128)}, f32[512,2048]{1,...) custom-call(bf16[512,1536]{1,0:T(8,128)(2,1)} %broadcast_select_fusion.1.x_ref, ...), custom_call_target="tpu_custom_call" | custom-call | flops 2013265920 | bytes 6815744 | tf_op jit(solution)/shard_map/pallas_call | solution.py:57
  449.1 16.8 %shard_map.303 = (f32[512,2048]{1,0:T(8,128)}, bf16[512,2048]{1,0:T(8,128)(2,1)}, f32[512,1536]{1,0:T(8,128)}, bf16[512,1536]{1,0:T(8,128)(2,1)}) custom-call(bf16[512,1536]{1,0:T(8,128)(2,1)} %broadcast_select_fusion.1.x_ref, f32[512,2048]{1,0:T(8,128)} %get-tuple-element.149.keep_ref, f32[512,2048]{1,0:T(8,128)} %get-tuple-element.150.local_ref, ...), custom_call_target="tpu_custom_call" | custom-call | flops 1207959552 | bytes 6291456 | tf_op jit(solution)/shard_map/pallas_call | solution.py:57
  465.9 33.9 %shard_map.304 = (bf16[512,4608]{1,0:T(8,128)(2,1)}, bf16[512,4608]{1,0:T(8,128)(2,1)}, bf16[512,4608]{1,0:T(8,128)(2,1)}, bf16[512,1536]{1,0:T(8,128)(2,1)}) custom-call(bf16[512,1536]{1,0:T(8,128)(2,1)} %get-tuple-element.180.x_ref, f32[512,1536]{1,0:T(8,128)} %get-tuple-element.157.mid_ref, bf16[1536,9216]{1,0:T(8,128)(2,1)} %all-gather.5.cloned.1.call-done.wg_ref.wu_ref, ...), custom_call_target="tpu_custom_call" | custom-call | flops 8153726976 | bytes 10616832 | tf_op jit(solution)/shard_map/pallas_call | solution.py:57
  499.9 36.5 %shard_map.305 = (bf16[2,512,4608]{2,1,0:T(8,128)(2,1)}, f32[512,1536]{1,0:T(8,128)}, bf16[512,1536]{1,0:T(8,128)(2,1)}, f32[1,1536]{1,0:T(1,128)}) custom-call(bf16[512,1536]{1,0:T(8,128)(2,1)} %bitcast.259, f32[512,1536]{1,0:T(8,128)} %get-tuple-element.157.mid_ref, f32[1,1536]{1,0:T(1,128)} %reshape.631.gain_ref, ...), custom_call_target="tpu_custom_call" | custom-call | flops 6522981376 | bytes 10616832 | tf_op jit(solution)/shard_map/pallas_call | solution.py:57
  563.7 18.9 %shard_map.308 = (f32[512,2048]{1,0:T(8,128)}, f32[16,2048]{1,0:T(8,128)}, f32[16,128,128]{2,1,0:T(8,128)}, f32[16,128,128]{2,1,0:T(8,128)}, f32[8,2048]{1,0:T(8,128)}) custom-call(f32[512,2048]{1,0:T(8,128)} %get-tuple-element.167.local_ref, f32[512,2048]{1,0:T(8,128)} %get-tuple-element.149.keep_ref, f32[512,2048]{1,0:T(8,128)} %get-tuple-element.163.hidden_ref, ...), custom_call_target="tpu_custom_call" | custom-call | flops 1073741824 | bytes 7340032 | tf_op jit(solution)/shard_map/pallas_call | solution.py:57
  632.5 36.6 %collective-permute-done.13 = bf16[512,1536]{1,0:T(8,128)(2,1)S(1)} collective-permute-done((bf16[512,1536]{1,0:T(8,128)(2,1)S(1)}, bf16[512,1536]{1,0:T(8,128)(2,1)S(1)}, u32[]{:S(2)}, u32[]{:S(2)}) %collective-permute-start.13) | collective-permute-done | bytes 1572896 | tf_op jit(solution)/shard_map/ppermute | solution.py:821
  674.1 16.6 %shard_map.310 = (bf16[1152,768]{1,0:T(8,128)(2,1)}, bf16[1152,768]{1,0:T(8,128)(2,1)}, bf16[1152,768]{1,0:T(8,128)(2,1)}, bf16[1152,768]{1,0:T(8,128)(2,1)}) custom-call(s32[2]{0:T(128)} %pad_add_fusion.place_ref, bf16[10240,512]{1,0:T(8,128)(2,1)} %bitcast_dynamic-update-slice_fusion.1.left_a, bf16[10240,512]{1,0:T(8,128)(2,1)} %collective-permute-done.14.left_b, ...), custom_call_target="tpu_custom_call" | custom-call | flops 1811939328 | bytes 1 | tf_op jit(solution)/shard_map/pallas_call | solution.py:780
  692.5 36.5 %shard_map.311 = (bf16[2,512,4608]{2,1,0:T(8,128)(2,1)}, f32[512,1536]{1,0:T(8,128)}, bf16[512,1536]{1,0:T(8,128)(2,1)}, f32[1,1536]{1,0:T(1,128)}) custom-call(bf16[512,1536]{1,0:T(8,128)(2,1)} %copy-done.2, f32[512,1536]{1,0:T(8,128)} %get-tuple-element.157.mid_ref, f32[1,1536]{1,0:T(1,128)} %reshape.631.gain_ref, ...), custom_call_target="tpu_custom_call" | custom-call | flops 6522981376 | bytes 10616832 | tf_op jit(solution)/shard_map/pallas_call | solution.py:57
  750.2 24.2 %collective-permute-done.18 = bf16[4,288,768]{2,1,0:T(8,128)(2,1)S(1)} collective-permute-done((bf16[4,288,768]{2,1,0:T(8,128)(2,1)S(1)}, bf16[4,288,768]{2,1,0:T(8,128)(2,1)S(1)}, u32[]{:S(2)}, u32[]{:S(2)}) %collective-permute-start.18) | collective-permute-done | bytes 1769504 | tf_op jit(solution)/shard_map/ppermute | solution.py:865
  791.3 19.8 %shard_map.314 = (bf16[384,2304]{1,0:T(8,128)(2,1)}, bf16[384,2304]{1,0:T(8,128)(2,1)}, bf16[384,2304]{1,0:T(8,128)(2,1)}, bf16[384,2304]{1,0:T(8,128)(2,1)}, bf...) custom-call(s32[2]{0:T(128)} %pad_add_fusion.place_ref, bf16[10240,512]{1,0:T(8,128)(2,1)} %bitcast_dynamic-update-slice_fusion.1.left_a, ...), custom_call_target="tpu_custom_call" | custom-call | flops 2717908992 | bytes 1 | tf_op jit(solution)/shard_map/pallas_call | solution.py:780
  833.5 19.1 %shard_map.315 = (f32[512,2048]{1,0:T(8,128)}, f32[16,2048]{1,0:T(8,128)}, f32[16,128,128]{2,1,0:T(8,128)}, f32[16,128,128]{2,1,0:T(8,128)}, f32[8,2048]{1,0:T(8,128)}) custom-call(f32[512,2048]{1,0:T(8,128)} %get-tuple-element.216.local_ref, f32[512,2048]{1,0:T(8,128)} %get-tuple-element.149.keep_ref, f32[512,2048]{1,0:T(8,128)} %get-tuple-element.163.hidden_ref, ...), custom_call_target="tpu_custom_call" | custom-call | flops 1073741824 | bytes 7340032 | tf_op jit(solution)/shard_map/pallas_call | solution.py:57
  852.7 18.8 %collective-permute-done.24 = bf16[4,96,2304]{2,1,0:T(8,128)(2,1)S(1)} collective-permute-done((bf16[4,96,2304]{2,1,0:T(8,128)(2,1)}, bf16[4,96,2304]{2,1,0:T(8,128)(2,1)S(1)}, u32[]{:S(2)}, u32[]{:S(2)}) %collective-permute-start.24) | collective-permute-done | bytes 1769504 | tf_op jit(solution)/shard_map/ppermute | solution.py:865
  945.3 21.0 %collective-permute-done.29 = bf16[4,96,2304]{2,1,0:T(8,128)(2,1)S(1)} collective-permute-done((bf16[4,96,2304]{2,1,0:T(8,128)(2,1)}, bf16[4,96,2304]{2,1,0:T(8,128)(2,1)S(1)}, u32[]{:S(2)}, u32[]{:S(2)}) %collective-permute-start.29) | collective-permute-done | bytes 1769504 | tf_op jit(solution)/shard_map/ppermute | solution.py:865
  982.2 22.9 %collective-permute-done.31 = bf16[4,128,1536]{2,1,0:T(8,128)(2,1)} collective-permute-done((bf16[4,128,1536]{2,1,0:T(8,128)(2,1)}, bf16[4,128,1536]{2,1,0:T(8,128)(2,1)}, u32[]{:S(2)}, u32[]{:S(2)}) %collective-permute-start.31) | collective-permute-done | bytes 1572896 | tf_op jit(solution)/shard_map/ppermute | solution.py:865
  1021.1 24.7 %collective-permute-done.32 = bf16[4,96,2048]{2,1,0:T(8,128)(2,1)} collective-permute-done((bf16[4,96,2048]{2,1,0:T(8,128)(2,1)}, bf16[4,96,2048]{2,1,0:T(8,128)(2,1)}, u32[]{:S(2)}, u32[]{:S(2)}) %collective-permute-start.32) | collective-permute-done | bytes 1572896 | tf_op jit(solution)/shard_map/ppermute | solution.py:865
  1052.5 39.5 %collective-permute-done.33 = bf16[4,96,2432]{2,1,0:T(8,128)(2,1)S(1)} collective-permute-done((bf16[4,96,2432]{2,1,0:T(8,128)(2,1)S(1)}, bf16[4,96,2432]{2,1,0:T(8,128)(2,1)S(1)}, u32[]{:S(2)}, u32[]{:S(2)}) %collective-permute-start.33) | collective-permute-done | bytes 1867808 | tf_op jit(solution)/shard_map/ppermute | solution.py:865
  1109.9 24.3 %reduce-scatter.10.cloned.1.call-done = bf16[1,96,2432]{2,1,0:T(8,128)(2,1)} async-done(((bf16[4,96,2432]{2,1,0:T(8,128)(2,1)}), bf16[1,96,2432]{2,1,0:T(8,128)(2,1)}) %reduce-scatter.10.cloned.1.call-update) | async-done | bytes 466960 | tf_op jit(solution)/shard_map/reduce_scatter | solution.py:874
  (333 shorter events, 380.5 us)
Async XLA Ops:
  7.3 181.2 %all-gather.3.cloned.1.call-start = ((), (), s32[]{:S(2)}) async-start(), calls=%async_computation.9 | async-start | bytes 36347904 | tf_op jit(solution)/shard_map/all_gather | solution.py:922
  14.5 320.6 %all-gather.5.cloned.1.call-start = ((), (), s32[]{:S(2)}) async-start(), calls=%async_computation.10 | async-start | bytes 30081024 | tf_op jit(solution)/shard_map/all_gather | solution.py:922
  17.2 1079.4 %reduce-scatter.24.cloned.1.call-start = ((), (), s32[]{:S(2)}) async-start(), calls=%async_computation.18 | async-start | bytes 2211840 | tf_op jit(solution)/shard_map/reduce_scatter | solution.py:874
  19.0 177.0 %collective-permute-start = (bf16[16,1536]{1,0:T(8,128)(2,1)S(1)}, bf16[16,1536]{1,0:T(8,128)(2,1)S(1)}, u32[]{:S(2)}, u32[]{:S(2)}) collective-permute-start(bf16[16,1536]{1,0:T(8,128)(2,1)S(1)} %pad_bitcast_fusion), channel_id=1, source_target_pairs={{0,4},{4,8},{8,12},{1,5},{5,9},{9,13},{2,6},{6,10},{10,14},{3,7},{... | collective-permute-start | bytes 147464 | tf_op jit(solution)/shard_map/ppermute | solution.py:821
  217.7 54.8 %collective-permute-start.1 = (f32[4,2048]{1,0:T(4,128)}, f32[4,2048]{1,0:T(4,128)S(1)}, u32[]{:S(2)}, u32[]{:S(2)}) collective-permute-start(f32[4,2048]{1,0:T(4,128)} %get-tuple-element.143), channel_id=1, source_target_pairs={{0,4},{4,8},{8,12},{1,5},{5,9},{9,13},{2,6},{6,10},{10,14},{3,7},{... | collective-permute-start | bytes 98312 | tf_op jit(solution)/shard_map/ppermute | solution.py:821
  220.7 51.8 %collective-permute-start.2 = (f32[4,2048]{1,0:T(4,128)}, f32[4,2048]{1,0:T(4,128)S(1)}, u32[]{:S(2)}, u32[]{:S(2)}) collective-permute-start(f32[4,2048]{1,0:T(4,128)} %get-tuple-element.143), channel_id=1, source_target_pairs={{0,8},{4,12},{1,9},{5,13},{2,10},{6,14},{3,11},{7,15},{16,24},{20,... | collective-permute-start | bytes 98312 | tf_op jit(solution)/shard_map/ppermute | solution.py:821
  225.0 47.6 %collective-permute-start.3 = (f32[4,2048]{1,0:T(4,128)}, f32[4,2048]{1,0:T(4,128)S(1)}, u32[]{:S(2)}, u32[]{:S(2)}) collective-permute-start(f32[4,2048]{1,0:T(4,128)} %get-tuple-element.143), channel_id=1, source_target_pairs={{0,12},{1,13},{2,14},{3,15},{16,28},{17,29},{18,30},{19,31}} | collective-permute-start | bytes 98312 | tf_op jit(solution)/shard_map/ppermute | solution.py:821
  630.4 39.0 %collective-permute-start.14 = (bf16[10240,512]{1,0:T(8,128)(2,1)}, bf16[10240,512]{1,0:T(8,128)(2,1)}, u32[]{:S(2)}, u32[]{:S(2)}) collective-permute-start(bf16[10240,512]{1,0:T(8,128)(2,1)} %bitcast_dynamic-update-slice_fusion.1.left_a), channel_id=1, source_target_pairs={{0,1},{1,0},{2,3},{3,2},{4,5},{5,4},{6,7},{7,6},{8,9},{9,8},{10,11... | collective-permute-start | bytes 31457288 | tf_op jit(solution)/shard_map/ppermute | solution.py:862
  690.7 40.9 %collective-permute-start.16 = (bf16[4,288,768]{2,1,0:T(8,128)(2,1)}, bf16[4,288,768]{2,1,0:T(8,128)(2,1)S(1)}, u32[]{:S(2)}, u32[]{:S(2)}) collective-permute-start(bf16[4,288,768]{2,1,0:T(8,128)(2,1)} %bitcast.319), channel_id=1, source_target_pairs={{0,2},{1,3},{2,0},{3,1},{4,6},{5,7},{6,4},{7,5},{8,10},{9,11},{10,... | collective-permute-start | bytes 5308424 | tf_op jit(solution)/shard_map/ppermute | solution.py:865
  733.2 42.9 %collective-permute-start.17 = (bf16[2,512,4608]{2,1,0:T(8,128)(2,1)}, bf16[2,512,4608]{2,1,0:T(8,128)(2,1)}, u32[]{:S(2)}, u32[]{:S(2)}) collective-permute-start(bf16[2,512,4608]{2,1,0:T(8,128)(2,1)} %get-tuple-element.209.right_a), channel_id=1, source_target_pairs={{0,1},{1,0},{2,3},{3,2},{4,5},{5,4},{6,7},{7,6},{8,9},{9,8},{10,11... | collective-permute-start | bytes 28311560 | tf_op jit(solution)/shard_map/ppermute | solution.py:862
  733.2 363.4 %reduce-scatter.26.cloned.1.call-start = ((), (), s32[]{:S(2)}) async-start(), calls=%async_computation.19 | async-start | bytes 2211840 | tf_op jit(solution)/shard_map/reduce_scatter | solution.py:874
  733.3 41.1 %collective-permute-start.18 = (bf16[4,288,768]{2,1,0:T(8,128)(2,1)S(1)}, bf16[4,288,768]{2,1,0:T(8,128)(2,1)S(1)}, u32[]{:S(2)}, u32[]{:S(2)}) collective-permute-start(bf16[4,288,768]{2,1,0:T(8,128)(2,1)S(1)} %bitcast.318), channel_id=1, source_target_pairs={{0,2},{1,3},{2,0},{3,1},{4,6},{5,7},{6,4},{7,5},{8,10},{9,11},{10,... | collective-permute-start | bytes 5308424 | tf_op jit(solution)/shard_map/ppermute | solution.py:865
  776.1 324.9 %reduce-scatter.16.cloned.1.call-start = ((), (), s32[]{:S(2)}) async-start(), calls=%async_computation.14 | async-start | bytes 2211840 | tf_op jit(solution)/shard_map/reduce_scatter | solution.py:874
  789.4 40.6 %collective-permute-start.22 = (bf16[4,96,2304]{2,1,0:T(8,128)(2,1)}, bf16[4,96,2304]{2,1,0:T(8,128)(2,1)S(1)}, u32[]{:S(2)}, u32[]{:S(2)}) collective-permute-start(bf16[4,96,2304]{2,1,0:T(8,128)(2,1)} %bitcast.317), channel_id=1, source_target_pairs={{0,2},{1,3},{2,0},{3,1},{4,6},{5,7},{6,4},{7,5},{8,10},{9,11},{10,... | collective-permute-start | bytes 5308424 | tf_op jit(solution)/shard_map/ppermute | solution.py:865
  831.7 269.3 %reduce-scatter.18.cloned.1.call-start = ((), (), s32[]{:S(2)}) async-start(), calls=%async_computation.15 | async-start | bytes 2211840 | tf_op jit(solution)/shard_map/reduce_scatter | solution.py:874
  831.7 39.7 %collective-permute-start.24 = (bf16[4,96,2304]{2,1,0:T(8,128)(2,1)}, bf16[4,96,2304]{2,1,0:T(8,128)(2,1)S(1)}, u32[]{:S(2)}, u32[]{:S(2)}) collective-permute-start(bf16[4,96,2304]{2,1,0:T(8,128)(2,1)} %bitcast.316), channel_id=1, source_target_pairs={{0,2},{1,3},{2,0},{3,1},{4,6},{5,7},{6,4},{7,5},{8,10},{9,11},{10,... | collective-permute-start | bytes 5308424 | tf_op jit(solution)/shard_map/ppermute | solution.py:865
  873.1 230.4 %reduce-scatter.20.cloned.1.call-start = ((), (), s32[]{:S(2)}) async-start(), calls=%async_computation.16 | async-start | bytes 2211840 | tf_op jit(solution)/shard_map/reduce_scatter | solution.py:874
  881.0 41.3 %collective-permute-start.27 = (bf16[4,96,2304]{2,1,0:T(8,128)(2,1)}, bf16[4,96,2304]{2,1,0:T(8,128)(2,1)}, u32[]{:S(2)}, u32[]{:S(2)}) collective-permute-start(bf16[4,96,2304]{2,1,0:T(8,128)(2,1)} %bitcast.315), channel_id=1, source_target_pairs={{0,2},{1,3},{2,0},{3,1},{4,6},{5,7},{6,4},{7,5},{8,10},{9,11},{10,... | collective-permute-start | bytes 5308424 | tf_op jit(solution)/shard_map/ppermute | solution.py:865
  925.5 178.0 %reduce-scatter.22.cloned.1.call-start = ((), (), s32[]{:S(2)}) async-start(), calls=%async_computation.17 | async-start | bytes 2211840 | tf_op jit(solution)/shard_map/reduce_scatter | solution.py:874
  925.8 40.4 %collective-permute-start.29 = (bf16[4,96,2304]{2,1,0:T(8,128)(2,1)}, bf16[4,96,2304]{2,1,0:T(8,128)(2,1)S(1)}, u32[]{:S(2)}, u32[]{:S(2)}) collective-permute-start(bf16[4,96,2304]{2,1,0:T(8,128)(2,1)} %bitcast.72), channel_id=1, source_target_pairs={{0,2},{1,3},{2,0},{3,1},{4,6},{5,7},{6,4},{7,5},{8,10},{9,11},{10,... | collective-permute-start | bytes 5308424 | tf_op jit(solution)/shard_map/ppermute | solution.py:865
  967.9 138.1 %reduce-scatter.14.cloned.1.call-start = ((), (), s32[]{:S(2)}) async-start(), calls=%async_computation.13 | async-start | bytes 1966080 | tf_op jit(solution)/shard_map/reduce_scatter | solution.py:874
  1008.2 99.8 %reduce-scatter.12.cloned.1.call-start = ((), (), s32[]{:S(2)}) async-start(), calls=%async_computation.12 | async-start | bytes 1966080 | tf_op jit(solution)/shard_map/reduce_scatter | solution.py:874
  1049.0 85.2 %reduce-scatter.10.cloned.1.call-start = ((), (), s32[]{:S(2)}) async-start(), calls=%async_computation.11 | async-start | bytes 2334720 | tf_op jit(solution)/shard_map/reduce_scatter | solution.py:874
  1050.5 41.4 %collective-permute-start.33 = (bf16[4,96,2432]{2,1,0:T(8,128)(2,1)S(1)}, bf16[4,96,2432]{2,1,0:T(8,128)(2,1)S(1)}, u32[]{:S(2)}, u32[]{:S(2)}) collective-permute-start(bf16[4,96,2432]{2,1,0:T(8,128)(2,1)S(1)} %pad_maximum_fusion.1), channel_id=1, source_target_pairs={{0,2},{1,3},{2,0},{3,1},{4,6},{5,7},{6,4},{7,5},{8,10},{9,11},{10,... | collective-permute-start | bytes 5603336 | tf_op jit(solution)/shard_map/ppermute | solution.py:865
  (71 other events, 1079.2 us)
Sparse Core Ops, SparseCore 0:
  14.6 173.8 all-gather.2
  190.7 144.4 all-gather.4
  733.4 38.1 reduce-scatter.23
  776.2 40.0 reduce-scatter.25
  831.8 42.3 reduce-scatter.15
  877.0 38.1 reduce-scatter.17
  925.6 38.8 reduce-scatter.19
  968.0 38.8 reduce-scatter.21
  1009.2 34.8 reduce-scatter.13
  1049.1 35.7 reduce-scatter.11
  1093.8 40.4 reduce-scatter.9

commit v2 on v1

--- a/solution.py
+++ b/solution.py
@@ -165,7 +165,7 @@
 def recur_in(x, halo, gain, w_in, first, gate_a, gate_i, vec, masks, groups, length):
     rows, dim = x.shape
     recur = vec.shape[1]
-    width = 256
+    width = 512
     blocks = recur // width
     block_f32 = columns(rows, width)
     heads = width // LANES
@@ -209,7 +209,7 @@
 
 def branch_in(x, w_in, first, recur):
     rows, dim = x.shape
-    width = 256
+    width = 512
     block = columns(rows, width)
     return call(
         branch_kernel,
@@ -284,7 +284,7 @@
 def recur_out(x, keep, local, act, segp, hin, w_out, gain, groups, length):
     rows, dim = x.shape
     recur = keep.shape[1]
-    width = 256
+    width = 512
     block = columns(rows, width)
     return call(
         functools.partial(recur_out_kernel, groups, length),
@@ -471,7 +471,7 @@
 def mix_back(low, w_out, act, slope, hidden, keep, groups, length):
     rows, dim = low.shape
     recur = keep.shape[1]
-    width = 256
+    width = 512
     block = columns(rows, width)
     return call(
         functools.partial(mix_back_kernel, groups, length),
@@ -621,7 +621,7 @@
 
 def gates_back(local, keep, hidden, ext, rate, igate, sege, segf, gin, hin, gate_a, gate_i, vec, masks, groups, length):
     rows, recur = local.shape
-    width = 256
+    width = 512
     heads = width // LANES
     block = columns(rows, width)
     seg = columns(SUB * groups, width)
@@ -856,7 +856,6 @@
         self.ny = self.fs // 2
         self.z, f = lax.axis_index("seq"), lax.axis_index("fsdp")
         self.y, self.core = f // 2, f % 2
-        self.got = None
 
     def core_swap(self, value):
         return lax.ppermute(value, "fsdp", [(i, i ^ 1) for i in range(self.fs)])
@@ -864,11 +863,8 @@
     def y_send(self, value, pairs):
         return lax.ppermute(value, "fsdp", [(2 * a + c, 2 * b + c) for a, b in pairs for c in range(2)])
 
-    def over_y(self, keep, send, beside=()):
-        if self.got is not None:
-            send = after(send, self.got)
-        self.got = self.y_send(send, [(0, 1), (1, 0)])
-        return add(after(keep, beside), self.got).astype(BF16)
+    def over_y(self, keep, send, since, beside):
+        return add(after(keep, beside), self.y_send(after(send, since), [(0, 1), (1, 0)])).astype(BF16)
 
     def over_z(self, shares):
         return lax.psum_scatter(shares, "seq", scatter_dimension=0, tiled=True)[0].astype(F32)
@@ -1036,84 +1032,77 @@
         halos.append(jnp.where(is_first, tails[m], received_halo))
     outs, saved = forward(xs, halos, True)
 
-    ff = [back_ff(m, own[m], saved) for m in micros]
-    mix = [back_mix(m, ff[m][2], saved) for m in micros]
-    gin = entering(jnp.concatenate([v[4] for v in mix], axis=0), parts_of * groups, True)
-    parts = [branch_back(after(v[0], mix[-1][4]), w_in, first, dim) for v in mix]
-    gates = [back_gates(m, mix[m], gin, saved) for m in micros]
-    sent = []
-    for m in micros:
-        dx = back_in(m, after(parts[m], gates[-1][0], *sent[-1:]), gates[m], ff[m][1], xs)[1]
-        sent.append(dx)
-
     scatter = Scatter()
     swap = scatter.core_swap
     place = jnp.stack([scatter.core, scatter.y]).astype(jnp.int32)
-    dx = sent[-1]
-    kinds = {"product": 14, "two": 9, "one": 0, "mixed": 7}
-    starts_at, stacked, total_rows = {}, [], 0
-    for name, index in kinds.items():
-        v = after(saved[0][index], dx)
+
+    ff = back_ff(0, own[0], saved)
+    mix = back_mix(0, ff[2], saved)
+    gin = entering(mix[4], groups, True)
+    product_t = after(saved[0][14], mix[4]).T
+    product_pair = (product_t, swap(product_t))
+    gates = back_gates(0, after(mix, product_t), gin, saved)
+    base = branch_back(after(mix[0], gates[0]), w_in, first, dim)
+    dx = back_in(0, base, gates, ff[1], xs)[1]
+    others = [after(saved[0][i], dx) for i in (9, 0, 7)]
+    starts_at, total_rows = [], 0
+    for i, v in enumerate(others):
         gap = -total_rows % v.shape[1]
         if gap:
-            stacked.append(jnp.zeros((rows, gap), BF16))
-        starts_at[name] = (total_rows + gap, v.shape[1])
+            others[i] = jnp.concatenate([jnp.zeros((rows, gap), BF16), v], axis=1)
+        starts_at.append((total_rows + gap, v.shape[1]))
         total_rows += gap + v.shape[1]
-        stacked.append(v)
-    lefts = jnp.concatenate([v.T for v in stacked], axis=0)
-    lefts = (lefts, swap(lefts))
-    dout = jnp.where(is_first, after(shifted(dx, "section", -1), lefts[0]), own[0])
-    dout, lefts = lax.optimization_barrier((dout, lefts))
+    others = jnp.concatenate([v.T for v in others], axis=0)
+    received = after(shifted(dx, "section", -1), others, product_pair)
+    others = after(others, received)
+    others = (others, swap(others))
+    lefts = {"product": (product_pair, 0, hidden_dim)}
+    for name, (at, k) in zip(("two", "one", "mixed"), starts_at):
+        lefts[name] = (others, at, k)
+    dout = jnp.where(is_first, received, own[0])
 
     def pair(value):
         value = value if value.ndim == 3 else value[None]
         return value, swap(value)
 
     def products(name, rights, pieces=1, chosen=None):
-        at, k = starts_at[name]
+        both, at, k = lefts[name]
         chosen = chosen or (0, pieces)
         if scatter.ny == 2:
-            return outer(lefts, at, k, rights, pieces, chosen, place, n, fs)
-        left = jnp.concatenate([v[at : at + k] for v in lefts], axis=1)
+            return outer(both, at, k, rights, pieces, chosen, place, n, fs)
+        left = jnp.concatenate([v[at : at + k] for v in both], axis=1)
         right = jnp.concatenate([jnp.concatenate(list(v), axis=1) for v in rights], axis=0)
         grad = nn_dot(left, right).astype(BF16)
         grad = pick(grad.reshape(n, scatter.ny, 2, -1, grad.shape[1]), scatter.core, 2)
         return [(p,) for p in jnp.split(grad, pieces, axis=3)[chosen[0] : sum(chosen)]]
 
-    def over_y(grads, *beside):
+    def over_y(grads, since, *beside):
         if scatter.ny == 2:
-            return scatter.over_y(*[g.reshape(n, -1, g.shape[1]) for g in grads], beside)
+            return scatter.over_y(*[g.reshape(n, -1, g.shape[1]) for g in grads], since, beside)
         (grad,) = grads
         return line_sum(lambda d: pick(grad, d, 1), scatter.y, scatter.ny, scatter.y_send).astype(BF16)
 
     down = products("product", pair(dout), 2)
     dgu, dmid, out_low, dgain_two = back_ff(0, after(dout, down), saved)
-    down_sums = [over_y(down[0], out_low)]
-    dgu, out_low = after((dgu, out_low), down_sums[0])
-    gu_pair = pair(dgu)
-    mix = back_mix(0, out_low, saved)
-    down_sums.append(over_y(down[1], mix[0]))
-    first_gate = products("two", after(gu_pair, down_sums[1]), 4, (0, 1))
-    gin = entering(after(mix[4], first_gate), groups, True)
-    gate_up = first_gate + products("two", after(gu_pair, first_gate), 4, (1, 3))
-    gate_up_sums = [over_y(gate_up[0], gate_up[1], gin)]
+    down_sums = [over_y(down[0], (), out_low)]
+    down_sums.append(None)
+    gu_pair = pair(after(dgu, down_sums[0]))
+    mix = back_mix(0, after(out_low, down_sums[0]), saved)
+    gate_up = products("two", after(gu_pair, mix[0]), 4, (0, 1))
+    down_sums[1] = over_y(down[1], out_low, gate_up[0])
+    gin = entering(after(mix[4], down_sums[1]), groups, True)
+    gate_up += products("two", after(gu_pair, down_sums[1]), 4, (1, 3))
+    gate_up_sums = [over_y(gate_up[0], (), gate_up[1], gin)]
     gates = back_gates(0, after(mix, gate_up_sums[0]), gin, saved)
-    gate_up_sums.append(over_y(gate_up[1], gates[0]))
+    gate_up_sums.append(over_y(gate_up[1], gin, gates[0]))
     out_low, dbranch, gates = after((out_low, mix[0], gates), gate_up_sums[1])
     out_pair, branch_pair = pair(out_low), pair(dbranch)
     base = branch_back(dbranch, w_in, first, dim)
     results = back_in(0, base, gates, dmid, xs)
-    gate_up_sums.append(over_y(gate_up[2], results[1], out_pair[1], branch_pair[1]))
+    gate_up_sums.append(over_y(gate_up[2], gates[0], results[1], out_pair[1], branch_pair[1]))
     input_pair = pair(after(results[0], gate_up_sums[2]))
     out = products("mixed", after(out_pair, gate_up_sums[2]))
     branch = products("one", after(branch_pair, out))
-    gate_up_sums.append(over_y(gate_up[3], branch))
-    into = products("one", after(input_pair, gate_up_sums[3]))
-    out_sum = over_y(out[0], into)
-    branch_sum = over_y(branch[0])
-
-    outputs = restore(outs[0], ends.shape)
-    input_grads = restore(results[1], ends.shape)
     dgain_one = results[2]
     dga, dgi, dvec = gates[2:5]
     ddecay = -8.0 * jax.nn.sigmoid(decays) * dvec[7:8]
@@ -1129,20 +1118,27 @@
     extra = fold_places(packed, dshare).reshape(n, scatter.ny, 2, dshare, -1)
     theirs = swap(pick(extra, 1 - scatter.core, 2).astype(BF16))
     extra = add(pick(extra, scatter.core, 2), theirs).astype(BF16)
+    gate_up_sums.append(over_y(gate_up[3], results[1], branch, extra))
+    into = products("one", after(input_pair, gate_up_sums[3]))
+    out_sum = over_y(out[0], branch, into)
     if scatter.ny == 2:
         sides = (pick(extra, scatter.y, 1), pick(extra, 1 - scatter.y, 1))
-        into = [
+        last = [
             jnp.concatenate([g.reshape(n, dshare, -1), v], axis=2).reshape(n * dshare, -1) for g, v in zip(into[0], sides)
         ]
     else:
-        into = (jnp.concatenate([into[0][0], extra], axis=3),)
-    input_sum = over_y(into)
-
-    sum_down = jnp.concatenate([scatter.over_z(v) for v in down_sums], axis=1)
-    sum_gate, sum_up = [
-        jnp.concatenate([scatter.over_z(v) for v in gate_up_sums[i : i + 2]], axis=1) for i in (0, 2)
-    ]
-    sum_out, sum_branch, sum_input = [scatter.over_z(v) for v in (out_sum, branch_sum, input_sum)]
+        last = (jnp.concatenate([into[0][0], extra], axis=3),)
+    branch_sum = over_y(branch[0], last)
+    input_sum = over_y(last, out_sum)
+
+    outputs = restore(outs[0], ends.shape)
+    input_grads = restore(results[1], ends.shape)
+    shares = down_sums + gate_up_sums + [out_sum, branch_sum, input_sum]
+    for i in range(1, len(shares)):
+        shares[i] = after(shares[i], shares[i - 1])
+    totals = [scatter.over_z(v) for v in shares]
+    sum_down, sum_gate, sum_up = [jnp.concatenate(totals[i : i + 2], axis=1) for i in (0, 2, 4)]
+    sum_out, sum_branch, sum_input = totals[6:]
     sum_input, sums = sum_input[:, :recur], sum_input[:, recur:]
     sums = unfold_rows(sums[None], small_rows, LANES)[0]
     gate_sums = [sums[r : r + heads * part].reshape(gate_a.shape) for r in (2 * SUB, 2 * SUB + heads * part)]

time: 1160 us -> 1120 us (0.966)
  waiting for transfers between devices: 500 us -> 479 us
  Pallas kernels: 435 us -> 419 us
    ppermute x9, waiting for transfers between devices: 181 us -> 164 us  [y_send(): lax.ppermute(value, 'fsdp', [(2 * a + c, 2 * b + c) for a, b in pairs for...]
    pallas_call x19, Pallas kernels: 363 us -> 347 us  [call(): pl.pallas_call(kernel, grid=grid, in_specs=in_specs, out_specs=out_specs,...]
    ppermute x17, waiting for transfers between devices: 78.7 us -> 62.1 us  [shifted(): return lax.ppermute(value, axis, pairs)]
  transfers between devices with their start and end apart: 45 -> 46, of which waited for: 22 -> 22; matrix products, arithmetic and copies ran while one was open for 7% -> 9% of each run, Pallas kernels for 20% -> 23%
where the time goes in v2:
time: 1120 us; the launch traced here: 1110 us
  waiting for transfers between devices  479 us (43%)
  Pallas kernels  419 us (37%)
  local copies, waits for them, and re-layouts  85.2 us (8%)
  starting transfers between devices  62.2 us (6%)
  other arithmetic  50.3 us (4%)
  between operations  15.2 us (1%)
    pallas_call x19, Pallas kernels, call(): pl.pallas_call(kernel, grid=grid, in_specs=in_specs, out_specs=out_specs,...  347 us
    all_gather x2, waiting for transfers between devices, gather(): return lax.all_gather(shard, ('seq', 'fsdp'), axis=0, tiled=True)  211 us
    ppermute x9, waiting for transfers between devices, y_send(): lax.ppermute(value, 'fsdp', [(2 * a + c, 2 * b + c) for a, b in pairs for...  164 us
    pallas_call x6, Pallas kernels, outer(): pl.pallas_call(functools.partial(outer_kernel, (n, fs, share), pieces), g...  72.1 us
    ppermute x17, waiting for transfers between devices, shifted(): return lax.ppermute(value, axis, pairs)  62.1 us
    ppermute x17, starting transfers between devices, shifted(): return lax.ppermute(value, axis, pairs)  41.3 us
    reduce_scatter x9, waiting for transfers between devices, over_z(): lax.psum_scatter(shares, 'seq', scatter_dimension=0, tiled=True)[0]  24.2 us
  transfers between devices with their start and end apart: 46, of which 22 were waited for; matrix products, arithmetic and copies ran while one was open for 9% of the time, Pallas kernels for 23%

profile of v2, /device:TPU:0, one launch (start us, length us, event | category | flops | bytes accessed | tf_op | source)
XLA Modules:
  0.0 1110.5 jit_solution(10462480292172173326)
XLA Ops:
  28.8 161.9 %all-gather.3.cloned.1.call-done.wi_ref.w_ref.folded_ref = bf16[1536,11136]{1,0:T(8,128)(2,1)} async-done(((bf16[96,11136]{1,0:T(8,128)(2,1)}), bf16[1536,11136]{1,0:T(8,128)(2,1)}) %all-gather.3.cloned.1.call-update) | async-done | bytes 34209808 | tf_op jit(solution)/shard_map/all_gather | solution.py:918
  199.7 18.4 %shard_map.296 = (bf16[512,1536]{1,0:T(8,128)(2,1)}, f32[2,280,2048]{2,1,0:T(8,128)}, f32[512,2048]{1,0:T(8,128)}, f32[512,2048]{1,0:T(8,128)}, f32[512,2048]{1,...) custom-call(bf16[512,1536]{1,0:T(8,128)(2,1)} %bitcast.254, bf16[16,1536]{1,0:T(8,128)(2,1)} %copy-done.30, ...), custom_call_target="tpu_custom_call" | custom-call | flops 2013265920 | bytes 6815744 | tf_op jit(solution)/shard_map/pallas_call | solution.py:57
  255.8 16.2 %shard_map.299.wd_ref = bf16[4608,1536]{1,0:T(8,128)(2,1)} custom-call(bf16[1536,11136]{1,0:T(8,128)(2,1)} %all-gather.3.cloned.1.call-done.wi_ref.w_ref.folded_ref), custom_call_target="tpu_custom_call" | custom-call | bytes 7077888 | tf_op jit(solution)/shard_map/pallas_call | solution.py:57
  272.9 15.1 %shard_map.298 = (f32[512,2048]{1,0:T(8,128)}, bf16[512,2048]{1,0:T(8,128)(2,1)}, f32[512,1536]{1,0:T(8,128)}, bf16[512,1536]{1,0:T(8,128)(2,1)}) custom-call(bf16[512,1536]{1,0:T(8,128)(2,1)} %bitcast.255, f32[512,2048]{1,0:T(8,128)} %get-tuple-element.146.keep_ref, f32[512,2048]{1,0:T(8,128)} %get-tuple-element.147.local_ref, ...), custom_call_target="tpu_custom_call" | custom-call | flops 1207959552 | bytes 6291456 | tf_op jit(solution)/shard_map/pallas_call | solution.py:57
  287.9 49.5 %all-gather.5.cloned.1.call-done.wg_ref.wu_ref = bf16[1536,9216]{1,0:T(8,128)(2,1)} async-done(((bf16[96,9216]{1,0:T(8,128)(2,1)}), bf16[1536,9216]{1,0:T(8,128)(2,1)}) %all-gather.5.cloned.1.call-update) | async-done | bytes 28311568 | tf_op jit(solution)/shard_map/all_gather | solution.py:918
  337.4 32.2 %shard_map.300 = bf16[512,1536]{1,0:T(8,128)(2,1)} custom-call(bf16[512,1536]{1,0:T(8,128)(2,1)} %get-tuple-element.153.x_ref, f32[512,1536]{1,0:T(8,128)} %get-tuple-element.154.mid_ref, bf16[1536,9216]{1,0:T(8,128)(2,1)} %all-gather.5.cloned.1.call-done.wg_ref.wu_ref, bf16[1536,9216]{1,0:T(8,128)(2,1)} %all-gather.5.cloned.1.call-done.wg_ref.wu_ref, ...), custom_call_target="tpu_custom_call" | custom-call | flops 8153726976 | bytes 10616832 | tf_op jit(solution)/shard_map/pallas_call | solution.py:57
  379.4 27.9 %collective-permute-done.4 = bf16[512,1536]{1,0:T(8,128)(2,1)S(1)} collective-permute-done((bf16[512,1536]{1,0:T(8,128)(2,1)}, bf16[512,1536]{1,0:T(8,128)(2,1)S(1)}, u32[]{:S(2)}, u32[]{:S(2)}) %collective-permute-start.4) | collective-permute-done | bytes 1572896 | tf_op jit(solution)/shard_map/ppermute | solution.py:821
  408.7 17.3 %shard_map.301 = (bf16[512,1536]{1,0:T(8,128)(2,1)}, f32[2,280,2048]{2,1,0:T(8,128)}, f32[512,2048]{1,0:T(8,128)}, f32[512,2048]{1,0:T(8,128)}, f32[512,2048]{1,...) custom-call(bf16[512,1536]{1,0:T(8,128)(2,1)} %broadcast_select_fusion.1.x_ref, ...), custom_call_target="tpu_custom_call" | custom-call | flops 2013265920 | bytes 6815744 | tf_op jit(solution)/shard_map/pallas_call | solution.py:57
  448.4 14.7 %shard_map.303 = (f32[512,2048]{1,0:T(8,128)}, bf16[512,2048]{1,0:T(8,128)(2,1)}, f32[512,1536]{1,0:T(8,128)}, bf16[512,1536]{1,0:T(8,128)(2,1)}) custom-call(bf16[512,1536]{1,0:T(8,128)(2,1)} %broadcast_select_fusion.1.x_ref, f32[512,2048]{1,0:T(8,128)} %get-tuple-element.155.keep_ref, f32[512,2048]{1,0:T(8,128)} %get-tuple-element.156.local_ref, ...), custom_call_target="tpu_custom_call" | custom-call | flops 1207959552 | bytes 6291456 | tf_op jit(solution)/shard_map/pallas_call | solution.py:57
  463.1 33.9 %shard_map.304 = (bf16[512,4608]{1,0:T(8,128)(2,1)}, bf16[512,4608]{1,0:T(8,128)(2,1)}, bf16[512,4608]{1,0:T(8,128)(2,1)}, bf16[512,1536]{1,0:T(8,128)(2,1)}) custom-call(bf16[512,1536]{1,0:T(8,128)(2,1)} %get-tuple-element.188.x_ref, f32[512,1536]{1,0:T(8,128)} %get-tuple-element.163.mid_ref, bf16[1536,9216]{1,0:T(8,128)(2,1)} %all-gather.5.cloned.1.call-done.wg_ref.wu_ref, ...), custom_call_target="tpu_custom_call" | custom-call | flops 8153726976 | bytes 10616832 | tf_op jit(solution)/shard_map/pallas_call | solution.py:57
  497.0 36.4 %shard_map.305 = (bf16[2,512,4608]{2,1,0:T(8,128)(2,1)}, f32[512,1536]{1,0:T(8,128)}, bf16[512,1536]{1,0:T(8,128)(2,1)}, f32[1,1536]{1,0:T(1,128)}) custom-call(bf16[512,1536]{1,0:T(8,128)(2,1)} %bitcast.256, f32[512,1536]{1,0:T(8,128)} %get-tuple-element.163.mid_ref, f32[1,1536]{1,0:T(1,128)} %reshape.633.gain_ref, ...), custom_call_target="tpu_custom_call" | custom-call | flops 6522981376 | bytes 10616832 | tf_op jit(solution)/shard_map/pallas_call | solution.py:57
  533.4 13.4 %shard_map.306 = (bf16[512,2048]{1,0:T(8,128)(2,1)}, f32[512,2048]{1,0:T(8,128)}, f32[16,2048]{1,0:T(8,128)}, f32[16,2048]{1,0:T(8,128)}, f32[4,2048]{1,0:T(4,128)}) custom-call(bf16[512,1536]{1,0:T(8,128)(2,1)} %get-tuple-element.167.low_ref, bf16[2048,1536]{1,0:T(8,128)(2,1)} %reshape.570.wo_ref, f32[512,2048]{1,0:T(8,128)} %get-tuple-element.160.act_ref, ...), custom_call_target="tpu_custom_call" | custom-call | flops 1610612736 | bytes 6291456 | tf_op jit(solution)/shard_map/pallas_call | solution.py:57
  563.3 17.6 %shard_map.307 = (f32[512,2048]{1,0:T(8,128)}, f32[16,2048]{1,0:T(8,128)}, f32[16,128,128]{2,1,0:T(8,128)}, f32[16,128,128]{2,1,0:T(8,128)}, f32[8,2048]{1,0:T(8,128)}) custom-call(f32[512,2048]{1,0:T(8,128)} %get-tuple-element.177.local_ref, f32[512,2048]{1,0:T(8,128)} %get-tuple-element.155.keep_ref, f32[512,2048]{1,0:T(8,128)} %get-tuple-element.169.hidden_ref, ...), custom_call_target="tpu_custom_call" | custom-call | flops 1073741824 | bytes 7340032 | tf_op jit(solution)/shard_map/pallas_call | solution.py:57
  620.1 23.2 %collective-permute-done.13 = bf16[512,1536]{1,0:T(8,128)(2,1)} collective-permute-done((bf16[512,1536]{1,0:T(8,128)(2,1)}, bf16[512,1536]{1,0:T(8,128)(2,1)}, u32[]{:S(2)}, u32[]{:S(2)}) %collective-permute-start.13) | collective-permute-done | bytes 1572896 | tf_op jit(solution)/shard_map/ppermute | solution.py:821
  649.5 16.7 %shard_map.310 = (bf16[1152,768]{1,0:T(8,128)(2,1)}, bf16[1152,768]{1,0:T(8,128)(2,1)}, bf16[1152,768]{1,0:T(8,128)(2,1)}, bf16[1152,768]{1,0:T(8,128)(2,1)}) custom-call(s32[2]{0:T(128)} %pad_add_fusion.place_ref, bf16[4608,512]{1,0:T(8,128)(2,1)} %bitcast.258, bf16[4608,512]{1,0:T(8,128)(2,1)} %collective-permute-done.14.left_b, ...), custom_call_target="tpu_custom_call" | custom-call | flops 1811939328 | bytes 1 | tf_op jit(solution)/shard_map/pallas_call | solution.py:780
  668.0 36.4 %shard_map.311 = (bf16[2,512,4608]{2,1,0:T(8,128)(2,1)}, f32[512,1536]{1,0:T(8,128)}, bf16[512,1536]{1,0:T(8,128)(2,1)}, f32[1,1536]{1,0:T(1,128)}) custom-call(bf16[512,1536]{1,0:T(8,128)(2,1)} %copy-done.2, f32[512,1536]{1,0:T(8,128)} %get-tuple-element.163.mid_ref, f32[1,1536]{1,0:T(1,128)} %reshape.633.gain_ref, ...), custom_call_target="tpu_custom_call" | custom-call | flops 6522981376 | bytes 10616832 | tf_op jit(solution)/shard_map/pallas_call | solution.py:57
  757.5 19.9 %shard_map.314 = (bf16[384,2304]{1,0:T(8,128)(2,1)}, bf16[384,2304]{1,0:T(8,128)(2,1)}, bf16[384,2304]{1,0:T(8,128)(2,1)}, bf16[384,2304]{1,0:T(8,128)(2,1)}, bf...) custom-call(s32[2]{0:T(128)} %pad_add_fusion.place_ref, bf16[6144,512]{1,0:T(8,128)(2,1)} %pad_maximum_fusion.left_a, ...), custom_call_target="tpu_custom_call" | custom-call | flops 2717908992 | bytes 1 | tf_op jit(solution)/shard_map/pallas_call | solution.py:780
  799.2 17.7 %shard_map.315 = (f32[512,2048]{1,0:T(8,128)}, f32[16,2048]{1,0:T(8,128)}, f32[16,128,128]{2,1,0:T(8,128)}, f32[16,128,128]{2,1,0:T(8,128)}, f32[8,2048]{1,0:T(8,128)}) custom-call(f32[512,2048]{1,0:T(8,128)} %get-tuple-element.221.local_ref, f32[512,2048]{1,0:T(8,128)} %get-tuple-element.155.keep_ref, f32[512,2048]{1,0:T(8,128)} %get-tuple-element.169.hidden_ref, ...), custom_call_target="tpu_custom_call" | custom-call | flops 1073741824 | bytes 7340032 | tf_op jit(solution)/shard_map/pallas_call | solution.py:57
  816.9 19.5 %collective-permute-done.25 = bf16[4,96,2304]{2,1,0:T(8,128)(2,1)S(1)} collective-permute-done((bf16[4,96,2304]{2,1,0:T(8,128)(2,1)}, bf16[4,96,2304]{2,1,0:T(8,128)(2,1)S(1)}, u32[]{:S(2)}, u32[]{:S(2)}) %collective-permute-start.25) | collective-permute-done | bytes 1769504 | tf_op jit(solution)/shard_map/ppermute | solution.py:864
  871.3 15.9 %collective-permute-done.28 = bf16[4,96,2304]{2,1,0:T(8,128)(2,1)} collective-permute-done((bf16[4,96,2304]{2,1,0:T(8,128)(2,1)}, bf16[4,96,2304]{2,1,0:T(8,128)(2,1)}, u32[]{:S(2)}, u32[]{:S(2)}) %collective-permute-start.28) | collective-permute-done | bytes 1769504 | tf_op jit(solution)/shard_map/ppermute | solution.py:864
  948.9 22.9 %collective-permute-done.32 = bf16[4,128,1536]{2,1,0:T(8,128)(2,1)} collective-permute-done((bf16[4,128,1536]{2,1,0:T(8,128)(2,1)}, bf16[4,128,1536]{2,1,0:T(8,128)(2,1)}, u32[]{:S(2)}, u32[]{:S(2)}) %collective-permute-start.32) | collective-permute-done | bytes 1572896 | tf_op jit(solution)/shard_map/ppermute | solution.py:864
  976.7 34.5 %collective-permute-done.34 = bf16[4,96,2048]{2,1,0:T(8,128)(2,1)} collective-permute-done((bf16[4,96,2048]{2,1,0:T(8,128)(2,1)}, bf16[4,96,2048]{2,1,0:T(8,128)(2,1)}, u32[]{:S(2)}, u32[]{:S(2)}) %collective-permute-start.34) | collective-permute-done | bytes 1572896 | tf_op jit(solution)/shard_map/ppermute | solution.py:864
  1017.9 39.5 %collective-permute-done.33 = bf16[4,96,2432]{2,1,0:T(8,128)(2,1)S(1)} collective-permute-done((bf16[4,96,2432]{2,1,0:T(8,128)(2,1)S(1)}, bf16[4,96,2432]{2,1,0:T(8,128)(2,1)S(1)}, u32[]{:S(2)}, u32[]{:S(2)}) %collective-permute-start.33) | collective-permute-done | bytes 1867808 | tf_op jit(solution)/shard_map/ppermute | solution.py:864
  1075.2 24.2 %reduce-scatter.10.cloned.1.call-done = bf16[1,96,2432]{2,1,0:T(8,128)(2,1)} async-done(((bf16[4,96,2432]{2,1,0:T(8,128)(2,1)}), bf16[1,96,2432]{2,1,0:T(8,128)(2,1)}) %reduce-scatter.10.cloned.1.call-update) | async-done | bytes 466960 | tf_op jit(solution)/shard_map/reduce_scatter | solution.py:870
  (318 shorter events, 370.5 us)
Async XLA Ops:
  7.2 183.6 %all-gather.3.cloned.1.call-start = ((), (), s32[]{:S(2)}) async-start(), calls=%async_computation.9 | async-start | bytes 36347904 | tf_op jit(solution)/shard_map/all_gather | solution.py:918
  16.8 320.6 %all-gather.5.cloned.1.call-start = ((), (), s32[]{:S(2)}) async-start(), calls=%async_computation.10 | async-start | bytes 30081024 | tf_op jit(solution)/shard_map/all_gather | solution.py:918
  19.5 1044.2 %reduce-scatter.24.cloned.1.call-start = ((), (), s32[]{:S(2)}) async-start(), calls=%async_computation.18 | async-start | bytes 2211840 | tf_op jit(solution)/shard_map/reduce_scatter | solution.py:870
  21.3 177.1 %collective-permute-start = (bf16[16,1536]{1,0:T(8,128)(2,1)S(1)}, bf16[16,1536]{1,0:T(8,128)(2,1)S(1)}, u32[]{:S(2)}, u32[]{:S(2)}) collective-permute-start(bf16[16,1536]{1,0:T(8,128)(2,1)S(1)} %pad_bitcast_fusion.1), channel_id=1, source_target_pairs={{0,4},{4,8},{8,12},{1,5},{5,9},{9,13},{2,6},{6,10},{10,14},{3,7},{... | collective-permute-start | bytes 147464 | tf_op jit(solution)/shard_map/ppermute | solution.py:821
  218.1 53.9 %collective-permute-start.3 = (f32[4,2048]{1,0:T(4,128)}, f32[4,2048]{1,0:T(4,128)S(1)}, u32[]{:S(2)}, u32[]{:S(2)}) collective-permute-start(f32[4,2048]{1,0:T(4,128)} %get-tuple-element.149), channel_id=1, source_target_pairs={{0,12},{1,13},{2,14},{3,15},{16,28},{17,29},{18,30},{19,31}} | collective-permute-start | bytes 98312 | tf_op jit(solution)/shard_map/ppermute | solution.py:821
  223.2 48.8 %collective-permute-start.2 = (f32[4,2048]{1,0:T(4,128)}, f32[4,2048]{1,0:T(4,128)S(1)}, u32[]{:S(2)}, u32[]{:S(2)}) collective-permute-start(f32[4,2048]{1,0:T(4,128)} %get-tuple-element.149), channel_id=1, source_target_pairs={{0,8},{4,12},{1,9},{5,13},{2,10},{6,14},{3,11},{7,15},{16,24},{20,... | collective-permute-start | bytes 98312 | tf_op jit(solution)/shard_map/ppermute | solution.py:821
  224.5 47.6 %collective-permute-start.1 = (f32[4,2048]{1,0:T(4,128)}, f32[4,2048]{1,0:T(4,128)S(1)}, u32[]{:S(2)}, u32[]{:S(2)}) collective-permute-start(f32[4,2048]{1,0:T(4,128)} %get-tuple-element.149), channel_id=1, source_target_pairs={{0,4},{4,8},{8,12},{1,5},{5,9},{9,13},{2,6},{6,10},{10,14},{3,7},{... | collective-permute-start | bytes 98312 | tf_op jit(solution)/shard_map/ppermute | solution.py:821
  553.5 89.7 %collective-permute-start.14 = (bf16[4608,512]{1,0:T(8,128)(2,1)}, bf16[4608,512]{1,0:T(8,128)(2,1)}, u32[]{:S(2)}, u32[]{:S(2)}) collective-permute-start(bf16[4608,512]{1,0:T(8,128)(2,1)} %bitcast.257), channel_id=1, source_target_pairs={{0,1},{1,0},{2,3},{3,2},{4,5},{5,4},{6,7},{7,6},{8,9},{9,8},{10,11... | collective-permute-start | bytes 14155784 | tf_op jit(solution)/shard_map/ppermute | solution.py:861
  604.7 38.6 %collective-permute-start.13 = (bf16[512,1536]{1,0:T(8,128)(2,1)}, bf16[512,1536]{1,0:T(8,128)(2,1)}, u32[]{:S(2)}, u32[]{:S(2)}) collective-permute-start(bf16[512,1536]{1,0:T(8,128)(2,1)} %get-tuple-element.187), channel_id=1, source_target_pairs={{16,0},{17,1},{18,2},{19,3},{20,4},{21,5},{22,6},{23,7},{24,8},{25... | collective-permute-start | bytes 4718600 | tf_op jit(solution)/shard_map/ppermute | solution.py:821
  666.2 40.9 %collective-permute-start.16 = (bf16[4,288,768]{2,1,0:T(8,128)(2,1)}, bf16[4,288,768]{2,1,0:T(8,128)(2,1)S(1)}, u32[]{:S(2)}, u32[]{:S(2)}) collective-permute-start(bf16[4,288,768]{2,1,0:T(8,128)(2,1)} %bitcast.321), channel_id=1, source_target_pairs={{0,2},{1,3},{2,0},{3,1},{4,6},{5,7},{6,4},{7,5},{8,10},{9,11},{10,... | collective-permute-start | bytes 5308424 | tf_op jit(solution)/shard_map/ppermute | solution.py:864
  709.3 354.4 %reduce-scatter.26.cloned.1.call-start = ((), (), s32[]{:S(2)}) async-start(), calls=%async_computation.19 | async-start | bytes 2211840 | tf_op jit(solution)/shard_map/reduce_scatter | solution.py:870
  709.5 40.6 %collective-permute-start.19 = (bf16[4,288,768]{2,1,0:T(8,128)(2,1)S(1)}, bf16[4,288,768]{2,1,0:T(8,128)(2,1)S(1)}, u32[]{:S(2)}, u32[]{:S(2)}) collective-permute-start(bf16[4,288,768]{2,1,0:T(8,128)(2,1)S(1)} %bitcast.320), channel_id=1, source_target_pairs={{0,2},{1,3},{2,0},{3,1},{4,6},{5,7},{6,4},{7,5},{8,10},{9,11},{10,... | collective-permute-start | bytes 5308424 | tf_op jit(solution)/shard_map/ppermute | solution.py:864
  751.8 314.5 %reduce-scatter.16.cloned.1.call-start = ((), (), s32[]{:S(2)}) async-start(), calls=%async_computation.14 | async-start | bytes 2211840 | tf_op jit(solution)/shard_map/reduce_scatter | solution.py:870
  755.7 39.9 %collective-permute-start.23 = (bf16[4,96,2304]{2,1,0:T(8,128)(2,1)}, bf16[4,96,2304]{2,1,0:T(8,128)(2,1)S(1)}, u32[]{:S(2)}, u32[]{:S(2)}) collective-permute-start(bf16[4,96,2304]{2,1,0:T(8,128)(2,1)} %bitcast.319), channel_id=1, source_target_pairs={{0,2},{1,3},{2,0},{3,1},{4,6},{5,7},{6,4},{7,5},{8,10},{9,11},{10,... | collective-permute-start | bytes 5308424 | tf_op jit(solution)/shard_map/ppermute | solution.py:864
  797.3 268.9 %reduce-scatter.18.cloned.1.call-start = ((), (), s32[]{:S(2)}) async-start(), calls=%async_computation.15 | async-start | bytes 2211840 | tf_op jit(solution)/shard_map/reduce_scatter | solution.py:870
  797.4 39.0 %collective-permute-start.25 = (bf16[4,96,2304]{2,1,0:T(8,128)(2,1)}, bf16[4,96,2304]{2,1,0:T(8,128)(2,1)S(1)}, u32[]{:S(2)}, u32[]{:S(2)}) collective-permute-start(bf16[4,96,2304]{2,1,0:T(8,128)(2,1)} %bitcast.318), channel_id=1, source_target_pairs={{0,2},{1,3},{2,0},{3,1},{4,6},{5,7},{6,4},{7,5},{8,10},{9,11},{10,... | collective-permute-start | bytes 5308424 | tf_op jit(solution)/shard_map/ppermute | solution.py:864
  838.0 230.7 %reduce-scatter.20.cloned.1.call-start = ((), (), s32[]{:S(2)}) async-start(), calls=%async_computation.16 | async-start | bytes 2211840 | tf_op jit(solution)/shard_map/reduce_scatter | solution.py:870
  845.9 41.3 %collective-permute-start.28 = (bf16[4,96,2304]{2,1,0:T(8,128)(2,1)}, bf16[4,96,2304]{2,1,0:T(8,128)(2,1)}, u32[]{:S(2)}, u32[]{:S(2)}) collective-permute-start(bf16[4,96,2304]{2,1,0:T(8,128)(2,1)} %bitcast.317), channel_id=1, source_target_pairs={{0,2},{1,3},{2,0},{3,1},{4,6},{5,7},{6,4},{7,5},{8,10},{9,11},{10,... | collective-permute-start | bytes 5308424 | tf_op jit(solution)/shard_map/ppermute | solution.py:864
  890.4 178.4 %reduce-scatter.22.cloned.1.call-start = ((), (), s32[]{:S(2)}) async-start(), calls=%async_computation.17 | async-start | bytes 2211840 | tf_op jit(solution)/shard_map/reduce_scatter | solution.py:870
  890.7 40.5 %collective-permute-start.31 = (bf16[4,96,2304]{2,1,0:T(8,128)(2,1)}, bf16[4,96,2304]{2,1,0:T(8,128)(2,1)}, u32[]{:S(2)}, u32[]{:S(2)}) collective-permute-start(bf16[4,96,2304]{2,1,0:T(8,128)(2,1)} %bitcast.316), channel_id=1, source_target_pairs={{0,2},{1,3},{2,0},{3,1},{4,6},{5,7},{6,4},{7,5},{8,10},{9,11},{10,... | collective-permute-start | bytes 5308424 | tf_op jit(solution)/shard_map/ppermute | solution.py:864
  934.4 136.9 %reduce-scatter.14.cloned.1.call-start = ((), (), s32[]{:S(2)}) async-start(), calls=%async_computation.13 | async-start | bytes 1966080 | tf_op jit(solution)/shard_map/reduce_scatter | solution.py:870
  974.8 98.4 %reduce-scatter.12.cloned.1.call-start = ((), (), s32[]{:S(2)}) async-start(), calls=%async_computation.12 | async-start | bytes 1966080 | tf_op jit(solution)/shard_map/reduce_scatter | solution.py:870
  1014.4 84.9 %reduce-scatter.10.cloned.1.call-start = ((), (), s32[]{:S(2)}) async-start(), calls=%async_computation.11 | async-start | bytes 2334720 | tf_op jit(solution)/shard_map/reduce_scatter | solution.py:870
  1016.0 41.4 %collective-permute-start.33 = (bf16[4,96,2432]{2,1,0:T(8,128)(2,1)S(1)}, bf16[4,96,2432]{2,1,0:T(8,128)(2,1)S(1)}, u32[]{:S(2)}, u32[]{:S(2)}) collective-permute-start(bf16[4,96,2432]{2,1,0:T(8,128)(2,1)S(1)} %pad_maximum_fusion.2), channel_id=1, source_target_pairs={{0,2},{1,3},{2,0},{3,1},{4,6},{5,7},{6,4},{7,5},{8,10},{9,11},{10,... | collective-permute-start | bytes 5603336 | tf_op jit(solution)/shard_map/ppermute | solution.py:864
  (65 other events, 1013.1 us)
Sparse Core Ops, SparseCore 0:
  16.9 173.8 all-gather.2
  192.9 144.4 all-gather.4
  709.4 39.1 reduce-scatter.23
  751.9 39.4 reduce-scatter.25
  797.5 41.4 reduce-scatter.15
  841.9 37.4 reduce-scatter.17
  890.5 38.5 reduce-scatter.19
  934.5 38.5 reduce-scatter.21
  975.4 34.9 reduce-scatter.13
  1014.5 35.4 reduce-scatter.11
  1059.2 40.0 reduce-scatter.9

commit v3 on v2

--- a/solution.py
+++ b/solution.py
@@ -365,13 +365,35 @@
     return back, jnp.sum(values * q * grad, axis=0, keepdims=True)
 
 
+def down_back_kernel(dout_ref, wd_ref, dproduct_ref):
+    dproduct_ref[...] = nt_dot(dout_ref[...], wd_ref[...]).astype(BF16)
+
+
+def down_back(dout, w_down):
+    rows, dim = dout.shape
+    hidden = w_down.shape[0]
+    width = 512
+    return call(
+        down_back_kernel,
+        (hidden // width,),
+        [whole((rows, dim)), pl.BlockSpec((width, dim), lambda c: (c, 0))],
+        columns(rows, width),
+        struct((rows, hidden), BF16),
+        [],
+        2 * rows * dim * hidden,
+        2 * dim * hidden + 4 * rows * hidden,
+        (dout, w_down),
+    )
+
+
 def ff_back_kernel(
+    ready,
     dout_ref, mid_ref, gain_ref, act_ref, slope_ref, wg_ref, wu_ref, wd_ref,
     dgu_ref, dmid_ref, low_ref, dgain_ref,
     acc,
 ):
     c = pl.program_id(0)
-    dproduct = nt_dot(dout_ref[...], wd_ref[...])
+    dproduct = wd_ref[...].astype(F32) if ready else nt_dot(dout_ref[...], wd_ref[...])
     dgate = (dproduct * slope_ref[...].astype(F32)).astype(BF16)
     dup = (dproduct * act_ref[...].astype(F32)).astype(BF16)
     dgu_ref[0] = dgate
@@ -395,7 +417,7 @@
         dgain_ref[...] = dgain
 
 
-def feed_forward_back(dout, middle, gain, act, slope, w_gu, w_down):
+def feed_forward_back(dout, middle, gain, act, slope, w_gu, w_down, dproduct=None):
     rows, dim = dout.shape
     hidden = w_down.shape[0]
     width = 512
@@ -403,11 +425,11 @@
     block = columns(rows, width)
     full = whole((rows, dim))
     return call(
-        ff_back_kernel,
+        functools.partial(ff_back_kernel, dproduct is not None),
         (blocks,),
         [
             full, full, whole(gain.shape), block, block, columns(dim, width), columns(dim, width, blocks),
-            pl.BlockSpec((width, dim), lambda c: (c, 0)),
+            pl.BlockSpec((width, dim), lambda c: (c, 0)) if dproduct is None else block,
         ],
         [pl.BlockSpec((2, rows, width), lambda c: (0, 0, c)), full, full, whole((1, dim))],
         [
@@ -417,7 +439,7 @@
         [pltpu.VMEM((rows, dim), F32)],
         6 * rows * dim * hidden * 1.2,
         6 * dim * hidden,
-        (dout, middle, gain, act, slope, w_gu, w_gu, w_down),
+        (dout, middle, gain, act, slope, w_gu, w_gu, w_down if dproduct is None else dproduct),
     )
 
 
@@ -1001,8 +1023,8 @@
             )
         return outs, saved
 
-    def back_ff(m, dout, saved):
-        return feed_forward_back(dout, saved[m][8], gain_two, saved[m][12], saved[m][13], w_gu, w_down_all)
+    def back_ff(m, dout, saved, dproduct=None):
+        return feed_forward_back(dout, saved[m][8], gain_two, saved[m][12], saved[m][13], w_gu, w_down_all, dproduct)
 
     def back_mix(m, low, saved):
         return mix_back(low, w_out_all, saved[m][10], saved[m][11], saved[m][6], saved[m][4], groups, length)
@@ -1024,7 +1046,8 @@
     outs, _ = forward(own, tails, False)
     xs, halos = [], []
     for m in micros:
-        received = shifted(outs[m], "section", 1)
+        dproduct = down_back(after(own[m], outs[m]), w_down_all)
+        received = after(shifted(outs[m], "section", 1), dproduct)
         received_halo = lax.ppermute(
             tail_rows(outs[m], groups, length), ("section", "seq"), [(i, n + i + 1) for i in range(n - 1)]
         )
@@ -1036,7 +1059,7 @@
     swap = scatter.core_swap
     place = jnp.stack([scatter.core, scatter.y]).astype(jnp.int32)
 
-    ff = back_ff(0, own[0], saved)
+    ff = back_ff(0, own[0], saved, dproduct)
     mix = back_mix(0, ff[2], saved)
     gin = entering(mix[4], groups, True)
     product_t = after(saved[0][14], mix[4]).T
@@ -1095,7 +1118,7 @@
     gate_up_sums = [over_y(gate_up[0], (), gate_up[1], gin)]
     gates = back_gates(0, after(mix, gate_up_sums[0]), gin, saved)
     gate_up_sums.append(over_y(gate_up[1], gin, gates[0]))
-    out_low, dbranch, gates = after((out_low, mix[0], gates), gate_up_sums[1])
+    out_low, dbranch = after((out_low, mix[0]), gate_up_sums[1])
     out_pair, branch_pair = pair(out_low), pair(dbranch)
     base = branch_back(dbranch, w_in, first, dim)
     results = back_in(0, base, gates, dmid, xs)
@@ -1128,8 +1151,8 @@
         ]
     else:
         last = (jnp.concatenate([into[0][0], extra], axis=3),)
-    branch_sum = over_y(branch[0], last)
-    input_sum = over_y(last, out_sum)
+    branch_sum = over_y(branch[0], out_sum, last)
+    input_sum = over_y(last, branch_sum)
 
     outputs = restore(outs[0], ends.shape)
     input_grads = restore(results[1], ends.shape)

time: 1120 us -> 1110 us (level)
  waiting for transfers between devices: 479 us -> 458 us
    ppermute x17, waiting for transfers between devices: 62.1 us -> 42.8 us  [shifted(): return lax.ppermute(value, axis, pairs)]
    pallas_call x19 -> x20, Pallas kernels: 347 us -> 355 us  [call(): pl.pallas_call(kernel, grid=grid, in_specs=in_specs, out_specs=out_specs,...]
  transfers between devices with their start and end apart: 46 -> 46, of which waited for: 22 -> 20; matrix products, arithmetic and copies ran while one was open for 9% -> 9% of each run, Pallas kernels for 23% -> 24%
where the time goes in v3:
time: 1110 us; the launch traced here: 1100 us
  waiting for transfers between devices  458 us (41%)
  Pallas kernels  427 us (38%)
  local copies, waits for them, and re-layouts  86 us (8%)
  starting transfers between devices  62.1 us (6%)
  other arithmetic  50.5 us (5%)
  between operations  15.5 us (1%)
    pallas_call x20, Pallas kernels, call(): pl.pallas_call(kernel, grid=grid, in_specs=in_specs, out_specs=out_specs,...  355 us
    all_gather x2, waiting for transfers between devices, gather(): return lax.all_gather(shard, ('seq', 'fsdp'), axis=0, tiled=True)  212 us
    ppermute x9, waiting for transfers between devices, y_send(): lax.ppermute(value, 'fsdp', [(2 * a + c, 2 * b + c) for a, b in pairs for...  162 us
    pallas_call x6, Pallas kernels, outer(): pl.pallas_call(functools.partial(outer_kernel, (n, fs, share), pieces), g...  72 us
    ppermute x17, waiting for transfers between devices, shifted(): return lax.ppermute(value, axis, pairs)  42.8 us
    ppermute x17, starting transfers between devices, shifted(): return lax.ppermute(value, axis, pairs)  41 us
    reduce_scatter x9, waiting for transfers between devices, over_z(): lax.psum_scatter(shares, 'seq', scatter_dimension=0, tiled=True)[0]  26.5 us
  transfers between devices with their start and end apart: 46, of which 20 were waited for; matrix products, arithmetic and copies ran while one was open for 9% of the time, Pallas kernels for 24%

profile of v3, /device:TPU:0, one launch (start us, length us, event | category | flops | bytes accessed | tf_op | source)
XLA Modules:
  0.0 1099.0 jit_solution(3416558023764898881)
XLA Ops:
  28.8 161.9 %all-gather.3.cloned.1.call-done.wi_ref.w_ref.folded_ref = bf16[1536,11136]{1,0:T(8,128)(2,1)} async-done(((bf16[96,11136]{1,0:T(8,128)(2,1)}), bf16[1536,11136]{1,0:T(8,128)(2,1)}) %all-gather.3.cloned.1.call-update) | async-done | bytes 34209808 | tf_op jit(solution)/shard_map/all_gather | solution.py:940
  199.6 18.4 %shard_map.296 = (bf16[512,1536]{1,0:T(8,128)(2,1)}, f32[2,280,2048]{2,1,0:T(8,128)}, f32[512,2048]{1,0:T(8,128)}, f32[512,2048]{1,0:T(8,128)}, f32[512,2048]{1,...) custom-call(bf16[512,1536]{1,0:T(8,128)(2,1)} %bitcast.254, bf16[16,1536]{1,0:T(8,128)(2,1)} %copy-done.30, ...), custom_call_target="tpu_custom_call" | custom-call | flops 2013265920 | bytes 6815744 | tf_op jit(solution)/shard_map/pallas_call | solution.py:57
  255.6 16.2 %shard_map.299.wd_ref = bf16[4608,1536]{1,0:T(8,128)(2,1)} custom-call(bf16[1536,11136]{1,0:T(8,128)(2,1)} %all-gather.3.cloned.1.call-done.wi_ref.w_ref.folded_ref), custom_call_target="tpu_custom_call" | custom-call | bytes 7077888 | tf_op jit(solution)/shard_map/pallas_call | solution.py:57
  272.8 15.1 %shard_map.298 = (f32[512,2048]{1,0:T(8,128)}, bf16[512,2048]{1,0:T(8,128)(2,1)}, f32[512,1536]{1,0:T(8,128)}, bf16[512,1536]{1,0:T(8,128)(2,1)}) custom-call(bf16[512,1536]{1,0:T(8,128)(2,1)} %bitcast.255, f32[512,2048]{1,0:T(8,128)} %get-tuple-element.144.keep_ref, f32[512,2048]{1,0:T(8,128)} %get-tuple-element.145.local_ref, ...), custom_call_target="tpu_custom_call" | custom-call | flops 1207959552 | bytes 6291456 | tf_op jit(solution)/shard_map/pallas_call | solution.py:57
  287.8 49.6 %all-gather.5.cloned.1.call-done.wg_ref.wu_ref = bf16[1536,9216]{1,0:T(8,128)(2,1)} async-done(((bf16[96,9216]{1,0:T(8,128)(2,1)}), bf16[1536,9216]{1,0:T(8,128)(2,1)}) %all-gather.5.cloned.1.call-update) | async-done | bytes 28311568 | tf_op jit(solution)/shard_map/all_gather | solution.py:940
  337.4 32.1 %shard_map.300 = bf16[512,1536]{1,0:T(8,128)(2,1)} custom-call(bf16[512,1536]{1,0:T(8,128)(2,1)} %get-tuple-element.151.x_ref, f32[512,1536]{1,0:T(8,128)} %get-tuple-element.152.mid_ref, bf16[1536,9216]{1,0:T(8,128)(2,1)} %all-gather.5.cloned.1.call-done.wg_ref.wu_ref, bf16[1536,9216]{1,0:T(8,128)(2,1)} %all-gather.5.cloned.1.call-done.wg_ref.wu_ref, ...), custom_call_target="tpu_custom_call" | custom-call | flops 8153726976 | bytes 10616832 | tf_op jit(solution)/shard_map/pallas_call | solution.py:57
  377.1 14.3 %shard_map.301.wd_ref = bf16[512,4608]{1,0:T(8,128)(2,1)} custom-call(bf16[512,1536]{1,0:T(8,128)(2,1)} %bitcast.256, bf16[4608,1536]{1,0:T(8,128)(2,1)} %shard_map.299.wd_ref), custom_call_target="tpu_custom_call" | custom-call | flops 1811939328 | bytes 5898240 | tf_op jit(solution)/shard_map/pallas_call | solution.py:57
  392.1 15.2 %collective-permute-done.4 = bf16[512,1536]{1,0:T(8,128)(2,1)S(1)} collective-permute-done((bf16[512,1536]{1,0:T(8,128)(2,1)}, bf16[512,1536]{1,0:T(8,128)(2,1)S(1)}, u32[]{:S(2)}, u32[]{:S(2)}) %collective-permute-start.4) | collective-permute-done | bytes 1572896 | tf_op jit(solution)/shard_map/ppermute | solution.py:843
  408.6 17.3 %shard_map.302 = (bf16[512,1536]{1,0:T(8,128)(2,1)}, f32[2,280,2048]{2,1,0:T(8,128)}, f32[512,2048]{1,0:T(8,128)}, f32[512,2048]{1,0:T(8,128)}, f32[512,2048]{1,...) custom-call(bf16[512,1536]{1,0:T(8,128)(2,1)} %broadcast_select_fusion.1.x_ref, ...), custom_call_target="tpu_custom_call" | custom-call | flops 2013265920 | bytes 6815744 | tf_op jit(solution)/shard_map/pallas_call | solution.py:57
  447.9 14.7 %shard_map.304 = (f32[512,2048]{1,0:T(8,128)}, bf16[512,2048]{1,0:T(8,128)(2,1)}, f32[512,1536]{1,0:T(8,128)}, bf16[512,1536]{1,0:T(8,128)(2,1)}) custom-call(bf16[512,1536]{1,0:T(8,128)(2,1)} %broadcast_select_fusion.1.x_ref, f32[512,2048]{1,0:T(8,128)} %get-tuple-element.155.keep_ref, f32[512,2048]{1,0:T(8,128)} %get-tuple-element.156.local_ref, ...), custom_call_target="tpu_custom_call" | custom-call | flops 1207959552 | bytes 6291456 | tf_op jit(solution)/shard_map/pallas_call | solution.py:57
  462.5 33.9 %shard_map.305 = (bf16[512,4608]{1,0:T(8,128)(2,1)}, bf16[512,4608]{1,0:T(8,128)(2,1)}, bf16[512,4608]{1,0:T(8,128)(2,1)}, bf16[512,1536]{1,0:T(8,128)(2,1)}) custom-call(bf16[512,1536]{1,0:T(8,128)(2,1)} %get-tuple-element.188.x_ref, f32[512,1536]{1,0:T(8,128)} %get-tuple-element.163.mid_ref, bf16[1536,9216]{1,0:T(8,128)(2,1)} %all-gather.5.cloned.1.call-done.wg_ref.wu_ref, ...), custom_call_target="tpu_custom_call" | custom-call | flops 8153726976 | bytes 10616832 | tf_op jit(solution)/shard_map/pallas_call | solution.py:57
  496.5 30.2 %shard_map.306 = (bf16[2,512,4608]{2,1,0:T(8,128)(2,1)}, f32[512,1536]{1,0:T(8,128)}, bf16[512,1536]{1,0:T(8,128)(2,1)}, f32[1,1536]{1,0:T(1,128)}) custom-call(bf16[512,1536]{1,0:T(8,128)(2,1)} %bitcast.257, f32[512,1536]{1,0:T(8,128)} %get-tuple-element.163.mid_ref, f32[1,1536]{1,0:T(1,128)} %reshape.633.gain_ref, ...), custom_call_target="tpu_custom_call" | custom-call | flops 6522981376 | bytes 10616832 | tf_op jit(solution)/shard_map/pallas_call | solution.py:57
  556.5 17.7 %shard_map.308 = (f32[512,2048]{1,0:T(8,128)}, f32[16,2048]{1,0:T(8,128)}, f32[16,128,128]{2,1,0:T(8,128)}, f32[16,128,128]{2,1,0:T(8,128)}, f32[8,2048]{1,0:T(8,128)}) custom-call(f32[512,2048]{1,0:T(8,128)} %get-tuple-element.177.local_ref, f32[512,2048]{1,0:T(8,128)} %get-tuple-element.155.keep_ref, f32[512,2048]{1,0:T(8,128)} %get-tuple-element.169.hidden_ref, ...), custom_call_target="tpu_custom_call" | custom-call | flops 1073741824 | bytes 7340032 | tf_op jit(solution)/shard_map/pallas_call | solution.py:57
  613.6 23.0 %collective-permute-done.13 = bf16[512,1536]{1,0:T(8,128)(2,1)} collective-permute-done((bf16[512,1536]{1,0:T(8,128)(2,1)}, bf16[512,1536]{1,0:T(8,128)(2,1)}, u32[]{:S(2)}, u32[]{:S(2)}) %collective-permute-start.13) | collective-permute-done | bytes 1572896 | tf_op jit(solution)/shard_map/ppermute | solution.py:843
  642.8 16.6 %shard_map.311 = (bf16[1152,768]{1,0:T(8,128)(2,1)}, bf16[1152,768]{1,0:T(8,128)(2,1)}, bf16[1152,768]{1,0:T(8,128)(2,1)}, bf16[1152,768]{1,0:T(8,128)(2,1)}) custom-call(s32[2]{0:T(128)} %pad_add_fusion.place_ref, bf16[4608,512]{1,0:T(8,128)(2,1)} %bitcast.259, bf16[4608,512]{1,0:T(8,128)(2,1)} %collective-permute-done.14.left_b, ...), custom_call_target="tpu_custom_call" | custom-call | flops 1811939328 | bytes 1 | tf_op jit(solution)/shard_map/pallas_call | solution.py:802
  661.2 36.5 %shard_map.312 = (bf16[2,512,4608]{2,1,0:T(8,128)(2,1)}, f32[512,1536]{1,0:T(8,128)}, bf16[512,1536]{1,0:T(8,128)(2,1)}, f32[1,1536]{1,0:T(1,128)}) custom-call(bf16[512,1536]{1,0:T(8,128)(2,1)} %copy-done.2, f32[512,1536]{1,0:T(8,128)} %get-tuple-element.163.mid_ref, f32[1,1536]{1,0:T(1,128)} %reshape.633.gain_ref, ...), custom_call_target="tpu_custom_call" | custom-call | flops 6522981376 | bytes 10616832 | tf_op jit(solution)/shard_map/pallas_call | solution.py:57
  750.8 19.9 %shard_map.315 = (bf16[384,2304]{1,0:T(8,128)(2,1)}, bf16[384,2304]{1,0:T(8,128)(2,1)}, bf16[384,2304]{1,0:T(8,128)(2,1)}, bf16[384,2304]{1,0:T(8,128)(2,1)}, bf...) custom-call(s32[2]{0:T(128)} %pad_add_fusion.place_ref, bf16[6144,512]{1,0:T(8,128)(2,1)} %pad_maximum_fusion.left_a, ...), custom_call_target="tpu_custom_call" | custom-call | flops 2717908992 | bytes 1 | tf_op jit(solution)/shard_map/pallas_call | solution.py:802
  792.4 17.7 %shard_map.316 = (f32[512,2048]{1,0:T(8,128)}, f32[16,2048]{1,0:T(8,128)}, f32[16,128,128]{2,1,0:T(8,128)}, f32[16,128,128]{2,1,0:T(8,128)}, f32[8,2048]{1,0:T(8,128)}) custom-call(f32[512,2048]{1,0:T(8,128)} %get-tuple-element.221.local_ref, f32[512,2048]{1,0:T(8,128)} %get-tuple-element.155.keep_ref, f32[512,2048]{1,0:T(8,128)} %get-tuple-element.169.hidden_ref, ...), custom_call_target="tpu_custom_call" | custom-call | flops 1073741824 | bytes 7340032 | tf_op jit(solution)/shard_map/pallas_call | solution.py:57
  810.1 19.5 %collective-permute-done.24 = bf16[4,96,2304]{2,1,0:T(8,128)(2,1)S(1)} collective-permute-done((bf16[4,96,2304]{2,1,0:T(8,128)(2,1)}, bf16[4,96,2304]{2,1,0:T(8,128)(2,1)S(1)}, u32[]{:S(2)}, u32[]{:S(2)}) %collective-permute-start.24) | collective-permute-done | bytes 1769504 | tf_op jit(solution)/shard_map/ppermute | solution.py:886
  859.3 13.5 %collective-permute-done.28 = bf16[4,96,2304]{2,1,0:T(8,128)(2,1)} collective-permute-done((bf16[4,96,2304]{2,1,0:T(8,128)(2,1)}, bf16[4,96,2304]{2,1,0:T(8,128)(2,1)}, u32[]{:S(2)}, u32[]{:S(2)}) %collective-permute-start.28) | collective-permute-done | bytes 1769504 | tf_op jit(solution)/shard_map/ppermute | solution.py:886
  934.7 22.9 %collective-permute-done.32 = bf16[4,128,1536]{2,1,0:T(8,128)(2,1)} collective-permute-done((bf16[4,128,1536]{2,1,0:T(8,128)(2,1)}, bf16[4,128,1536]{2,1,0:T(8,128)(2,1)}, u32[]{:S(2)}, u32[]{:S(2)}) %collective-permute-start.32) | collective-permute-done | bytes 1572896 | tf_op jit(solution)/shard_map/ppermute | solution.py:886
  962.5 34.5 %collective-permute-done.33 = bf16[4,96,2048]{2,1,0:T(8,128)(2,1)} collective-permute-done((bf16[4,96,2048]{2,1,0:T(8,128)(2,1)}, bf16[4,96,2048]{2,1,0:T(8,128)(2,1)}, u32[]{:S(2)}, u32[]{:S(2)}) %collective-permute-start.33) | collective-permute-done | bytes 1572896 | tf_op jit(solution)/shard_map/ppermute | solution.py:886
  1003.8 39.5 %collective-permute-done.34 = bf16[4,96,2432]{2,1,0:T(8,128)(2,1)S(1)} collective-permute-done((bf16[4,96,2432]{2,1,0:T(8,128)(2,1)S(1)}, bf16[4,96,2432]{2,1,0:T(8,128)(2,1)S(1)}, u32[]{:S(2)}, u32[]{:S(2)}) %collective-permute-start.34) | collective-permute-done | bytes 1867808 | tf_op jit(solution)/shard_map/ppermute | solution.py:886
  1061.1 26.5 %reduce-scatter.10.cloned.1.call-done = bf16[1,96,2432]{2,1,0:T(8,128)(2,1)} async-done(((bf16[4,96,2432]{2,1,0:T(8,128)(2,1)}), bf16[1,96,2432]{2,1,0:T(8,128)(2,1)}) %reduce-scatter.10.cloned.1.call-update) | async-done | bytes 466960 | tf_op jit(solution)/shard_map/reduce_scatter | solution.py:892
  (319 shorter events, 376.8 us)
Async XLA Ops:
  7.2 183.6 %all-gather.3.cloned.1.call-start = ((), (), s32[]{:S(2)}) async-start(), calls=%async_computation.9 | async-start | bytes 36347904 | tf_op jit(solution)/shard_map/all_gather | solution.py:940
  16.8 320.6 %all-gather.5.cloned.1.call-start = ((), (), s32[]{:S(2)}) async-start(), calls=%async_computation.10 | async-start | bytes 30081024 | tf_op jit(solution)/shard_map/all_gather | solution.py:940
  19.5 1030.1 %reduce-scatter.24.cloned.1.call-start = ((), (), s32[]{:S(2)}) async-start(), calls=%async_computation.18 | async-start | bytes 2211840 | tf_op jit(solution)/shard_map/reduce_scatter | solution.py:892
  21.3 177.0 %collective-permute-start = (bf16[16,1536]{1,0:T(8,128)(2,1)S(1)}, bf16[16,1536]{1,0:T(8,128)(2,1)S(1)}, u32[]{:S(2)}, u32[]{:S(2)}) collective-permute-start(bf16[16,1536]{1,0:T(8,128)(2,1)S(1)} %pad_bitcast_fusion.1), channel_id=1, source_target_pairs={{0,4},{4,8},{8,12},{1,5},{5,9},{9,13},{2,6},{6,10},{10,14},{3,7},{... | collective-permute-start | bytes 147464 | tf_op jit(solution)/shard_map/ppermute | solution.py:843
  218.1 53.8 %collective-permute-start.3 = (f32[4,2048]{1,0:T(4,128)}, f32[4,2048]{1,0:T(4,128)S(1)}, u32[]{:S(2)}, u32[]{:S(2)}) collective-permute-start(f32[4,2048]{1,0:T(4,128)} %get-tuple-element.147), channel_id=1, source_target_pairs={{0,12},{1,13},{2,14},{3,15},{16,28},{17,29},{18,30},{19,31}} | collective-permute-start | bytes 98312 | tf_op jit(solution)/shard_map/ppermute | solution.py:843
  223.2 48.7 %collective-permute-start.2 = (f32[4,2048]{1,0:T(4,128)}, f32[4,2048]{1,0:T(4,128)S(1)}, u32[]{:S(2)}, u32[]{:S(2)}) collective-permute-start(f32[4,2048]{1,0:T(4,128)} %get-tuple-element.147), channel_id=1, source_target_pairs={{0,8},{4,12},{1,9},{5,13},{2,10},{6,14},{3,11},{7,15},{16,24},{20,... | collective-permute-start | bytes 98312 | tf_op jit(solution)/shard_map/ppermute | solution.py:843
  224.5 47.5 %collective-permute-start.1 = (f32[4,2048]{1,0:T(4,128)}, f32[4,2048]{1,0:T(4,128)S(1)}, u32[]{:S(2)}, u32[]{:S(2)}) collective-permute-start(f32[4,2048]{1,0:T(4,128)} %get-tuple-element.147), channel_id=1, source_target_pairs={{0,4},{4,8},{8,12},{1,5},{5,9},{9,13},{2,6},{6,10},{10,14},{3,7},{... | collective-permute-start | bytes 98312 | tf_op jit(solution)/shard_map/ppermute | solution.py:843
  546.8 89.8 %collective-permute-start.14 = (bf16[4608,512]{1,0:T(8,128)(2,1)}, bf16[4608,512]{1,0:T(8,128)(2,1)}, u32[]{:S(2)}, u32[]{:S(2)}) collective-permute-start(bf16[4608,512]{1,0:T(8,128)(2,1)} %bitcast.258), channel_id=1, source_target_pairs={{0,1},{1,0},{2,3},{3,2},{4,5},{5,4},{6,7},{7,6},{8,9},{9,8},{10,11... | collective-permute-start | bytes 14155784 | tf_op jit(solution)/shard_map/ppermute | solution.py:883
  598.0 38.6 %collective-permute-start.13 = (bf16[512,1536]{1,0:T(8,128)(2,1)}, bf16[512,1536]{1,0:T(8,128)(2,1)}, u32[]{:S(2)}, u32[]{:S(2)}) collective-permute-start(bf16[512,1536]{1,0:T(8,128)(2,1)} %get-tuple-element.187), channel_id=1, source_target_pairs={{16,0},{17,1},{18,2},{19,3},{20,4},{21,5},{22,6},{23,7},{24,8},{25... | collective-permute-start | bytes 4718600 | tf_op jit(solution)/shard_map/ppermute | solution.py:843
  659.4 40.9 %collective-permute-start.16 = (bf16[4,288,768]{2,1,0:T(8,128)(2,1)}, bf16[4,288,768]{2,1,0:T(8,128)(2,1)S(1)}, u32[]{:S(2)}, u32[]{:S(2)}) collective-permute-start(bf16[4,288,768]{2,1,0:T(8,128)(2,1)} %bitcast.321), channel_id=1, source_target_pairs={{0,2},{1,3},{2,0},{3,1},{4,6},{5,7},{6,4},{7,5},{8,10},{9,11},{10,... | collective-permute-start | bytes 5308424 | tf_op jit(solution)/shard_map/ppermute | solution.py:886
  702.5 347.1 %reduce-scatter.26.cloned.1.call-start = ((), (), s32[]{:S(2)}) async-start(), calls=%async_computation.19 | async-start | bytes 2211840 | tf_op jit(solution)/shard_map/reduce_scatter | solution.py:892
  702.8 40.6 %collective-permute-start.19 = (bf16[4,288,768]{2,1,0:T(8,128)(2,1)S(1)}, bf16[4,288,768]{2,1,0:T(8,128)(2,1)S(1)}, u32[]{:S(2)}, u32[]{:S(2)}) collective-permute-start(bf16[4,288,768]{2,1,0:T(8,128)(2,1)S(1)} %bitcast.320), channel_id=1, source_target_pairs={{0,2},{1,3},{2,0},{3,1},{4,6},{5,7},{6,4},{7,5},{8,10},{9,11},{10,... | collective-permute-start | bytes 5308424 | tf_op jit(solution)/shard_map/ppermute | solution.py:886
  745.0 307.1 %reduce-scatter.16.cloned.1.call-start = ((), (), s32[]{:S(2)}) async-start(), calls=%async_computation.14 | async-start | bytes 2211840 | tf_op jit(solution)/shard_map/reduce_scatter | solution.py:892
  749.0 39.9 %collective-permute-start.23 = (bf16[4,96,2304]{2,1,0:T(8,128)(2,1)}, bf16[4,96,2304]{2,1,0:T(8,128)(2,1)S(1)}, u32[]{:S(2)}, u32[]{:S(2)}) collective-permute-start(bf16[4,96,2304]{2,1,0:T(8,128)(2,1)} %bitcast.319), channel_id=1, source_target_pairs={{0,2},{1,3},{2,0},{3,1},{4,6},{5,7},{6,4},{7,5},{8,10},{9,11},{10,... | collective-permute-start | bytes 5308424 | tf_op jit(solution)/shard_map/ppermute | solution.py:886
  790.6 261.6 %reduce-scatter.18.cloned.1.call-start = ((), (), s32[]{:S(2)}) async-start(), calls=%async_computation.15 | async-start | bytes 2211840 | tf_op jit(solution)/shard_map/reduce_scatter | solution.py:892
  790.6 39.0 %collective-permute-start.24 = (bf16[4,96,2304]{2,1,0:T(8,128)(2,1)}, bf16[4,96,2304]{2,1,0:T(8,128)(2,1)S(1)}, u32[]{:S(2)}, u32[]{:S(2)}) collective-permute-start(bf16[4,96,2304]{2,1,0:T(8,128)(2,1)} %bitcast.318), channel_id=1, source_target_pairs={{0,2},{1,3},{2,0},{3,1},{4,6},{5,7},{6,4},{7,5},{8,10},{9,11},{10,... | collective-permute-start | bytes 5308424 | tf_op jit(solution)/shard_map/ppermute | solution.py:886
  831.3 223.4 %reduce-scatter.20.cloned.1.call-start = ((), (), s32[]{:S(2)}) async-start(), calls=%async_computation.16 | async-start | bytes 2211840 | tf_op jit(solution)/shard_map/reduce_scatter | solution.py:892
  831.4 41.3 %collective-permute-start.28 = (bf16[4,96,2304]{2,1,0:T(8,128)(2,1)}, bf16[4,96,2304]{2,1,0:T(8,128)(2,1)}, u32[]{:S(2)}, u32[]{:S(2)}) collective-permute-start(bf16[4,96,2304]{2,1,0:T(8,128)(2,1)} %bitcast.317), channel_id=1, source_target_pairs={{0,2},{1,3},{2,0},{3,1},{4,6},{5,7},{6,4},{7,5},{8,10},{9,11},{10,... | collective-permute-start | bytes 5308424 | tf_op jit(solution)/shard_map/ppermute | solution.py:886
  876.1 178.6 %reduce-scatter.22.cloned.1.call-start = ((), (), s32[]{:S(2)}) async-start(), calls=%async_computation.17 | async-start | bytes 2211840 | tf_op jit(solution)/shard_map/reduce_scatter | solution.py:892
  876.4 40.6 %collective-permute-start.31 = (bf16[4,96,2304]{2,1,0:T(8,128)(2,1)}, bf16[4,96,2304]{2,1,0:T(8,128)(2,1)}, u32[]{:S(2)}, u32[]{:S(2)}) collective-permute-start(bf16[4,96,2304]{2,1,0:T(8,128)(2,1)} %bitcast.100), channel_id=1, source_target_pairs={{0,2},{1,3},{2,0},{3,1},{4,6},{5,7},{6,4},{7,5},{8,10},{9,11},{10,... | collective-permute-start | bytes 5308424 | tf_op jit(solution)/shard_map/ppermute | solution.py:886
  920.1 137.1 %reduce-scatter.14.cloned.1.call-start = ((), (), s32[]{:S(2)}) async-start(), calls=%async_computation.13 | async-start | bytes 1966080 | tf_op jit(solution)/shard_map/reduce_scatter | solution.py:892
  960.7 98.4 %reduce-scatter.12.cloned.1.call-start = ((), (), s32[]{:S(2)}) async-start(), calls=%async_computation.12 | async-start | bytes 1966080 | tf_op jit(solution)/shard_map/reduce_scatter | solution.py:892
  1000.3 87.3 %reduce-scatter.10.cloned.1.call-start = ((), (), s32[]{:S(2)}) async-start(), calls=%async_computation.11 | async-start | bytes 2334720 | tf_op jit(solution)/shard_map/reduce_scatter | solution.py:892
  1001.8 41.4 %collective-permute-start.34 = (bf16[4,96,2432]{2,1,0:T(8,128)(2,1)S(1)}, bf16[4,96,2432]{2,1,0:T(8,128)(2,1)S(1)}, u32[]{:S(2)}, u32[]{:S(2)}) collective-permute-start(bf16[4,96,2432]{2,1,0:T(8,128)(2,1)S(1)} %pad_maximum_fusion.2), channel_id=1, source_target_pairs={{0,2},{1,3},{2,0},{3,1},{4,6},{5,7},{6,4},{7,5},{8,10},{9,11},{10,... | collective-permute-start | bytes 5603336 | tf_op jit(solution)/shard_map/ppermute | solution.py:886
  (65 other events, 915.4 us)
Sparse Core Ops, SparseCore 0:
  16.9 173.8 all-gather.2
  192.9 144.4 all-gather.4
  702.6 39.1 reduce-scatter.23
  745.1 39.4 reduce-scatter.25
  790.7 41.4 reduce-scatter.15
  835.1 38.2 reduce-scatter.17
  876.2 40.8 reduce-scatter.19
  920.2 40.8 reduce-scatter.21
  963.4 35.1 reduce-scatter.13
  1000.8 37.4 reduce-scatter.11
  1045.1 42.4 reduce-scatter.9

commit v4 on v3

--- a/solution.py
+++ b/solution.py
@@ -317,7 +317,7 @@
         act_ref[...] = act.astype(BF16)
         slope_ref[...] = (up * slope).astype(BF16)
         product = (act * up).astype(BF16)
-        product_ref[...] = product
+        product_ref[...] = product.T
     else:
         product = (gelu(gate) * up).astype(BF16)
     part = nn_dot(product, wd_ref[...])
@@ -341,7 +341,6 @@
     width = 512
     blocks = hidden // width
     block = columns(rows, width)
-    kept = 3 if save else 0
     return call(
         functools.partial(ff_kernel, save),
         (blocks,),
@@ -349,8 +348,9 @@
             whole(x.shape), whole(middle.shape), columns(dim, width), columns(dim, width, blocks),
             pl.BlockSpec((width, dim), lambda c: (c, 0)),
         ],
-        [block] * kept + [whole((rows, dim))],
-        [struct((rows, hidden), BF16)] * kept + [struct((rows, dim), BF16)],
+        ([block] * 2 + [pl.BlockSpec((width, rows), lambda c: (c, 0))] if save else []) + [whole((rows, dim))],
+        ([struct((rows, hidden), BF16)] * 2 + [struct((hidden, rows), BF16)] if save else [])
+        + [struct((rows, dim), BF16)],
         [pltpu.VMEM((rows, dim), F32)],
         6 * rows * dim * hidden * 1.5,
         6 * dim * hidden,
@@ -1062,9 +1062,9 @@
     ff = back_ff(0, own[0], saved, dproduct)
     mix = back_mix(0, ff[2], saved)
     gin = entering(mix[4], groups, True)
-    product_t = after(saved[0][14], mix[4]).T
-    product_pair = (product_t, swap(product_t))
-    gates = back_gates(0, after(mix, product_t), gin, saved)
+    product_t = saved[0][14]
+    product_pair = (product_t, swap(after(product_t, mix[4])))
+    gates = back_gates(0, mix, gin, saved)
     base = branch_back(after(mix[0], gates[0]), w_in, first, dim)
     dx = back_in(0, base, gates, ff[1], xs)[1]
     others = [after(saved[0][i], dx) for i in (9, 0, 7)]

time: 1110 us -> 1100 us (level)
  transfers between devices with their start and end apart: 46 -> 46, of which waited for: 20 -> 20; matrix products, arithmetic and copies ran while one was open for 9% -> 9% of each run, Pallas kernels for 24% -> 25%
where the time goes in v4:
time: 1100 us; the launch traced here: 1090 us
  waiting for transfers between devices  458 us (42%)
  Pallas kernels  427 us (39%)
  local copies, waits for them, and re-layouts  79.2 us (7%)
  starting transfers between devices  62.3 us (6%)
  other arithmetic  50.5 us (5%)
  between operations  15.2 us (1%)
    pallas_call x20, Pallas kernels, call(): pl.pallas_call(kernel, grid=grid, in_specs=in_specs, out_specs=out_specs,...  355 us
    all_gather x2, waiting for transfers between devices, gather(): return lax.all_gather(shard, ('seq', 'fsdp'), axis=0, tiled=True)  212 us
    ppermute x9, waiting for transfers between devices, y_send(): lax.ppermute(value, 'fsdp', [(2 * a + c, 2 * b + c) for a, b in pairs for...  162 us
    pallas_call x6, Pallas kernels, outer(): pl.pallas_call(functools.partial(outer_kernel, (n, fs, share), pieces), g...  72 us
    ppermute x17, waiting for transfers between devices, shifted(): return lax.ppermute(value, axis, pairs)  43.2 us
    ppermute x17, starting transfers between devices, shifted(): return lax.ppermute(value, axis, pairs)  41.4 us
    reduce_scatter x9, waiting for transfers between devices, over_z(): lax.psum_scatter(shares, 'seq', scatter_dimension=0, tiled=True)[0]  26.4 us
  transfers between devices with their start and end apart: 46, of which 20 were waited for; matrix products, arithmetic and copies ran while one was open for 9% of the time, Pallas kernels for 25%

profile of v4, /device:TPU:0, one launch (start us, length us, event | category | flops | bytes accessed | tf_op | source)
XLA Modules:
  0.0 1092.3 jit_solution(7017086872294165350)
XLA Ops:
  28.9 161.9 %all-gather.3.cloned.1.call-done.wi_ref.w_ref.folded_ref = bf16[1536,11136]{1,0:T(8,128)(2,1)} async-done(((bf16[96,11136]{1,0:T(8,128)(2,1)}), bf16[1536,11136]{1,0:T(8,128)(2,1)}) %all-gather.3.cloned.1.call-update) | async-done | bytes 34209808 | tf_op jit(solution)/shard_map/all_gather | solution.py:940
  199.6 18.4 %shard_map.296 = (bf16[512,1536]{1,0:T(8,128)(2,1)}, f32[2,280,2048]{2,1,0:T(8,128)}, f32[512,2048]{1,0:T(8,128)}, f32[512,2048]{1,0:T(8,128)}, f32[512,2048]{1,...) custom-call(bf16[512,1536]{1,0:T(8,128)(2,1)} %bitcast.253, bf16[16,1536]{1,0:T(8,128)(2,1)} %copy-done.30, ...), custom_call_target="tpu_custom_call" | custom-call | flops 2013265920 | bytes 6815744 | tf_op jit(solution)/shard_map/pallas_call | solution.py:57
  255.6 16.2 %shard_map.299.wd_ref = bf16[4608,1536]{1,0:T(8,128)(2,1)} custom-call(bf16[1536,11136]{1,0:T(8,128)(2,1)} %all-gather.3.cloned.1.call-done.wi_ref.w_ref.folded_ref), custom_call_target="tpu_custom_call" | custom-call | bytes 7077888 | tf_op jit(solution)/shard_map/pallas_call | solution.py:57
  272.7 15.1 %shard_map.298 = (f32[512,2048]{1,0:T(8,128)}, bf16[512,2048]{1,0:T(8,128)(2,1)}, f32[512,1536]{1,0:T(8,128)}, bf16[512,1536]{1,0:T(8,128)(2,1)}) custom-call(bf16[512,1536]{1,0:T(8,128)(2,1)} %bitcast.254, f32[512,2048]{1,0:T(8,128)} %get-tuple-element.141.keep_ref, f32[512,2048]{1,0:T(8,128)} %get-tuple-element.142.local_ref, ...), custom_call_target="tpu_custom_call" | custom-call | flops 1207959552 | bytes 6291456 | tf_op jit(solution)/shard_map/pallas_call | solution.py:57
  287.8 49.6 %all-gather.5.cloned.1.call-done.wg_ref.wu_ref = bf16[1536,9216]{1,0:T(8,128)(2,1)} async-done(((bf16[96,9216]{1,0:T(8,128)(2,1)}), bf16[1536,9216]{1,0:T(8,128)(2,1)}) %all-gather.5.cloned.1.call-update) | async-done | bytes 28311568 | tf_op jit(solution)/shard_map/all_gather | solution.py:940
  337.4 32.1 %shard_map.300 = bf16[512,1536]{1,0:T(8,128)(2,1)} custom-call(bf16[512,1536]{1,0:T(8,128)(2,1)} %get-tuple-element.148.x_ref, f32[512,1536]{1,0:T(8,128)} %get-tuple-element.149.mid_ref, bf16[1536,9216]{1,0:T(8,128)(2,1)} %all-gather.5.cloned.1.call-done.wg_ref.wu_ref, bf16[1536,9216]{1,0:T(8,128)(2,1)} %all-gather.5.cloned.1.call-done.wg_ref.wu_ref, ...), custom_call_target="tpu_custom_call" | custom-call | flops 8153726976 | bytes 10616832 | tf_op jit(solution)/shard_map/pallas_call | solution.py:57
  377.1 14.3 %shard_map.301.wd_ref = bf16[512,4608]{1,0:T(8,128)(2,1)} custom-call(bf16[512,1536]{1,0:T(8,128)(2,1)} %bitcast.255, bf16[4608,1536]{1,0:T(8,128)(2,1)} %shard_map.299.wd_ref), custom_call_target="tpu_custom_call" | custom-call | flops 1811939328 | bytes 5898240 | tf_op jit(solution)/shard_map/pallas_call | solution.py:57
  392.1 15.2 %collective-permute-done.4 = bf16[512,1536]{1,0:T(8,128)(2,1)S(1)} collective-permute-done((bf16[512,1536]{1,0:T(8,128)(2,1)}, bf16[512,1536]{1,0:T(8,128)(2,1)S(1)}, u32[]{:S(2)}, u32[]{:S(2)}) %collective-permute-start.4) | collective-permute-done | bytes 1572896 | tf_op jit(solution)/shard_map/ppermute | solution.py:843
  408.6 17.4 %shard_map.302 = (bf16[512,1536]{1,0:T(8,128)(2,1)}, f32[2,280,2048]{2,1,0:T(8,128)}, f32[512,2048]{1,0:T(8,128)}, f32[512,2048]{1,0:T(8,128)}, f32[512,2048]{1,...) custom-call(bf16[512,1536]{1,0:T(8,128)(2,1)} %broadcast_select_fusion.1.x_ref, ...), custom_call_target="tpu_custom_call" | custom-call | flops 2013265920 | bytes 6815744 | tf_op jit(solution)/shard_map/pallas_call | solution.py:57
  448.2 14.7 %shard_map.304 = (f32[512,2048]{1,0:T(8,128)}, bf16[512,2048]{1,0:T(8,128)(2,1)}, f32[512,1536]{1,0:T(8,128)}, bf16[512,1536]{1,0:T(8,128)(2,1)}) custom-call(bf16[512,1536]{1,0:T(8,128)(2,1)} %broadcast_select_fusion.1.x_ref, f32[512,2048]{1,0:T(8,128)} %get-tuple-element.152.keep_ref, f32[512,2048]{1,0:T(8,128)} %get-tuple-element.153.local_ref, ...), custom_call_target="tpu_custom_call" | custom-call | flops 1207959552 | bytes 6291456 | tf_op jit(solution)/shard_map/pallas_call | solution.py:57
  462.9 33.9 %shard_map.305 = (bf16[512,4608]{1,0:T(8,128)(2,1)}, bf16[512,4608]{1,0:T(8,128)(2,1)}, bf16[4608,512]{1,0:T(8,128)(2,1)}, bf16[512,1536]{1,0:T(8,128)(2,1)}) custom-call(bf16[512,1536]{1,0:T(8,128)(2,1)} %get-tuple-element.180.x_ref, f32[512,1536]{1,0:T(8,128)} %get-tuple-element.160.mid_ref, bf16[1536,9216]{1,0:T(8,128)(2,1)} %all-gather.5.cloned.1.call-done.wg_ref.wu_ref, ...), custom_call_target="tpu_custom_call" | custom-call | flops 8153726976 | bytes 10616832 | tf_op jit(solution)/shard_map/pallas_call | solution.py:57
  496.8 30.2 %shard_map.306 = (bf16[2,512,4608]{2,1,0:T(8,128)(2,1)}, f32[512,1536]{1,0:T(8,128)}, bf16[512,1536]{1,0:T(8,128)(2,1)}, f32[1,1536]{1,0:T(1,128)}) custom-call(bf16[512,1536]{1,0:T(8,128)(2,1)} %bitcast.256, f32[512,1536]{1,0:T(8,128)} %get-tuple-element.160.mid_ref, f32[1,1536]{1,0:T(1,128)} %reshape.633.gain_ref, ...), custom_call_target="tpu_custom_call" | custom-call | flops 6522981376 | bytes 10616832 | tf_op jit(solution)/shard_map/pallas_call | solution.py:57
  550.3 17.5 %shard_map.308 = (f32[512,2048]{1,0:T(8,128)}, f32[16,2048]{1,0:T(8,128)}, f32[16,128,128]{2,1,0:T(8,128)}, f32[16,128,128]{2,1,0:T(8,128)}, f32[8,2048]{1,0:T(8,128)}) custom-call(f32[512,2048]{1,0:T(8,128)} %get-tuple-element.168.local_ref, f32[512,2048]{1,0:T(8,128)} %get-tuple-element.152.keep_ref, f32[512,2048]{1,0:T(8,128)} %get-tuple-element.166.hidden_ref, ...), custom_call_target="tpu_custom_call" | custom-call | flops 1073741824 | bytes 7340032 | tf_op jit(solution)/shard_map/pallas_call | solution.py:57
  607.4 23.0 %collective-permute-done.13 = bf16[512,1536]{1,0:T(8,128)(2,1)} collective-permute-done((bf16[512,1536]{1,0:T(8,128)(2,1)}, bf16[512,1536]{1,0:T(8,128)(2,1)}, u32[]{:S(2)}, u32[]{:S(2)}) %collective-permute-start.13) | collective-permute-done | bytes 1572896 | tf_op jit(solution)/shard_map/ppermute | solution.py:843
  636.5 16.7 %shard_map.311 = (bf16[1152,768]{1,0:T(8,128)(2,1)}, bf16[1152,768]{1,0:T(8,128)(2,1)}, bf16[1152,768]{1,0:T(8,128)(2,1)}, bf16[1152,768]{1,0:T(8,128)(2,1)}) custom-call(s32[2]{0:T(128)} %pad_add_fusion.place_ref, bf16[4608,512]{1,0:T(8,128)(2,1)} %get-tuple-element.185.left_a, bf16[4608,512]{1,0:T(8,128)(2,1)} %collective-permute-done.14.left_b, ...), custom_call_target="tpu_custom_call" | custom-call | flops 1811939328 | bytes 1 | tf_op jit(solution)/shard_map/pallas_call | solution.py:802
  655.0 36.4 %shard_map.312 = (bf16[2,512,4608]{2,1,0:T(8,128)(2,1)}, f32[512,1536]{1,0:T(8,128)}, bf16[512,1536]{1,0:T(8,128)(2,1)}, f32[1,1536]{1,0:T(1,128)}) custom-call(bf16[512,1536]{1,0:T(8,128)(2,1)} %copy-done.2, f32[512,1536]{1,0:T(8,128)} %get-tuple-element.160.mid_ref, f32[1,1536]{1,0:T(1,128)} %reshape.633.gain_ref, ...), custom_call_target="tpu_custom_call" | custom-call | flops 6522981376 | bytes 10616832 | tf_op jit(solution)/shard_map/pallas_call | solution.py:57
  744.6 19.9 %shard_map.315 = (bf16[384,2304]{1,0:T(8,128)(2,1)}, bf16[384,2304]{1,0:T(8,128)(2,1)}, bf16[384,2304]{1,0:T(8,128)(2,1)}, bf16[384,2304]{1,0:T(8,128)(2,1)}, bf...) custom-call(s32[2]{0:T(128)} %pad_add_fusion.place_ref, bf16[6144,512]{1,0:T(8,128)(2,1)} %pad_maximum_fusion.left_a, ...), custom_call_target="tpu_custom_call" | custom-call | flops 2717908992 | bytes 1 | tf_op jit(solution)/shard_map/pallas_call | solution.py:802
  786.2 17.6 %shard_map.316 = (f32[512,2048]{1,0:T(8,128)}, f32[16,2048]{1,0:T(8,128)}, f32[16,128,128]{2,1,0:T(8,128)}, f32[16,128,128]{2,1,0:T(8,128)}, f32[8,2048]{1,0:T(8,128)}) custom-call(f32[512,2048]{1,0:T(8,128)} %get-tuple-element.215.local_ref, f32[512,2048]{1,0:T(8,128)} %get-tuple-element.152.keep_ref, f32[512,2048]{1,0:T(8,128)} %get-tuple-element.166.hidden_ref, ...), custom_call_target="tpu_custom_call" | custom-call | flops 1073741824 | bytes 7340032 | tf_op jit(solution)/shard_map/pallas_call | solution.py:57
  803.8 19.6 %collective-permute-done.24 = bf16[4,96,2304]{2,1,0:T(8,128)(2,1)S(1)} collective-permute-done((bf16[4,96,2304]{2,1,0:T(8,128)(2,1)}, bf16[4,96,2304]{2,1,0:T(8,128)(2,1)S(1)}, u32[]{:S(2)}, u32[]{:S(2)}) %collective-permute-start.24) | collective-permute-done | bytes 1769504 | tf_op jit(solution)/shard_map/ppermute | solution.py:886
  838.6 13.3 %shard_map.318 = (bf16[512,2048]{1,0:T(8,128)(2,1)}, bf16[512,1536]{1,0:T(8,128)(2,1)}, f32[1,1536]{1,0:T(1,128)}) custom-call(f32[512,1536]{1,0:T(8,128)} %shard_map.317.part_ref, f32[512,2048]{1,0:T(8,128)} %get-tuple-element.218.din_ref, f32[16,2048]{1,0:T(8,128)} %copy-done.33, bf16[1536,11136]{1,0:T(8,128)(2,1)} %all-gather.3.cloned.1.call-done.wi_ref.w_ref.folded_ref, ...), custom_call_target="tpu_custom_call" | custom-call | flops 1207959552 | bytes 3670016 | tf_op jit(solution)/shard_map/pallas_call | solution.py:57
  928.3 22.9 %collective-permute-done.32 = bf16[4,128,1536]{2,1,0:T(8,128)(2,1)} collective-permute-done((bf16[4,128,1536]{2,1,0:T(8,128)(2,1)}, bf16[4,128,1536]{2,1,0:T(8,128)(2,1)}, u32[]{:S(2)}, u32[]{:S(2)}) %collective-permute-start.32) | collective-permute-done | bytes 1572896 | tf_op jit(solution)/shard_map/ppermute | solution.py:886
  956.1 34.6 %collective-permute-done.33 = bf16[4,96,2048]{2,1,0:T(8,128)(2,1)} collective-permute-done((bf16[4,96,2048]{2,1,0:T(8,128)(2,1)}, bf16[4,96,2048]{2,1,0:T(8,128)(2,1)}, u32[]{:S(2)}, u32[]{:S(2)}) %collective-permute-start.33) | collective-permute-done | bytes 1572896 | tf_op jit(solution)/shard_map/ppermute | solution.py:886
  997.4 39.5 %collective-permute-done.34 = bf16[4,96,2432]{2,1,0:T(8,128)(2,1)S(1)} collective-permute-done((bf16[4,96,2432]{2,1,0:T(8,128)(2,1)S(1)}, bf16[4,96,2432]{2,1,0:T(8,128)(2,1)S(1)}, u32[]{:S(2)}, u32[]{:S(2)}) %collective-permute-start.34) | collective-permute-done | bytes 1867808 | tf_op jit(solution)/shard_map/ppermute | solution.py:886
  1054.7 26.4 %reduce-scatter.10.cloned.1.call-done = bf16[1,96,2432]{2,1,0:T(8,128)(2,1)} async-done(((bf16[4,96,2432]{2,1,0:T(8,128)(2,1)}), bf16[1,96,2432]{2,1,0:T(8,128)(2,1)}) %reduce-scatter.10.cloned.1.call-update) | async-done | bytes 466960 | tf_op jit(solution)/shard_map/reduce_scatter | solution.py:892
  (316 shorter events, 370.6 us)
Async XLA Ops:
  7.2 183.6 %all-gather.3.cloned.1.call-start = ((), (), s32[]{:S(2)}) async-start(), calls=%async_computation.9 | async-start | bytes 36347904 | tf_op jit(solution)/shard_map/all_gather | solution.py:940
  16.8 320.6 %all-gather.5.cloned.1.call-start = ((), (), s32[]{:S(2)}) async-start(), calls=%async_computation.10 | async-start | bytes 30081024 | tf_op jit(solution)/shard_map/all_gather | solution.py:940
  19.5 1023.7 %reduce-scatter.24.cloned.1.call-start = ((), (), s32[]{:S(2)}) async-start(), calls=%async_computation.18 | async-start | bytes 2211840 | tf_op jit(solution)/shard_map/reduce_scatter | solution.py:892
  21.3 177.0 %collective-permute-start = (bf16[16,1536]{1,0:T(8,128)(2,1)S(1)}, bf16[16,1536]{1,0:T(8,128)(2,1)S(1)}, u32[]{:S(2)}, u32[]{:S(2)}) collective-permute-start(bf16[16,1536]{1,0:T(8,128)(2,1)S(1)} %pad_bitcast_fusion.1), channel_id=1, source_target_pairs={{0,4},{4,8},{8,12},{1,5},{5,9},{9,13},{2,6},{6,10},{10,14},{3,7},{... | collective-permute-start | bytes 147464 | tf_op jit(solution)/shard_map/ppermute | solution.py:843
  218.1 53.8 %collective-permute-start.3 = (f32[4,2048]{1,0:T(4,128)}, f32[4,2048]{1,0:T(4,128)S(1)}, u32[]{:S(2)}, u32[]{:S(2)}) collective-permute-start(f32[4,2048]{1,0:T(4,128)} %get-tuple-element.144), channel_id=1, source_target_pairs={{0,12},{1,13},{2,14},{3,15},{16,28},{17,29},{18,30},{19,31}} | collective-permute-start | bytes 98312 | tf_op jit(solution)/shard_map/ppermute | solution.py:843
  223.2 48.7 %collective-permute-start.2 = (f32[4,2048]{1,0:T(4,128)}, f32[4,2048]{1,0:T(4,128)S(1)}, u32[]{:S(2)}, u32[]{:S(2)}) collective-permute-start(f32[4,2048]{1,0:T(4,128)} %get-tuple-element.144), channel_id=1, source_target_pairs={{0,8},{4,12},{1,9},{5,13},{2,10},{6,14},{3,11},{7,15},{16,24},{20,... | collective-permute-start | bytes 98312 | tf_op jit(solution)/shard_map/ppermute | solution.py:843
  224.5 47.5 %collective-permute-start.1 = (f32[4,2048]{1,0:T(4,128)}, f32[4,2048]{1,0:T(4,128)S(1)}, u32[]{:S(2)}, u32[]{:S(2)}) collective-permute-start(f32[4,2048]{1,0:T(4,128)} %get-tuple-element.144), channel_id=1, source_target_pairs={{0,4},{4,8},{8,12},{1,5},{5,9},{9,13},{2,6},{6,10},{10,14},{3,7},{... | collective-permute-start | bytes 98312 | tf_op jit(solution)/shard_map/ppermute | solution.py:843
  540.3 90.0 %collective-permute-start.14 = (bf16[4608,512]{1,0:T(8,128)(2,1)}, bf16[4608,512]{1,0:T(8,128)(2,1)}, u32[]{:S(2)}, u32[]{:S(2)}) collective-permute-start(bf16[4608,512]{1,0:T(8,128)(2,1)} %get-tuple-element.185.left_a), channel_id=1, source_target_pairs={{0,1},{1,0},{2,3},{3,2},{4,5},{5,4},{6,7},{7,6},{8,9},{9,8},{10,11... | collective-permute-start | bytes 14155784 | tf_op jit(solution)/shard_map/ppermute | solution.py:883
  591.8 38.5 %collective-permute-start.13 = (bf16[512,1536]{1,0:T(8,128)(2,1)}, bf16[512,1536]{1,0:T(8,128)(2,1)}, u32[]{:S(2)}, u32[]{:S(2)}) collective-permute-start(bf16[512,1536]{1,0:T(8,128)(2,1)} %get-tuple-element.179), channel_id=1, source_target_pairs={{16,0},{17,1},{18,2},{19,3},{20,4},{21,5},{22,6},{23,7},{24,8},{25... | collective-permute-start | bytes 4718600 | tf_op jit(solution)/shard_map/ppermute | solution.py:843
  653.2 40.9 %collective-permute-start.16 = (bf16[4,288,768]{2,1,0:T(8,128)(2,1)}, bf16[4,288,768]{2,1,0:T(8,128)(2,1)S(1)}, u32[]{:S(2)}, u32[]{:S(2)}) collective-permute-start(bf16[4,288,768]{2,1,0:T(8,128)(2,1)} %bitcast.318), channel_id=1, source_target_pairs={{0,2},{1,3},{2,0},{3,1},{4,6},{5,7},{6,4},{7,5},{8,10},{9,11},{10,... | collective-permute-start | bytes 5308424 | tf_op jit(solution)/shard_map/ppermute | solution.py:886
  696.3 347.0 %reduce-scatter.26.cloned.1.call-start = ((), (), s32[]{:S(2)}) async-start(), calls=%async_computation.19 | async-start | bytes 2211840 | tf_op jit(solution)/shard_map/reduce_scatter | solution.py:892
  696.6 40.6 %collective-permute-start.19 = (bf16[4,288,768]{2,1,0:T(8,128)(2,1)S(1)}, bf16[4,288,768]{2,1,0:T(8,128)(2,1)S(1)}, u32[]{:S(2)}, u32[]{:S(2)}) collective-permute-start(bf16[4,288,768]{2,1,0:T(8,128)(2,1)S(1)} %bitcast.317), channel_id=1, source_target_pairs={{0,2},{1,3},{2,0},{3,1},{4,6},{5,7},{6,4},{7,5},{8,10},{9,11},{10,... | collective-permute-start | bytes 5308424 | tf_op jit(solution)/shard_map/ppermute | solution.py:886
  738.8 307.0 %reduce-scatter.16.cloned.1.call-start = ((), (), s32[]{:S(2)}) async-start(), calls=%async_computation.14 | async-start | bytes 2211840 | tf_op jit(solution)/shard_map/reduce_scatter | solution.py:892
  742.8 39.9 %collective-permute-start.23 = (bf16[4,96,2304]{2,1,0:T(8,128)(2,1)}, bf16[4,96,2304]{2,1,0:T(8,128)(2,1)S(1)}, u32[]{:S(2)}, u32[]{:S(2)}) collective-permute-start(bf16[4,96,2304]{2,1,0:T(8,128)(2,1)} %bitcast.316), channel_id=1, source_target_pairs={{0,2},{1,3},{2,0},{3,1},{4,6},{5,7},{6,4},{7,5},{8,10},{9,11},{10,... | collective-permute-start | bytes 5308424 | tf_op jit(solution)/shard_map/ppermute | solution.py:886
  784.4 261.4 %reduce-scatter.18.cloned.1.call-start = ((), (), s32[]{:S(2)}) async-start(), calls=%async_computation.15 | async-start | bytes 2211840 | tf_op jit(solution)/shard_map/reduce_scatter | solution.py:892
  784.4 39.0 %collective-permute-start.24 = (bf16[4,96,2304]{2,1,0:T(8,128)(2,1)}, bf16[4,96,2304]{2,1,0:T(8,128)(2,1)S(1)}, u32[]{:S(2)}, u32[]{:S(2)}) collective-permute-start(bf16[4,96,2304]{2,1,0:T(8,128)(2,1)} %bitcast.315), channel_id=1, source_target_pairs={{0,2},{1,3},{2,0},{3,1},{4,6},{5,7},{6,4},{7,5},{8,10},{9,11},{10,... | collective-permute-start | bytes 5308424 | tf_op jit(solution)/shard_map/ppermute | solution.py:886
  825.1 223.2 %reduce-scatter.20.cloned.1.call-start = ((), (), s32[]{:S(2)}) async-start(), calls=%async_computation.16 | async-start | bytes 2211840 | tf_op jit(solution)/shard_map/reduce_scatter | solution.py:892
  825.2 41.3 %collective-permute-start.28 = (bf16[4,96,2304]{2,1,0:T(8,128)(2,1)}, bf16[4,96,2304]{2,1,0:T(8,128)(2,1)}, u32[]{:S(2)}, u32[]{:S(2)}) collective-permute-start(bf16[4,96,2304]{2,1,0:T(8,128)(2,1)} %bitcast.314), channel_id=1, source_target_pairs={{0,2},{1,3},{2,0},{3,1},{4,6},{5,7},{6,4},{7,5},{8,10},{9,11},{10,... | collective-permute-start | bytes 5308424 | tf_op jit(solution)/shard_map/ppermute | solution.py:886
  869.9 178.4 %reduce-scatter.22.cloned.1.call-start = ((), (), s32[]{:S(2)}) async-start(), calls=%async_computation.17 | async-start | bytes 2211840 | tf_op jit(solution)/shard_map/reduce_scatter | solution.py:892
  870.2 40.6 %collective-permute-start.31 = (bf16[4,96,2304]{2,1,0:T(8,128)(2,1)}, bf16[4,96,2304]{2,1,0:T(8,128)(2,1)}, u32[]{:S(2)}, u32[]{:S(2)}) collective-permute-start(bf16[4,96,2304]{2,1,0:T(8,128)(2,1)} %bitcast.99), channel_id=1, source_target_pairs={{0,2},{1,3},{2,0},{3,1},{4,6},{5,7},{6,4},{7,5},{8,10},{9,11},{10,... | collective-permute-start | bytes 5308424 | tf_op jit(solution)/shard_map/ppermute | solution.py:886
  913.8 137.0 %reduce-scatter.14.cloned.1.call-start = ((), (), s32[]{:S(2)}) async-start(), calls=%async_computation.13 | async-start | bytes 1966080 | tf_op jit(solution)/shard_map/reduce_scatter | solution.py:892
  954.3 98.4 %reduce-scatter.12.cloned.1.call-start = ((), (), s32[]{:S(2)}) async-start(), calls=%async_computation.12 | async-start | bytes 1966080 | tf_op jit(solution)/shard_map/reduce_scatter | solution.py:892
  993.9 87.2 %reduce-scatter.10.cloned.1.call-start = ((), (), s32[]{:S(2)}) async-start(), calls=%async_computation.11 | async-start | bytes 2334720 | tf_op jit(solution)/shard_map/reduce_scatter | solution.py:892
  995.5 41.4 %collective-permute-start.34 = (bf16[4,96,2432]{2,1,0:T(8,128)(2,1)S(1)}, bf16[4,96,2432]{2,1,0:T(8,128)(2,1)S(1)}, u32[]{:S(2)}, u32[]{:S(2)}) collective-permute-start(bf16[4,96,2432]{2,1,0:T(8,128)(2,1)S(1)} %pad_maximum_fusion.2), channel_id=1, source_target_pairs={{0,2},{1,3},{2,0},{3,1},{4,6},{5,7},{6,4},{7,5},{8,10},{9,11},{10,... | collective-permute-start | bytes 5603336 | tf_op jit(solution)/shard_map/ppermute | solution.py:886
  (64 other events, 910.6 us)
Sparse Core Ops, SparseCore 0:
  16.9 173.8 all-gather.2
  192.9 144.4 all-gather.4
  696.4 39.1 reduce-scatter.23
  738.9 39.4 reduce-scatter.25
  784.5 41.4 reduce-scatter.15
  828.8 38.2 reduce-scatter.17
  870.0 40.8 reduce-scatter.19
  914.0 40.8 reduce-scatter.21
  957.2 35.0 reduce-scatter.13
  994.4 37.4 reduce-scatter.11
  1038.7 42.3 reduce-scatter.9

commit v5 on v4

--- a/solution.py
+++ b/solution.py
@@ -520,7 +520,7 @@
 ):
     steps = length // SUB
     width = keep_ref.shape[1]
-    chunk = 4
+    chunk = 8
     sub = lax.broadcasted_iota(jnp.int32, (SUB, width), 0)
     taps = [vec_ref[k : k + 1, :] for k in range(CONV)]
     conv_bias, scale = vec_ref[4:5, :], vec_ref[7:8, :]

time: 1100 us -> 1100 us (level)
  no operation moved by 1% of the time
where the time goes in v5:
time: 1100 us; the launch traced here: 1090 us
  waiting for transfers between devices  459 us (42%)
  Pallas kernels  426 us (39%)
  local copies, waits for them, and re-layouts  79.2 us (7%)
  starting transfers between devices  62.3 us (6%)
  other arithmetic  50.5 us (5%)
  between operations  15.2 us (1%)
    pallas_call x20, Pallas kernels, call(): pl.pallas_call(kernel, grid=grid, in_specs=in_specs, out_specs=out_specs,...  354 us
    all_gather x2, waiting for transfers between devices, gather(): return lax.all_gather(shard, ('seq', 'fsdp'), axis=0, tiled=True)  212 us
    ppermute x9, waiting for transfers between devices, y_send(): lax.ppermute(value, 'fsdp', [(2 * a + c, 2 * b + c) for a, b in pairs for...  163 us
    pallas_call x6, Pallas kernels, outer(): pl.pallas_call(functools.partial(outer_kernel, (n, fs, share), pieces), g...  72 us
    ppermute x17, waiting for transfers between devices, shifted(): return lax.ppermute(value, axis, pairs)  43.2 us
    ppermute x17, starting transfers between devices, shifted(): return lax.ppermute(value, axis, pairs)  40.9 us
    reduce_scatter x9, waiting for transfers between devices, over_z(): lax.psum_scatter(shares, 'seq', scatter_dimension=0, tiled=True)[0]  26.5 us
  transfers between devices with their start and end apart: 46, of which 20 were waited for; matrix products, arithmetic and copies ran while one was open for 9% of the time, Pallas kernels for 25%

profile of v5, /device:TPU:0, one launch (start us, length us, event | category | flops | bytes accessed | tf_op | source)
XLA Modules:
  0.0 1092.2 jit_solution(18404929303706396089)
XLA Ops:
  28.9 161.9 %all-gather.3.cloned.1.call-done.wi_ref.w_ref.folded_ref = bf16[1536,11136]{1,0:T(8,128)(2,1)} async-done(((bf16[96,11136]{1,0:T(8,128)(2,1)}), bf16[1536,11136]{1,0:T(8,128)(2,1)}) %all-gather.3.cloned.1.call-update) | async-done | bytes 34209808 | tf_op jit(solution)/shard_map/all_gather | solution.py:940
  199.6 18.4 %shard_map.296 = (bf16[512,1536]{1,0:T(8,128)(2,1)}, f32[2,280,2048]{2,1,0:T(8,128)}, f32[512,2048]{1,0:T(8,128)}, f32[512,2048]{1,0:T(8,128)}, f32[512,2048]{1,...) custom-call(bf16[512,1536]{1,0:T(8,128)(2,1)} %bitcast.253, bf16[16,1536]{1,0:T(8,128)(2,1)} %copy-done.30, ...), custom_call_target="tpu_custom_call" | custom-call | flops 2013265920 | bytes 6815744 | tf_op jit(solution)/shard_map/pallas_call | solution.py:57
  255.6 16.2 %shard_map.299.wd_ref = bf16[4608,1536]{1,0:T(8,128)(2,1)} custom-call(bf16[1536,11136]{1,0:T(8,128)(2,1)} %all-gather.3.cloned.1.call-done.wi_ref.w_ref.folded_ref), custom_call_target="tpu_custom_call" | custom-call | bytes 7077888 | tf_op jit(solution)/shard_map/pallas_call | solution.py:57
  272.7 15.1 %shard_map.298 = (f32[512,2048]{1,0:T(8,128)}, bf16[512,2048]{1,0:T(8,128)(2,1)}, f32[512,1536]{1,0:T(8,128)}, bf16[512,1536]{1,0:T(8,128)(2,1)}) custom-call(bf16[512,1536]{1,0:T(8,128)(2,1)} %bitcast.254, f32[512,2048]{1,0:T(8,128)} %get-tuple-element.141.keep_ref, f32[512,2048]{1,0:T(8,128)} %get-tuple-element.142.local_ref, ...), custom_call_target="tpu_custom_call" | custom-call | flops 1207959552 | bytes 6291456 | tf_op jit(solution)/shard_map/pallas_call | solution.py:57
  287.7 49.7 %all-gather.5.cloned.1.call-done.wg_ref.wu_ref = bf16[1536,9216]{1,0:T(8,128)(2,1)} async-done(((bf16[96,9216]{1,0:T(8,128)(2,1)}), bf16[1536,9216]{1,0:T(8,128)(2,1)}) %all-gather.5.cloned.1.call-update) | async-done | bytes 28311568 | tf_op jit(solution)/shard_map/all_gather | solution.py:940
  337.4 32.1 %shard_map.300 = bf16[512,1536]{1,0:T(8,128)(2,1)} custom-call(bf16[512,1536]{1,0:T(8,128)(2,1)} %get-tuple-element.148.x_ref, f32[512,1536]{1,0:T(8,128)} %get-tuple-element.149.mid_ref, bf16[1536,9216]{1,0:T(8,128)(2,1)} %all-gather.5.cloned.1.call-done.wg_ref.wu_ref, bf16[1536,9216]{1,0:T(8,128)(2,1)} %all-gather.5.cloned.1.call-done.wg_ref.wu_ref, ...), custom_call_target="tpu_custom_call" | custom-call | flops 8153726976 | bytes 10616832 | tf_op jit(solution)/shard_map/pallas_call | solution.py:57
  377.1 14.3 %shard_map.301.wd_ref = bf16[512,4608]{1,0:T(8,128)(2,1)} custom-call(bf16[512,1536]{1,0:T(8,128)(2,1)} %bitcast.255, bf16[4608,1536]{1,0:T(8,128)(2,1)} %shard_map.299.wd_ref), custom_call_target="tpu_custom_call" | custom-call | flops 1811939328 | bytes 5898240 | tf_op jit(solution)/shard_map/pallas_call | solution.py:57
  392.1 15.2 %collective-permute-done.4 = bf16[512,1536]{1,0:T(8,128)(2,1)S(1)} collective-permute-done((bf16[512,1536]{1,0:T(8,128)(2,1)}, bf16[512,1536]{1,0:T(8,128)(2,1)S(1)}, u32[]{:S(2)}, u32[]{:S(2)}) %collective-permute-start.4) | collective-permute-done | bytes 1572896 | tf_op jit(solution)/shard_map/ppermute | solution.py:843
  408.6 17.4 %shard_map.302 = (bf16[512,1536]{1,0:T(8,128)(2,1)}, f32[2,280,2048]{2,1,0:T(8,128)}, f32[512,2048]{1,0:T(8,128)}, f32[512,2048]{1,0:T(8,128)}, f32[512,2048]{1,...) custom-call(bf16[512,1536]{1,0:T(8,128)(2,1)} %broadcast_select_fusion.1.x_ref, ...), custom_call_target="tpu_custom_call" | custom-call | flops 2013265920 | bytes 6815744 | tf_op jit(solution)/shard_map/pallas_call | solution.py:57
  448.1 14.7 %shard_map.304 = (f32[512,2048]{1,0:T(8,128)}, bf16[512,2048]{1,0:T(8,128)(2,1)}, f32[512,1536]{1,0:T(8,128)}, bf16[512,1536]{1,0:T(8,128)(2,1)}) custom-call(bf16[512,1536]{1,0:T(8,128)(2,1)} %broadcast_select_fusion.1.x_ref, f32[512,2048]{1,0:T(8,128)} %get-tuple-element.152.keep_ref, f32[512,2048]{1,0:T(8,128)} %get-tuple-element.153.local_ref, ...), custom_call_target="tpu_custom_call" | custom-call | flops 1207959552 | bytes 6291456 | tf_op jit(solution)/shard_map/pallas_call | solution.py:57
  462.8 33.9 %shard_map.305 = (bf16[512,4608]{1,0:T(8,128)(2,1)}, bf16[512,4608]{1,0:T(8,128)(2,1)}, bf16[4608,512]{1,0:T(8,128)(2,1)}, bf16[512,1536]{1,0:T(8,128)(2,1)}) custom-call(bf16[512,1536]{1,0:T(8,128)(2,1)} %get-tuple-element.180.x_ref, f32[512,1536]{1,0:T(8,128)} %get-tuple-element.160.mid_ref, bf16[1536,9216]{1,0:T(8,128)(2,1)} %all-gather.5.cloned.1.call-done.wg_ref.wu_ref, ...), custom_call_target="tpu_custom_call" | custom-call | flops 8153726976 | bytes 10616832 | tf_op jit(solution)/shard_map/pallas_call | solution.py:57
  496.7 30.2 %shard_map.306 = (bf16[2,512,4608]{2,1,0:T(8,128)(2,1)}, f32[512,1536]{1,0:T(8,128)}, bf16[512,1536]{1,0:T(8,128)(2,1)}, f32[1,1536]{1,0:T(1,128)}) custom-call(bf16[512,1536]{1,0:T(8,128)(2,1)} %bitcast.256, f32[512,1536]{1,0:T(8,128)} %get-tuple-element.160.mid_ref, f32[1,1536]{1,0:T(1,128)} %reshape.633.gain_ref, ...), custom_call_target="tpu_custom_call" | custom-call | flops 6522981376 | bytes 10616832 | tf_op jit(solution)/shard_map/pallas_call | solution.py:57
  550.2 17.2 %shard_map.308 = (f32[512,2048]{1,0:T(8,128)}, f32[16,2048]{1,0:T(8,128)}, f32[16,128,128]{2,1,0:T(8,128)}, f32[16,128,128]{2,1,0:T(8,128)}, f32[8,2048]{1,0:T(8,128)}) custom-call(f32[512,2048]{1,0:T(8,128)} %get-tuple-element.168.local_ref, f32[512,2048]{1,0:T(8,128)} %get-tuple-element.152.keep_ref, f32[512,2048]{1,0:T(8,128)} %get-tuple-element.166.hidden_ref, ...), custom_call_target="tpu_custom_call" | custom-call | flops 1073741824 | bytes 7340032 | tf_op jit(solution)/shard_map/pallas_call | solution.py:57
  606.9 23.0 %collective-permute-done.13 = bf16[512,1536]{1,0:T(8,128)(2,1)} collective-permute-done((bf16[512,1536]{1,0:T(8,128)(2,1)}, bf16[512,1536]{1,0:T(8,128)(2,1)}, u32[]{:S(2)}, u32[]{:S(2)}) %collective-permute-start.13) | collective-permute-done | bytes 1572896 | tf_op jit(solution)/shard_map/ppermute | solution.py:843
  636.1 16.7 %shard_map.311 = (bf16[1152,768]{1,0:T(8,128)(2,1)}, bf16[1152,768]{1,0:T(8,128)(2,1)}, bf16[1152,768]{1,0:T(8,128)(2,1)}, bf16[1152,768]{1,0:T(8,128)(2,1)}) custom-call(s32[2]{0:T(128)} %pad_add_fusion.place_ref, bf16[4608,512]{1,0:T(8,128)(2,1)} %get-tuple-element.185.left_a, bf16[4608,512]{1,0:T(8,128)(2,1)} %collective-permute-done.14.left_b, ...), custom_call_target="tpu_custom_call" | custom-call | flops 1811939328 | bytes 1 | tf_op jit(solution)/shard_map/pallas_call | solution.py:802
  654.6 36.4 %shard_map.312 = (bf16[2,512,4608]{2,1,0:T(8,128)(2,1)}, f32[512,1536]{1,0:T(8,128)}, bf16[512,1536]{1,0:T(8,128)(2,1)}, f32[1,1536]{1,0:T(1,128)}) custom-call(bf16[512,1536]{1,0:T(8,128)(2,1)} %copy-done.2, f32[512,1536]{1,0:T(8,128)} %get-tuple-element.160.mid_ref, f32[1,1536]{1,0:T(1,128)} %reshape.633.gain_ref, ...), custom_call_target="tpu_custom_call" | custom-call | flops 6522981376 | bytes 10616832 | tf_op jit(solution)/shard_map/pallas_call | solution.py:57
  744.3 19.9 %shard_map.315 = (bf16[384,2304]{1,0:T(8,128)(2,1)}, bf16[384,2304]{1,0:T(8,128)(2,1)}, bf16[384,2304]{1,0:T(8,128)(2,1)}, bf16[384,2304]{1,0:T(8,128)(2,1)}, bf...) custom-call(s32[2]{0:T(128)} %pad_add_fusion.place_ref, bf16[6144,512]{1,0:T(8,128)(2,1)} %pad_maximum_fusion.left_a, ...), custom_call_target="tpu_custom_call" | custom-call | flops 2717908992 | bytes 1 | tf_op jit(solution)/shard_map/pallas_call | solution.py:802
  786.0 17.4 %shard_map.316 = (f32[512,2048]{1,0:T(8,128)}, f32[16,2048]{1,0:T(8,128)}, f32[16,128,128]{2,1,0:T(8,128)}, f32[16,128,128]{2,1,0:T(8,128)}, f32[8,2048]{1,0:T(8,128)}) custom-call(f32[512,2048]{1,0:T(8,128)} %get-tuple-element.215.local_ref, f32[512,2048]{1,0:T(8,128)} %get-tuple-element.152.keep_ref, f32[512,2048]{1,0:T(8,128)} %get-tuple-element.166.hidden_ref, ...), custom_call_target="tpu_custom_call" | custom-call | flops 1073741824 | bytes 7340032 | tf_op jit(solution)/shard_map/pallas_call | solution.py:57
  803.4 19.8 %collective-permute-done.24 = bf16[4,96,2304]{2,1,0:T(8,128)(2,1)S(1)} collective-permute-done((bf16[4,96,2304]{2,1,0:T(8,128)(2,1)}, bf16[4,96,2304]{2,1,0:T(8,128)(2,1)S(1)}, u32[]{:S(2)}, u32[]{:S(2)}) %collective-permute-start.24) | collective-permute-done | bytes 1769504 | tf_op jit(solution)/shard_map/ppermute | solution.py:886
  852.7 13.6 %collective-permute-done.28 = bf16[4,96,2304]{2,1,0:T(8,128)(2,1)} collective-permute-done((bf16[4,96,2304]{2,1,0:T(8,128)(2,1)}, bf16[4,96,2304]{2,1,0:T(8,128)(2,1)}, u32[]{:S(2)}, u32[]{:S(2)}) %collective-permute-start.28) | collective-permute-done | bytes 1769504 | tf_op jit(solution)/shard_map/ppermute | solution.py:886
  928.1 22.9 %collective-permute-done.32 = bf16[4,128,1536]{2,1,0:T(8,128)(2,1)} collective-permute-done((bf16[4,128,1536]{2,1,0:T(8,128)(2,1)}, bf16[4,128,1536]{2,1,0:T(8,128)(2,1)}, u32[]{:S(2)}, u32[]{:S(2)}) %collective-permute-start.32) | collective-permute-done | bytes 1572896 | tf_op jit(solution)/shard_map/ppermute | solution.py:886
  956.0 34.5 %collective-permute-done.33 = bf16[4,96,2048]{2,1,0:T(8,128)(2,1)} collective-permute-done((bf16[4,96,2048]{2,1,0:T(8,128)(2,1)}, bf16[4,96,2048]{2,1,0:T(8,128)(2,1)}, u32[]{:S(2)}, u32[]{:S(2)}) %collective-permute-start.33) | collective-permute-done | bytes 1572896 | tf_op jit(solution)/shard_map/ppermute | solution.py:886
  997.2 39.5 %collective-permute-done.34 = bf16[4,96,2432]{2,1,0:T(8,128)(2,1)S(1)} collective-permute-done((bf16[4,96,2432]{2,1,0:T(8,128)(2,1)S(1)}, bf16[4,96,2432]{2,1,0:T(8,128)(2,1)S(1)}, u32[]{:S(2)}, u32[]{:S(2)}) %collective-permute-start.34) | collective-permute-done | bytes 1867808 | tf_op jit(solution)/shard_map/ppermute | solution.py:886
  1054.5 26.5 %reduce-scatter.10.cloned.1.call-done = bf16[1,96,2432]{2,1,0:T(8,128)(2,1)} async-done(((bf16[4,96,2432]{2,1,0:T(8,128)(2,1)}), bf16[1,96,2432]{2,1,0:T(8,128)(2,1)}) %reduce-scatter.10.cloned.1.call-update) | async-done | bytes 466960 | tf_op jit(solution)/shard_map/reduce_scatter | solution.py:892
  (316 shorter events, 370.5 us)
Async XLA Ops:
  7.2 183.6 %all-gather.3.cloned.1.call-start = ((), (), s32[]{:S(2)}) async-start(), calls=%async_computation.9 | async-start | bytes 36347904 | tf_op jit(solution)/shard_map/all_gather | solution.py:940
  16.8 320.6 %all-gather.5.cloned.1.call-start = ((), (), s32[]{:S(2)}) async-start(), calls=%async_computation.10 | async-start | bytes 30081024 | tf_op jit(solution)/shard_map/all_gather | solution.py:940
  19.5 1023.5 %reduce-scatter.24.cloned.1.call-start = ((), (), s32[]{:S(2)}) async-start(), calls=%async_computation.18 | async-start | bytes 2211840 | tf_op jit(solution)/shard_map/reduce_scatter | solution.py:892
  21.3 177.0 %collective-permute-start = (bf16[16,1536]{1,0:T(8,128)(2,1)S(1)}, bf16[16,1536]{1,0:T(8,128)(2,1)S(1)}, u32[]{:S(2)}, u32[]{:S(2)}) collective-permute-start(bf16[16,1536]{1,0:T(8,128)(2,1)S(1)} %pad_bitcast_fusion.1), channel_id=1, source_target_pairs={{0,4},{4,8},{8,12},{1,5},{5,9},{9,13},{2,6},{6,10},{10,14},{3,7},{... | collective-permute-start | bytes 147464 | tf_op jit(solution)/shard_map/ppermute | solution.py:843
  218.1 53.7 %collective-permute-start.3 = (f32[4,2048]{1,0:T(4,128)}, f32[4,2048]{1,0:T(4,128)S(1)}, u32[]{:S(2)}, u32[]{:S(2)}) collective-permute-start(f32[4,2048]{1,0:T(4,128)} %get-tuple-element.144), channel_id=1, source_target_pairs={{0,12},{1,13},{2,14},{3,15},{16,28},{17,29},{18,30},{19,31}} | collective-permute-start | bytes 98312 | tf_op jit(solution)/shard_map/ppermute | solution.py:843
  223.2 48.6 %collective-permute-start.2 = (f32[4,2048]{1,0:T(4,128)}, f32[4,2048]{1,0:T(4,128)S(1)}, u32[]{:S(2)}, u32[]{:S(2)}) collective-permute-start(f32[4,2048]{1,0:T(4,128)} %get-tuple-element.144), channel_id=1, source_target_pairs={{0,8},{4,12},{1,9},{5,13},{2,10},{6,14},{3,11},{7,15},{16,24},{20,... | collective-permute-start | bytes 98312 | tf_op jit(solution)/shard_map/ppermute | solution.py:843
  224.5 47.4 %collective-permute-start.1 = (f32[4,2048]{1,0:T(4,128)}, f32[4,2048]{1,0:T(4,128)S(1)}, u32[]{:S(2)}, u32[]{:S(2)}) collective-permute-start(f32[4,2048]{1,0:T(4,128)} %get-tuple-element.144), channel_id=1, source_target_pairs={{0,4},{4,8},{8,12},{1,5},{5,9},{9,13},{2,6},{6,10},{10,14},{3,7},{... | collective-permute-start | bytes 98312 | tf_op jit(solution)/shard_map/ppermute | solution.py:843
  540.2 89.7 %collective-permute-start.14 = (bf16[4608,512]{1,0:T(8,128)(2,1)}, bf16[4608,512]{1,0:T(8,128)(2,1)}, u32[]{:S(2)}, u32[]{:S(2)}) collective-permute-start(bf16[4608,512]{1,0:T(8,128)(2,1)} %get-tuple-element.185.left_a), channel_id=1, source_target_pairs={{0,1},{1,0},{2,3},{3,2},{4,5},{5,4},{6,7},{7,6},{8,9},{9,8},{10,11... | collective-permute-start | bytes 14155784 | tf_op jit(solution)/shard_map/ppermute | solution.py:883
  591.3 38.5 %collective-permute-start.13 = (bf16[512,1536]{1,0:T(8,128)(2,1)}, bf16[512,1536]{1,0:T(8,128)(2,1)}, u32[]{:S(2)}, u32[]{:S(2)}) collective-permute-start(bf16[512,1536]{1,0:T(8,128)(2,1)} %get-tuple-element.179), channel_id=1, source_target_pairs={{16,0},{17,1},{18,2},{19,3},{20,4},{21,5},{22,6},{23,7},{24,8},{25... | collective-permute-start | bytes 4718600 | tf_op jit(solution)/shard_map/ppermute | solution.py:843
  652.8 40.9 %collective-permute-start.16 = (bf16[4,288,768]{2,1,0:T(8,128)(2,1)}, bf16[4,288,768]{2,1,0:T(8,128)(2,1)S(1)}, u32[]{:S(2)}, u32[]{:S(2)}) collective-permute-start(bf16[4,288,768]{2,1,0:T(8,128)(2,1)} %bitcast.318), channel_id=1, source_target_pairs={{0,2},{1,3},{2,0},{3,1},{4,6},{5,7},{6,4},{7,5},{8,10},{9,11},{10,... | collective-permute-start | bytes 5308424 | tf_op jit(solution)/shard_map/ppermute | solution.py:886
  695.9 347.2 %reduce-scatter.26.cloned.1.call-start = ((), (), s32[]{:S(2)}) async-start(), calls=%async_computation.19 | async-start | bytes 2211840 | tf_op jit(solution)/shard_map/reduce_scatter | solution.py:892
  696.3 40.6 %collective-permute-start.19 = (bf16[4,288,768]{2,1,0:T(8,128)(2,1)S(1)}, bf16[4,288,768]{2,1,0:T(8,128)(2,1)S(1)}, u32[]{:S(2)}, u32[]{:S(2)}) collective-permute-start(bf16[4,288,768]{2,1,0:T(8,128)(2,1)S(1)} %bitcast.317), channel_id=1, source_target_pairs={{0,2},{1,3},{2,0},{3,1},{4,6},{5,7},{6,4},{7,5},{8,10},{9,11},{10,... | collective-permute-start | bytes 5308424 | tf_op jit(solution)/shard_map/ppermute | solution.py:886
  738.6 307.0 %reduce-scatter.16.cloned.1.call-start = ((), (), s32[]{:S(2)}) async-start(), calls=%async_computation.14 | async-start | bytes 2211840 | tf_op jit(solution)/shard_map/reduce_scatter | solution.py:892
  742.5 39.9 %collective-permute-start.23 = (bf16[4,96,2304]{2,1,0:T(8,128)(2,1)}, bf16[4,96,2304]{2,1,0:T(8,128)(2,1)S(1)}, u32[]{:S(2)}, u32[]{:S(2)}) collective-permute-start(bf16[4,96,2304]{2,1,0:T(8,128)(2,1)} %bitcast.316), channel_id=1, source_target_pairs={{0,2},{1,3},{2,0},{3,1},{4,6},{5,7},{6,4},{7,5},{8,10},{9,11},{10,... | collective-permute-start | bytes 5308424 | tf_op jit(solution)/shard_map/ppermute | solution.py:886
  784.1 261.5 %reduce-scatter.18.cloned.1.call-start = ((), (), s32[]{:S(2)}) async-start(), calls=%async_computation.15 | async-start | bytes 2211840 | tf_op jit(solution)/shard_map/reduce_scatter | solution.py:892
  784.2 39.0 %collective-permute-start.24 = (bf16[4,96,2304]{2,1,0:T(8,128)(2,1)}, bf16[4,96,2304]{2,1,0:T(8,128)(2,1)S(1)}, u32[]{:S(2)}, u32[]{:S(2)}) collective-permute-start(bf16[4,96,2304]{2,1,0:T(8,128)(2,1)} %bitcast.315), channel_id=1, source_target_pairs={{0,2},{1,3},{2,0},{3,1},{4,6},{5,7},{6,4},{7,5},{8,10},{9,11},{10,... | collective-permute-start | bytes 5308424 | tf_op jit(solution)/shard_map/ppermute | solution.py:886
  824.8 223.3 %reduce-scatter.20.cloned.1.call-start = ((), (), s32[]{:S(2)}) async-start(), calls=%async_computation.16 | async-start | bytes 2211840 | tf_op jit(solution)/shard_map/reduce_scatter | solution.py:892
  825.0 41.3 %collective-permute-start.28 = (bf16[4,96,2304]{2,1,0:T(8,128)(2,1)}, bf16[4,96,2304]{2,1,0:T(8,128)(2,1)}, u32[]{:S(2)}, u32[]{:S(2)}) collective-permute-start(bf16[4,96,2304]{2,1,0:T(8,128)(2,1)} %bitcast.314), channel_id=1, source_target_pairs={{0,2},{1,3},{2,0},{3,1},{4,6},{5,7},{6,4},{7,5},{8,10},{9,11},{10,... | collective-permute-start | bytes 5308424 | tf_op jit(solution)/shard_map/ppermute | solution.py:886
  869.6 178.5 %reduce-scatter.22.cloned.1.call-start = ((), (), s32[]{:S(2)}) async-start(), calls=%async_computation.17 | async-start | bytes 2211840 | tf_op jit(solution)/shard_map/reduce_scatter | solution.py:892
  869.9 40.6 %collective-permute-start.31 = (bf16[4,96,2304]{2,1,0:T(8,128)(2,1)}, bf16[4,96,2304]{2,1,0:T(8,128)(2,1)}, u32[]{:S(2)}, u32[]{:S(2)}) collective-permute-start(bf16[4,96,2304]{2,1,0:T(8,128)(2,1)} %bitcast.99), channel_id=1, source_target_pairs={{0,2},{1,3},{2,0},{3,1},{4,6},{5,7},{6,4},{7,5},{8,10},{9,11},{10,... | collective-permute-start | bytes 5308424 | tf_op jit(solution)/shard_map/ppermute | solution.py:886
  913.6 137.0 %reduce-scatter.14.cloned.1.call-start = ((), (), s32[]{:S(2)}) async-start(), calls=%async_computation.13 | async-start | bytes 1966080 | tf_op jit(solution)/shard_map/reduce_scatter | solution.py:892
  954.1 98.4 %reduce-scatter.12.cloned.1.call-start = ((), (), s32[]{:S(2)}) async-start(), calls=%async_computation.12 | async-start | bytes 1966080 | tf_op jit(solution)/shard_map/reduce_scatter | solution.py:892
  993.7 87.2 %reduce-scatter.10.cloned.1.call-start = ((), (), s32[]{:S(2)}) async-start(), calls=%async_computation.11 | async-start | bytes 2334720 | tf_op jit(solution)/shard_map/reduce_scatter | solution.py:892
  995.3 41.4 %collective-permute-start.34 = (bf16[4,96,2432]{2,1,0:T(8,128)(2,1)S(1)}, bf16[4,96,2432]{2,1,0:T(8,128)(2,1)S(1)}, u32[]{:S(2)}, u32[]{:S(2)}) collective-permute-start(bf16[4,96,2432]{2,1,0:T(8,128)(2,1)S(1)} %pad_maximum_fusion.2), channel_id=1, source_target_pairs={{0,2},{1,3},{2,0},{3,1},{4,6},{5,7},{6,4},{7,5},{8,10},{9,11},{10,... | collective-permute-start | bytes 5603336 | tf_op jit(solution)/shard_map/ppermute | solution.py:886
  (64 other events, 910.8 us)
Sparse Core Ops, SparseCore 0:
  16.9 173.8 all-gather.2
  192.9 144.4 all-gather.4
  696.0 39.1 reduce-scatter.23
  738.7 39.4 reduce-scatter.25
  784.2 41.4 reduce-scatter.15
  828.6 38.2 reduce-scatter.17
  869.7 40.8 reduce-scatter.19
  913.7 40.8 reduce-scatter.21
  956.9 35.0 reduce-scatter.13
  994.2 37.4 reduce-scatter.11
  1038.5 42.3 reduce-scatter.9
